TPU v7x, 32 devices: a whole 2x2x4 slice. The times are simulated.
32 devices in a mesh: dp: 16 (over z, y, x), head: 2 (over core).
Axes of the slice: x: 2, y: 2, z: 4, core: 2. Of those that a mesh axis runs over, the one named last changes fastest.
Arguments:
- tokens: bfloat16 [16, 2048, 768], P('dp'), may hold values from -6 to 6
- segment_ids: int32 [16, 2048], P('dp'), may hold values from 0 to 3, never falling along the last dimension, each value on 1 to 1024 neighbouring positions
- counts: int32 [16], P('dp'), may hold values from 512 to 2048, as said below
- w_qkv: bfloat16 [3, 768, 768], P(None, 'dp', 'head'), may hold values from -0.21875 to 0.21875
- w_out: bfloat16 [768, 768], P('head', 'dp'), may hold values from -1.25 to 1.25
- w_in: bfloat16 [2, 768, 1152], P(None, ('dp', 'head')), may hold values from -0.21875 to 0.21875
- w_down: bfloat16 [1152, 768], P(None, ('dp', 'head')), may hold values from -0.1875 to 0.1875
- ln1_gain: bfloat16 [768], P(('dp', 'head')), may hold values from 0.5 to 1.5
- ln2_gain: bfloat16 [768], P(('dp', 'head')), may hold values from 0.5 to 1.5
- cotangent: bfloat16 [16, 2048, 768], P('dp', 'head'), may hold values from -6 to 6
Outputs:
- result: bfloat16 [16, 2048, 768], P('dp', 'head')
- grad_tokens: float32 [16, 2048, 768], P('dp', 'head')
- grad_w_qkv: float32 [3, 768, 768], P(None, 'dp', 'head')
- grad_w_out: float32 [768, 768], P('head', 'dp')
- grad_w_in: float32 [2, 768, 1152], P(None, ('dp', 'head'))
- grad_w_down: float32 [1152, 768], P(None, ('dp', 'head'))
- grad_ln1: float32 [768], P(('dp', 'head'))
- grad_ln2: float32 [768], P(('dp', 'head'))
Inputs may be any that keep to these rules, and one draw needn't show every extreme that they name: `segment_ids`: ids never fall along a row; each document spans 1 to 1024 positions and some document exactly 1024. `counts`: some row is full in every draw.
All inputs are finite; a program needn't handle non-finite values.
Results may differ from a plain program's by a relative error of at most 0.018.
Values may be sent and summed in bfloat16 or wider, within the bound.
No kernel may reach another device: no remote copies, remote signals or barrier semaphores. Data moves between devices by JAX's collectives and lax.ppermute only.
A program may use at most 256 MiB of HBM per device.

v0:
```python
import math

import jax
import jax.numpy as jnp
from jax import lax
from jax.sharding import PartitionSpec as P

HEAD_DIM = 64


layer_eps = 1e-05
rope_theta = 160000.0
neg_large = -1e30


def layer_norm(values, gain):
    center = values - jnp.mean(values, axis=-1, keepdims=True)
    spread = jnp.mean(center * center, axis=-1, keepdims=True)
    return center * lax.rsqrt(spread + layer_eps) * gain


def rotary_tables(length, head_size):
    freqs = rope_theta ** (-jnp.arange(0, head_size, 2).astype(jnp.float32) / head_size)
    angles = jnp.arange(length).astype(jnp.float32)[:, None] * freqs[None, :]
    angles = jnp.concatenate([angles, angles], axis=1)
    return (jnp.cos(angles), jnp.sin(angles))


def rotate_half(values):
    middle = values.shape[-1] // 2
    return jnp.concatenate([-values[..., middle:], values[..., :middle]], axis=-1)


def rotate_back(values):
    middle = values.shape[-1] // 2
    return jnp.concatenate([values[..., middle:], -values[..., :middle]], axis=-1)


def block_mask(seg_query, seg_keys, count_valid, start_row):
    row_ids = start_row + jnp.arange(seg_query.shape[0], dtype=jnp.int32)
    col_ids = jnp.arange(seg_keys.shape[0], dtype=jnp.int32)
    allowed = (seg_query[:, None] == seg_keys[None, :]) & (col_ids[None, :] < count_valid)
    return allowed | (row_ids[:, None] == col_ids[None, :])


def gated_unit(up_part, gate_part):
    return jax.nn.gelu(up_part, approximate=False) * gate_part


def forward_row(items):
    q_row, k_row, v_row, seg_row, count_valid = items
    row_length, heads_here, head_size = q_row.shape
    block = min(512, row_length)
    blocks = row_length // block
    score_scale = 1.0 / math.sqrt(head_size)

    def forward_one_block(parts):
        q_blk, seg_blk, start_row = parts
        scores = (
            jnp.einsum("qhe,khe->hqk", q_blk, k_row, preferred_element_type=jnp.float32)
            * score_scale
        )
        scores = jnp.where(
            block_mask(seg_blk, seg_row, count_valid, start_row)[None], scores, neg_large
        )
        top_score = jnp.max(scores, axis=-1, keepdims=True)
        expo = jnp.exp(scores - top_score)
        total = jnp.sum(expo, axis=-1, keepdims=True)
        probs = (expo / total).astype(jnp.bfloat16)
        outs = jnp.einsum("hqk,khe->qhe", probs, v_row, preferred_element_type=jnp.float32)
        return (outs, (top_score + jnp.log(total))[..., 0])

    starts = jnp.arange(blocks, dtype=jnp.int32) * block
    outs, log_sums = lax.map(
        forward_one_block,
        (
            q_row.reshape(blocks, block, heads_here, head_size),
            seg_row.reshape(blocks, block),
            starts,
        ),
    )
    return (outs.reshape(row_length, heads_here, head_size), log_sums)


def backward_row(items):
    q_row, k_row, v_row, grad_row, log_sums, seg_row, count_valid = items
    row_length, heads_here, head_size = q_row.shape
    block = min(512, row_length)
    blocks = row_length // block
    score_scale = 1.0 / math.sqrt(head_size)

    def backward_one_block(carry, parts):
        grad_keys, grad_values = carry
        q_blk, grad_blk, lse_blk, seg_blk, start_row = parts
        scores = (
            jnp.einsum("qhe,khe->hqk", q_blk, k_row, preferred_element_type=jnp.float32)
            * score_scale
        )
        scores = jnp.where(
            block_mask(seg_blk, seg_row, count_valid, start_row)[None], scores, neg_large
        )
        probs = jnp.exp(scores - lse_blk[..., None])
        grad_probs = jnp.einsum("qhe,khe->hqk", grad_blk, v_row, preferred_element_type=jnp.float32)
        inner = jnp.sum(probs * grad_probs, axis=-1, keepdims=True)
        grad_scores = (probs * (grad_probs - inner)).astype(jnp.bfloat16)
        grad_query = (
            jnp.einsum("hqk,khe->qhe", grad_scores, k_row, preferred_element_type=jnp.float32)
            * score_scale
        )
        grad_keys = (
            grad_keys
            + jnp.einsum("hqk,qhe->khe", grad_scores, q_blk, preferred_element_type=jnp.float32)
            * score_scale
        )
        grad_values = grad_values + jnp.einsum(
            "hqk,qhe->khe", probs.astype(jnp.bfloat16), grad_blk, preferred_element_type=jnp.float32
        )
        return ((grad_keys, grad_values), grad_query)

    starts = jnp.arange(blocks, dtype=jnp.int32) * block
    zeros = jnp.zeros((row_length, heads_here, head_size), jnp.float32)
    shaped = (
        q_row.reshape(blocks, block, heads_here, head_size),
        grad_row.reshape(blocks, block, heads_here, head_size),
        log_sums,
        seg_row.reshape(blocks, block),
        starts,
    )
    (grad_keys, grad_values), grad_query = lax.scan(backward_one_block, (zeros, zeros), shaped)
    return (grad_query.reshape(row_length, heads_here, head_size), grad_keys, grad_values)


def local(tokens, segment_ids, counts, w_qkv, w_out, w_in, w_down, ln1_gain, ln2_gain, cotangent):
    row_count, row_length, width = tokens.shape
    part_count = lax.axis_size("head")
    part_index = lax.axis_index("head")
    half_length = row_length // part_count
    first_row = part_index * half_length
    head_size = HEAD_DIM
    w_qkv_all, w_out_all = (
        lax.all_gather(w_qkv, "dp", axis=1, tiled=True),
        lax.all_gather(w_out, "dp", axis=1, tiled=True),
    )
    w_in_all, w_down_all, gain_one_all, gain_two_all = (
        lax.all_gather(w_in, ("dp", "head"), axis=1, tiled=True),
        lax.all_gather(w_down, ("dp", "head"), axis=1, tiled=True),
        lax.all_gather(ln1_gain, ("dp", "head"), axis=0, tiled=True),
        lax.all_gather(ln2_gain, ("dp", "head"), axis=0, tiled=True),
    )
    gain_one = gain_one_all.astype(jnp.float32)
    gain_two = gain_two_all.astype(jnp.float32)
    local_width = w_qkv_all.shape[2]
    heads_here = local_width // head_size
    all_tokens = row_count * row_length
    half_tokens = row_count * half_length
    inputs32 = tokens.astype(jnp.float32)
    normed1 = layer_norm(inputs32, gain_one).astype(jnp.bfloat16).reshape(all_tokens, width)
    qkv = jnp.einsum("nd,kde->kne", normed1, w_qkv_all, preferred_element_type=jnp.float32)
    qkv = qkv.reshape(3, row_count, row_length, heads_here, head_size)
    cosines, sines = rotary_tables(row_length, head_size)
    cos_b = cosines[None, :, None, :]
    sin_b = sines[None, :, None, :]
    query = (qkv[0] * cos_b + rotate_half(qkv[0]) * sin_b).astype(jnp.bfloat16)
    keyset = (qkv[1] * cos_b + rotate_half(qkv[1]) * sin_b).astype(jnp.bfloat16)
    valueset = qkv[2].astype(jnp.bfloat16)
    attended, log_sums = lax.map(forward_row, (query, keyset, valueset, segment_ids, counts))
    attended_low = attended.reshape(all_tokens, local_width).astype(jnp.bfloat16)
    partial_out = jnp.dot(attended_low, w_out_all, preferred_element_type=jnp.float32).reshape(
        row_count, row_length, width
    )
    summed = lax.psum(partial_out.astype(jnp.bfloat16), "head").astype(jnp.float32)
    attn_half = lax.dynamic_slice_in_dim(summed, first_row, half_length, 1)
    positions = first_row + jnp.arange(half_length, dtype=jnp.int32)
    valid_half = (positions[None, :] < counts[:, None]).astype(jnp.float32)[..., None]
    inputs_half = lax.dynamic_slice_in_dim(inputs32, first_row, half_length, 1)
    hidden = inputs_half + valid_half * attn_half
    normed2 = layer_norm(hidden, gain_two).astype(jnp.bfloat16).reshape(half_tokens, width)
    up_gate = jnp.einsum("nd,kdf->knf", normed2, w_in_all, preferred_element_type=jnp.float32)
    mixed = gated_unit(up_gate[0], up_gate[1]).astype(jnp.bfloat16)
    ffn_out = jnp.dot(mixed, w_down_all, preferred_element_type=jnp.float32).reshape(
        row_count, half_length, width
    )
    result = hidden + valid_half * ffn_out
    grad_result = cotangent.astype(jnp.float32)
    grad_ffn = (valid_half * grad_result).astype(jnp.bfloat16).reshape(half_tokens, width)
    grad_down = jnp.einsum("nf,nd->fd", mixed, grad_ffn, preferred_element_type=jnp.float32)
    grad_mixed = jnp.einsum("nd,fd->nf", grad_ffn, w_down_all, preferred_element_type=jnp.float32)
    unused_value, gated_pull = jax.vjp(gated_unit, up_gate[0], up_gate[1])
    grad_up, grad_gate = gated_pull(grad_mixed)
    grad_pair = jnp.stack([grad_up, grad_gate]).astype(jnp.bfloat16)
    grad_in = jnp.einsum("nd,knf->kdf", normed2, grad_pair, preferred_element_type=jnp.float32)
    grad_normed2 = jnp.einsum(
        "knf,kdf->nd", grad_pair, w_in_all, preferred_element_type=jnp.float32
    ).reshape(row_count, half_length, width)
    unused_norm, norm_two_pull = jax.vjp(layer_norm, hidden, gain_two)
    grad_hidden_norm, grad_gain_two = norm_two_pull(grad_normed2)
    grad_hidden = grad_result + grad_hidden_norm
    grad_attn_half = (valid_half * grad_hidden).astype(jnp.bfloat16)
    grad_attn = lax.all_gather(grad_attn_half, "head", axis=1, tiled=True).reshape(
        all_tokens, width
    )
    grad_out_local = jnp.einsum(
        "nc,nd->cd", attended_low, grad_attn, preferred_element_type=jnp.float32
    )
    grad_attended = jnp.einsum(
        "nd,cd->nc", grad_attn, w_out_all, preferred_element_type=jnp.float32
    )
    grad_attended = grad_attended.astype(jnp.bfloat16).reshape(
        row_count, row_length, heads_here, head_size
    )
    grad_query, grad_keys, grad_values = lax.map(
        backward_row, (query, keyset, valueset, grad_attended, log_sums, segment_ids, counts)
    )
    grad_query_pre = grad_query * cos_b + rotate_back(grad_query * sin_b)
    grad_keys_pre = grad_keys * cos_b + rotate_back(grad_keys * sin_b)
    grad_qkv = (
        jnp.stack([grad_query_pre, grad_keys_pre, grad_values])
        .astype(jnp.bfloat16)
        .reshape(3, all_tokens, local_width)
    )
    grad_qkv_local = jnp.einsum(
        "nd,kne->kde", normed1, grad_qkv, preferred_element_type=jnp.float32
    )
    grad_normed1 = jnp.einsum(
        "kne,kde->nd", grad_qkv, w_qkv_all, preferred_element_type=jnp.float32
    ).reshape(row_count, row_length, width)
    grad_normed1_half = lax.psum_scatter(
        grad_normed1.astype(jnp.bfloat16), "head", scatter_dimension=1, tiled=True
    ).astype(jnp.float32)
    unused_first, norm_one_pull = jax.vjp(layer_norm, inputs_half, gain_one)
    grad_inputs_norm, grad_gain_one = norm_one_pull(grad_normed1_half)
    grad_tokens = grad_hidden + grad_inputs_norm
    grad_qkv_shard, grad_out_shard = (
        lax.psum_scatter(grad_qkv_local, "dp", scatter_dimension=1, tiled=True),
        lax.psum_scatter(grad_out_local, "dp", scatter_dimension=1, tiled=True),
    )
    grad_in_shard, grad_down_shard, grad_one_shard, grad_two_shard = (
        lax.psum_scatter(grad_in, ("dp", "head"), scatter_dimension=1, tiled=True),
        lax.psum_scatter(grad_down, ("dp", "head"), scatter_dimension=1, tiled=True),
        lax.psum_scatter(grad_gain_one, ("dp", "head"), scatter_dimension=0, tiled=True),
        lax.psum_scatter(grad_gain_two, ("dp", "head"), scatter_dimension=0, tiled=True),
    )
    return (
        result.astype(jnp.bfloat16),
        grad_tokens,
        grad_qkv_shard,
        grad_out_shard,
        grad_in_shard,
        grad_down_shard,
        grad_one_shard,
        grad_two_shard,
    )


def solution(mesh):
    placed = (
        P("dp", None, None),
        P("dp", None),
        P("dp"),
        P(None, "dp", "head"),
        P("head", "dp"),
        P(None, ("dp", "head"), None),
        P(None, ("dp", "head")),
        P(("dp", "head")),
        P(("dp", "head")),
        P("dp", "head", None),
    )
    return jax.shard_map(
        local,
        mesh=mesh,
        in_specs=placed,
        out_specs=(
            P("dp", "head", None),
            P("dp", "head", None),
            P(None, "dp", "head"),
            P("head", "dp"),
            P(None, ("dp", "head"), None),
            P(None, ("dp", "head")),
            P(("dp", "head")),
            P(("dp", "head")),
        ),
        check_vma=False,
    )
```

profile of v0, /device:TPU:0, one launch (start us, length us, event | category | flops | bytes accessed | tf_op | source)
XLA Modules:
  0.0 1368.5 jit_solution(17598973813826857219)
XLA Ops:
  10.5 42.0 %all-reduce.8 = (bf16[768]{0:T(1024)(128)(2,1)S(1)}, bf16[768]{0:T(1024)(128)(2,1)}) all-reduce(bf16[768]{0:T(1024)(128)(2,1)S(1)} %dynamic-update-slice, bf16[768]{0:T(1024)(128)(2,1)S(1)} %dynamic-update-slice.1), channel_id=1, replica_groups=mesh['dp'=16,'head'=2] {'dp','head'}, use_global_device_ids=true, to_apply=%add | all-reduce | flops 1536 | bytes 6144
  58.1 46.8 %all_gather.23 = bf16[384,768]{0,1:T(8,128)(2,1)} all-gather(bf16[384,48]{0,1:T(8,128)(2,1)S(1)} %copy-done.40), channel_id=1, replica_groups=mesh['dp'=16,'head'=2] {'dp'}, dimensions={1}, use_global_device_ids=true | all-gather | bytes 626688 | tf_op jit(solution)/shard_map/all_gather | solution.py:142
  147.3 155.9 %while.47 = (s32[]{:T(128)}, bf16[4,512,6,64]{1,3,2,0:T(8,128)(2,1)S(1)}, f32[4,6,512]{2,1,0:T(8,128)S(1)}, s32[4,512]{1,0:T(4,128)S(1)}, s32[2048]{0:T(1024)S(1...) while((s32[]{:T(128)}, ...), condition=%wide.region_5.6_spmd, body=%wide.region_2.5_spmd.sunk | while | flops 1690304000 | bytes 84158608 | solution.py:74
  334.6 58.8 %all-gather.7.cloned.1.call-done = bf16[2,768,1152]{2,1,0:T(8,128)(2,1)} async-done(((bf16[2,24,1152]{2,1,0:T(8,128)(2,1)}), bf16[2,768,1152]{2,1,0:T(8,128)(2,1)}) %all-gather.7.cloned.1.call-update) | async-done | bytes 3538960 | tf_op jit(solution)/shard_map/all_gather | solution.py:145
  475.8 411.4 %while.48 = (s32[]{:T(128)}, f32[2048,6,64]{0,2,1:T(8,128)}, f32[2048,6,64]{0,2,1:T(8,128)}, f32[4,512,6,64]{1,0,3,2:T(4,128)}, bf16[4,512,6,64]{1,3,2,0:T(8,128...) while((s32[]{:T(128)}, f32[2048,6,64]{0,2,1:T(8,128)}, ...), condition=%wide.region_13.14_spmd.clone, body=%wide.region_11.13_spmd.clone.sunk | while | flops 4129226240 | bytes 215853264 | solution.py:129
  504.2 18.1 %multiply_reduce_fusion.5 = (f32[6,512]{1,0:T(8,128)S(1)}, f32[6,512,2048]{2,1,0:T(8,128)}) fusion(f32[6,512,2048]{2,1,0:T(8,128)} %fusion.209, f32[6,512]{1,0:T(8,128)S(1)} %dynamic-slice_bitcast_fusion.2, pred[512,2048]{1,0:T(8,128)(4,1)S(1)} %fusion.210, bf16[2048,6,64]{0,2,1:T(8,128)(2,1)} %get-tuple-element.624, ...), kind=kOutput, calls=%fused_computation.21.clone.1 | convolution fusion | flops 836760576 | bytes 53370884 | tf_op jit(solution)/shard_map/while/body/eval_jaxpr/while/body/eval_jaxpr/qhe,khe->hqk/dot_general | solution.py:103
  522.4 21.5 %multiply_convert_fusion.6 = bf16[6,512,2048]{2,1,0:T(8,128)(2,1)} fusion(f32[6,512,2048]{2,1,0:T(8,128)} %get-tuple-element.547, f32[6,512,2048]{2,1,0:T(8,128)} %fusion.209, f32[6,512]{1,0:T(8,128)S(1)} %get-tuple-element.548, f32[6,512]{1,0:T(8,128)S(1)} %dynamic-slice_bitcast_fusion.2, pred[512,2048]{1,0:T(8,128)(4,1)S(1)} %fusion.210), kind=kLoop, calls=%fused_computation.20.clone.1 | loop fusion | flops 37748736 | bytes 63987712 | tf_op jit(solution)/shard_map/while/body/eval_jaxpr/while/body/eval_jaxpr/convert_element_type | solution.py:105
  562.0 16.1 %dynamic_update_slice.31 = f32[4,512,6,64]{1,0,3,2:T(4,128)} dynamic-update-slice(f32[4,512,6,64]{1,0,3,2:T(4,128)} %get-tuple-element.600, f32[1,512,6,64]{1,0,3,2:T(1,128)S(1)} %copy.90, s32[]{:T(128)S(6)} %copy.110, s32[]{:T(128)} %constant.56.clone.1..sunk, s32[]{:T(128)} %constant.56.clone.1..sunk, s32[]{:T(128)} %constant.56.clone.1..sunk) | dynamic-update-slice | bytes 1572868 | tf_op jit(solution)/shard_map/while/body/eval_jaxpr/while/body/jit(dynamic_update_index_in_dim)/dynamic_update_slice | solution.py:74
  593.6 14.3 %bitcast_add_fusion.6 = f32[2048,6,64]{0,2,1:T(8,128)} fusion(f32[2048,6,64]{0,2,1:T(8,128)} %get-tuple-element.599, f32[6,512,2048]{2,1,0:T(8,128)} %fusion.209, f32[6,512]{1,0:T(8,128)S(1)} %dynamic-slice_bitcast_fusion.2, pred[512,2048]{1,0:T(8,128)(4,1)S(1)} %fusion.210, pred[]{:T(512)S(6)} %compare.3, ...), kind=kOutput, calls=%fused_computation.28.clone.1 | convolution fusion | flops 832045056 | bytes 32911364 | tf_op jit(solution)/shard_map/while/body/eval_jaxpr/while/body/eval_jaxpr/hqk,qhe->khe/dot_general | solution.py:115
  607.9 18.2 %multiply_reduce_fusion.5 = (f32[6,512]{1,0:T(8,128)S(1)}, f32[6,512,2048]{2,1,0:T(8,128)}) fusion(f32[6,512,2048]{2,1,0:T(8,128)} %fusion.209, f32[6,512]{1,0:T(8,128)S(1)} %dynamic-slice_bitcast_fusion.2, pred[512,2048]{1,0:T(8,128)(4,1)S(1)} %fusion.210, bf16[2048,6,64]{0,2,1:T(8,128)(2,1)} %get-tuple-element.624, ...), kind=kOutput, calls=%fused_computation.21.clone.1 | convolution fusion | flops 836760576 | bytes 53370884 | tf_op jit(solution)/shard_map/while/body/eval_jaxpr/while/body/eval_jaxpr/qhe,khe->hqk/dot_general | solution.py:103
  626.1 21.2 %multiply_convert_fusion.6 = bf16[6,512,2048]{2,1,0:T(8,128)(2,1)} fusion(f32[6,512,2048]{2,1,0:T(8,128)} %get-tuple-element.547, f32[6,512,2048]{2,1,0:T(8,128)} %fusion.209, f32[6,512]{1,0:T(8,128)S(1)} %get-tuple-element.548, f32[6,512]{1,0:T(8,128)S(1)} %dynamic-slice_bitcast_fusion.2, pred[512,2048]{1,0:T(8,128)(4,1)S(1)} %fusion.210), kind=kLoop, calls=%fused_computation.20.clone.1 | loop fusion | flops 37748736 | bytes 63987712 | tf_op jit(solution)/shard_map/while/body/eval_jaxpr/while/body/eval_jaxpr/convert_element_type | solution.py:105
  666.3 16.0 %dynamic_update_slice.31 = f32[4,512,6,64]{1,0,3,2:T(4,128)} dynamic-update-slice(f32[4,512,6,64]{1,0,3,2:T(4,128)} %get-tuple-element.600, f32[1,512,6,64]{1,0,3,2:T(1,128)S(1)} %copy.90, s32[]{:T(128)S(6)} %copy.110, s32[]{:T(128)} %constant.56.clone.1..sunk, s32[]{:T(128)} %constant.56.clone.1..sunk, s32[]{:T(128)} %constant.56.clone.1..sunk) | dynamic-update-slice | bytes 1572868 | tf_op jit(solution)/shard_map/while/body/eval_jaxpr/while/body/jit(dynamic_update_index_in_dim)/dynamic_update_slice | solution.py:74
  696.7 13.7 %bitcast_add_fusion.6 = f32[2048,6,64]{0,2,1:T(8,128)} fusion(f32[2048,6,64]{0,2,1:T(8,128)} %get-tuple-element.599, f32[6,512,2048]{2,1,0:T(8,128)} %fusion.209, f32[6,512]{1,0:T(8,128)S(1)} %dynamic-slice_bitcast_fusion.2, pred[512,2048]{1,0:T(8,128)(4,1)S(1)} %fusion.210, pred[]{:T(512)S(6)} %compare.3, ...), kind=kOutput, calls=%fused_computation.28.clone.1 | convolution fusion | flops 832045056 | bytes 32911364 | tf_op jit(solution)/shard_map/while/body/eval_jaxpr/while/body/eval_jaxpr/hqk,qhe->khe/dot_general | solution.py:115
  710.4 18.1 %multiply_reduce_fusion.5 = (f32[6,512]{1,0:T(8,128)S(1)}, f32[6,512,2048]{2,1,0:T(8,128)}) fusion(f32[6,512,2048]{2,1,0:T(8,128)} %fusion.209, f32[6,512]{1,0:T(8,128)S(1)} %dynamic-slice_bitcast_fusion.2, pred[512,2048]{1,0:T(8,128)(4,1)S(1)} %fusion.210, bf16[2048,6,64]{0,2,1:T(8,128)(2,1)} %get-tuple-element.624, ...), kind=kOutput, calls=%fused_computation.21.clone.1 | convolution fusion | flops 836760576 | bytes 53370884 | tf_op jit(solution)/shard_map/while/body/eval_jaxpr/while/body/eval_jaxpr/qhe,khe->hqk/dot_general | solution.py:103
  728.5 21.2 %multiply_convert_fusion.6 = bf16[6,512,2048]{2,1,0:T(8,128)(2,1)} fusion(f32[6,512,2048]{2,1,0:T(8,128)} %get-tuple-element.547, f32[6,512,2048]{2,1,0:T(8,128)} %fusion.209, f32[6,512]{1,0:T(8,128)S(1)} %get-tuple-element.548, f32[6,512]{1,0:T(8,128)S(1)} %dynamic-slice_bitcast_fusion.2, pred[512,2048]{1,0:T(8,128)(4,1)S(1)} %fusion.210), kind=kLoop, calls=%fused_computation.20.clone.1 | loop fusion | flops 37748736 | bytes 63987712 | tf_op jit(solution)/shard_map/while/body/eval_jaxpr/while/body/eval_jaxpr/convert_element_type | solution.py:105
  768.7 16.0 %dynamic_update_slice.31 = f32[4,512,6,64]{1,0,3,2:T(4,128)} dynamic-update-slice(f32[4,512,6,64]{1,0,3,2:T(4,128)} %get-tuple-element.600, f32[1,512,6,64]{1,0,3,2:T(1,128)S(1)} %copy.90, s32[]{:T(128)S(6)} %copy.110, s32[]{:T(128)} %constant.56.clone.1..sunk, s32[]{:T(128)} %constant.56.clone.1..sunk, s32[]{:T(128)} %constant.56.clone.1..sunk) | dynamic-update-slice | bytes 1572868 | tf_op jit(solution)/shard_map/while/body/eval_jaxpr/while/body/jit(dynamic_update_index_in_dim)/dynamic_update_slice | solution.py:74
  812.8 18.1 %multiply_reduce_fusion.5 = (f32[6,512]{1,0:T(8,128)S(1)}, f32[6,512,2048]{2,1,0:T(8,128)}) fusion(f32[6,512,2048]{2,1,0:T(8,128)} %fusion.209, f32[6,512]{1,0:T(8,128)S(1)} %dynamic-slice_bitcast_fusion.2, pred[512,2048]{1,0:T(8,128)(4,1)S(1)} %fusion.210, bf16[2048,6,64]{0,2,1:T(8,128)(2,1)} %get-tuple-element.624, ...), kind=kOutput, calls=%fused_computation.21.clone.1 | convolution fusion | flops 836760576 | bytes 53370884 | tf_op jit(solution)/shard_map/while/body/eval_jaxpr/while/body/eval_jaxpr/qhe,khe->hqk/dot_general | solution.py:103
  830.9 21.2 %multiply_convert_fusion.6 = bf16[6,512,2048]{2,1,0:T(8,128)(2,1)} fusion(f32[6,512,2048]{2,1,0:T(8,128)} %get-tuple-element.547, f32[6,512,2048]{2,1,0:T(8,128)} %fusion.209, f32[6,512]{1,0:T(8,128)S(1)} %get-tuple-element.548, f32[6,512]{1,0:T(8,128)S(1)} %dynamic-slice_bitcast_fusion.2, pred[512,2048]{1,0:T(8,128)(4,1)S(1)} %fusion.210), kind=kLoop, calls=%fused_computation.20.clone.1 | loop fusion | flops 37748736 | bytes 63987712 | tf_op jit(solution)/shard_map/while/body/eval_jaxpr/while/body/eval_jaxpr/convert_element_type | solution.py:105
  871.1 16.0 %dynamic_update_slice.31 = f32[4,512,6,64]{1,0,3,2:T(4,128)} dynamic-update-slice(f32[4,512,6,64]{1,0,3,2:T(4,128)} %get-tuple-element.600, f32[1,512,6,64]{1,0,3,2:T(1,128)S(1)} %copy.90, s32[]{:T(128)S(6)} %copy.110, s32[]{:T(128)} %constant.56.clone.1..sunk, s32[]{:T(128)} %constant.56.clone.1..sunk, s32[]{:T(128)} %constant.56.clone.1..sunk) | dynamic-update-slice | bytes 1572868 | tf_op jit(solution)/shard_map/while/body/eval_jaxpr/while/body/jit(dynamic_update_index_in_dim)/dynamic_update_slice | solution.py:74
  943.9 16.3 %fusion.94 = f32[1152,768]{0,1:T(8,128)} fusion(f32[2,1024,1152]{2,1,0:T(8,128)} %copy-done.5, bf16[1,1024,768]{2,1,0:T(8,128)(2,1)S(1)} %copy-done.21, f32[1024]{0:T(1024)S(1)} %copy-done.35), kind=kOutput, calls=%fused_computation.162 | convolution fusion | flops 1892155392 | bytes 14553088 | tf_op jit(solution)/shard_map/nf,nd->fd/dot_general | solution.py:186
  978.5 132.7 %all-reduce.15.cloned.1.call-done = f32[3,768,384]{2,0,1:T(4,128)} async-done(((f32[3,768,384]{2,0,1:T(4,128)}), f32[3,768,384]{2,0,1:T(4,128)}) %all-reduce.15.cloned.1.call-update) | async-done | bytes 3538960
  1130.5 40.6 %all-reduce.7 = (f32[768]{0:T(1024)S(1)}, f32[768]{0:T(1024)S(1)}) all-reduce(f32[768]{0:T(1024)S(1)} %get-tuple-element.317, f32[768]{0:T(1024)S(1)} %copy-done.46), channel_id=7, replica_groups=mesh['dp'=16,'head'=2] {'dp','head'}, use_global_device_ids=true, to_apply=%region_24.25.clone | all-reduce | flops 1536 | bytes 12288
  1177.0 56.8 %reduce-scatter.10.cloned.1.call-done = f32[1152,24]{0,1:T(8,128)} async-done(((f32[1152,768]{0,1:T(8,128)}), f32[1152,24]{0,1:T(8,128)}) %reduce-scatter.10.cloned.1.call-update) | async-done | bytes 110608
  1233.8 127.6 %reduce-scatter.8.cloned.1.call-done = f32[384,48]{0,1:T(8,128)} async-done(((f32[384,768]{0,1:T(8,128)}), f32[384,48]{0,1:T(8,128)}) %reduce-scatter.8.cloned.1.call-update) | async-done | bytes 73744 | tf_op jit(solution)/shard_map/reduce_scatter | solution.py:235
  (297 shorter events, 579.0 us)
Async XLA Ops:
  7.2 49.6 %copy-start.6 = (bf16[1,2048,768]{2,1,0:T(8,128)(2,1)S(1)}, bf16[1,2048,768]{2,1,0:T(8,128)(2,1)}, u32[]{:S(2)}) copy-start(bf16[1,2048,768]{2,1,0:T(8,128)(2,1)} %param.14) | copy-start | bytes 9437188
  7.2 104.9 %all-gather.5.cloned.1.call-start = ((), (), s32[]{:S(2)}) async-start(), calls=%async_computation.3 | async-start | bytes 1880064 | tf_op jit(solution)/shard_map/all_gather | solution.py:141
  7.9 308.8 %all-gather.9.cloned.1.call-start = ((), (), s32[]{:S(2)}) async-start(), calls=%async_computation.6 | async-start | bytes 1824768 | tf_op jit(solution)/shard_map/all_gather | solution.py:146
  8.7 320.1 %all-reduce.13.cloned.1.call-start = ((), (), s32[]{:S(2)}) async-start(), calls=%async_computation.4 | async-start | bytes 6291456 | tf_op jit(solution)/shard_map/psum | solution.py:171
  52.5 59.6 %copy-start.36 = (f32[768]{0:T(1024)}, f32[768]{0:T(1024)S(1)}, u32[]{:S(2)}) copy-start(f32[768]{0:T(1024)S(1)} %convert_element_type.134) | copy-start | bytes 9220
  56.8 55.3 %copy-start.41 = (f32[2048]{0:T(1024)}, f32[2048]{0:T(1024)S(1)}, u32[]{:S(2)}) copy-start(f32[2048]{0:T(1024)S(1)} %broadcast_multiply_fusion.3) | copy-start | bytes 24580
  57.9 60.1 %copy-start.44 = (f32[2048]{0:T(1024)}, f32[2048]{0:T(1024)S(1)}, u32[]{:S(2)}) copy-start(f32[2048]{0:T(1024)S(1)} %add_rsqrt_fusion) | copy-start | bytes 24580
  121.6 21.6 %copy-start.8 = (f32[1,2048,384]{1,2,0:T(8,128)}, f32[1,2048,384]{1,2,0:T(8,128)S(1)}, u32[]{:S(2)}) copy-start(f32[1,2048,384]{1,2,0:T(8,128)S(1)} %get-tuple-element.383) | copy-start | bytes 9437188
  309.5 83.9 %all-gather.7.cloned.1.call-start = ((), (), s32[]{:S(2)}) async-start(), calls=%async_computation.5 | async-start | bytes 3649536 | tf_op jit(solution)/shard_map/all_gather | solution.py:145
  310.1 152.9 %all-gather.11.cloned.1.call-start = ((), (), s32[]{:S(2)}) async-start(), calls=%async_computation.7 | async-start | bytes 4718592 | tf_op jit(solution)/shard_map/all_gather | solution.py:199
  316.7 113.4 %copy-start.34 = (f32[1024]{0:T(1024)}, f32[1024]{0:T(1024)S(1)}, u32[]{:S(2)}) copy-start(f32[1024]{0:T(1024)S(1)} %fusion.111) | copy-start | bytes 12292
  400.4 13.2 copy-start.5
  413.5 7.3 copy-start.4
  413.5 7.3 copy-start.22
  413.5 7.3 copy-start.2
  420.8 7.8 copy-start.23
  433.5 543.3 %all-reduce.17.cloned.1.call-start = ((), (), s32[]{:S(2)}) async-start(), calls=%async_computation.11 | async-start | bytes 14155776
  462.9 648.3 %all-reduce.15.cloned.1.call-start = ((), (), s32[]{:S(2)}) async-start(), calls=%async_computation.10 | async-start | bytes 9437184
  899.4 6.0 copy-start.13
  932.7 190.8 %reduce-scatter.6.cloned.1.call-start = ((), (), s32[]{:S(2)}) async-start(), calls=%async_computation.8 | async-start | bytes 4718592 | tf_op jit(solution)/shard_map/reduce_scatter | solution.py:227
  942.5 291.2 %reduce-scatter.10.cloned.1.call-start = ((), (), s32[]{:S(2)}) async-start(), calls=%async_computation.12 | async-start | bytes 3649536
  960.3 401.1 %reduce-scatter.8.cloned.1.call-start = ((), (), s32[]{:S(2)}) async-start(), calls=%async_computation.9 | async-start | bytes 1253376 | tf_op jit(solution)/shard_map/reduce_scatter | solution.py:235
  1127.0 45.3 %copy-start.10 = (f32[1,1024,768]{2,1,0:T(8,128)S(1)}, f32[1,1024,768]{2,1,0:T(8,128)}, u32[]{:S(2)}) copy-start(f32[1,1024,768]{2,1,0:T(8,128)} %copy-done.9) | copy-start | bytes 9437188
  1127.0 45.3 %copy-start.39 = (f32[1024]{0:T(1024)S(1)}, f32[1024]{0:T(1024)}, u32[]{:S(2)}) copy-start(f32[1024]{0:T(1024)} %copy-done.38) | copy-start | bytes 12292
  (35 other events, 103.2 us)
Sparse Core Ops, SparseCore 0:
  10.7 62.7 all-gather.4
  76.3 55.3 all-gather.8
  309.6 19.0 all-reduce.12
  331.9 61.4 all-gather.6
  433.6 10.8 all-gather.10
  463.0 162.4 all-reduce.16
  932.8 178.3 all-reduce.14
  1113.5 9.9 reduce-scatter.5
  1129.5 104.2 reduce-scatter.9
  1238.9 122.4 reduce-scatter.7
where the time goes:
time: 1380 us; the launch traced here: 1370 us
  matrix products  430 us (31%)
  waiting for transfers between devices  395 us (29%)
  other arithmetic  236 us (17%)
  local copies, waits for them, and re-layouts  160 us (12%)
  blocking collectives  129 us (9%)
  between operations  16.5 us (1%)
    unnamed x13, waiting for transfers between devices  192 us
    reduce_scatter x1, waiting for transfers between devices, local(): lax.psum_scatter(grad_out_local, 'dp', scatter_dimension=1, tiled=True)  128 us
    convert_element_type x4, other arithmetic, backward_one_block(): grad_scores = (probs * (grad_probs - inner)).astype(jnp.bfloat16)  85.2 us
    unnamed x2, blocking collectives  82.7 us
    dot_general x4, matrix products, backward_one_block(): jnp.einsum('qhe,khe->hqk', grad_blk, v_row, preferred_element_type=jnp.fl...  72.6 us
    dynamic_update_slice x8, local copies, waits for them, and re-layouts, forward_row(): lax.map(forward_one_block, (q_row.reshape(blocks, block, heads_here, head...  67.4 us
    all_gather x1, waiting for transfers between devices, local(): lax.all_gather(w_in, ('dp', 'head'), axis=1, tiled=True)  58.8 us
    dot_general x4, matrix products, backward_one_block(): jnp.einsum('hqk,qhe->khe', probs.astype(jnp.bfloat16), grad_blk, preferre...  55 us
  transfers between devices with their start and end apart: 10, of which 6 were waited for; matrix products, arithmetic and copies ran while one was open for 57% of the time, Pallas kernels for 0%

commit v1 on v0

v1 whole, which is shorter than its diff:
```python
import functools
import math

import jax
import jax.numpy as jnp
from jax import lax
from jax.experimental import pallas as pl
from jax.experimental.pallas import tpu as pltpu
from jax.sharding import PartitionSpec as P

HEAD_DIM = 64
PAIR = 2 * HEAD_DIM
LAYER_EPS = 1e-05
ROPE_THETA = 160000.0
BIG = 1e30
LOG2_SCALE = math.log2(math.e) / math.sqrt(HEAD_DIM)
SCORE_SCALE = 1.0 / math.sqrt(HEAD_DIM)
ROW_BLOCK = 256
FWD_BQ, FWD_STEP = 512, 256
BWD_BQ, BWD_STEP = 256, 512
NT = (((1,), (1,)), ((), ()))
TN = (((0,), (0,)), ((), ()))
bf16 = jnp.bfloat16
f32 = jnp.float32
VMEM_LIMIT = 60 << 20


def vmem():
    return pl.BlockSpec(memory_space=pltpu.VMEM)


def smem():
    return pl.BlockSpec(memory_space=pltpu.SMEM)


def hbm():
    return pl.BlockSpec(memory_space=pl.ANY)


def params():
    return pltpu.CompilerParams(vmem_limit_bytes=VMEM_LIMIT)


def bit_groups(count):
    bits = count.bit_length() - 1
    shifts = []
    low = 0
    while low < bits:
        wide = min(2, bits - low)
        shifts.append((low, wide))
        low += wide
    return shifts[::-1]


def xor_permute(value, count, mask):
    return lax.ppermute(value, "dp", [(i, i ^ mask) for i in range(count)])


def core_swap(value):
    return lax.ppermute(value, "head", [(0, 1), (1, 0)])


def gather_parts(value, count):
    current = value[None]
    groups = bit_groups(count)
    for shift, wide in groups:
        parts = [current] + [xor_permute(current, count, j << shift) for j in range(1, 1 << wide)]
        if shift == 0:
            return parts
        current = jnp.stack(parts, axis=1).reshape((-1,) + value.shape)
    return [current]


def sum_kernel(count, *refs):
    ins, outs = refs[:count], refs[count:]
    for i, out in enumerate(outs):
        total = ins[0][i].astype(f32)
        for one in ins[1:]:
            total = total + one[i].astype(f32)
        out[...] = total.astype(out.dtype)


def sum_parts(arrays):
    m, rows, cols = arrays[0].shape
    return pl.pallas_call(
        functools.partial(sum_kernel, len(arrays)),
        out_shape=tuple(
            jax.ShapeDtypeStruct((rows, cols), f32 if i == 0 else bf16) for i in range(m)
        ),
        in_specs=[vmem()] * len(arrays),
        out_specs=(vmem(),) * m,
        compiler_params=params(),
        name="sum_parts",
    )(*arrays)


def reduce_parts(parts, count):
    high = len(parts[0])
    near = [parts[0]] + [xor_permute(parts[j], count, j) for j in range(1, len(parts))]
    pieces = sum_parts(near)
    shift = len(parts).bit_length() - 1
    total = pieces[0]
    for h in range(1, high):
        total = total + xor_permute(pieces[h], count, h << shift).astype(f32)
    return total


def placed_copies(parts, target, sems, me, rows):
    if len(parts) == 1:
        return [pltpu.make_async_copy(parts[0], target, sems.at[0])]
    copies = []
    wide = len(parts)
    for h in range(parts[0].shape[0]):
        for j in range(wide):
            own = jnp.bitwise_xor(me, h * wide + j)
            copies.append(
                pltpu.make_async_copy(
                    parts[j].at[h],
                    target.at[pl.ds(pl.multiple_of(own * rows, 16), rows)],
                    sems.at[h * wide + j],
                )
            )
    return copies


def document_starts(seg, length):
    starts = [jnp.int32(0)]
    for d in (1, 2, 3):
        starts.append(jnp.sum((seg < d).astype(jnp.int32)))
    return starts + [jnp.int32(length)]


def key_range(starts, live, first, size, length):
    last = jnp.minimum(first + size, live) - 1
    low = jnp.int32(0)
    high = jnp.int32(length)
    for d in (1, 2, 3):
        low = jnp.where(starts[d] <= first, starts[d], low)
    for d in (3, 2, 1):
        high = jnp.where(starts[d] > last, starts[d], high)
    high = jnp.minimum(high, live)
    return low, jnp.where(first < live, high, low)


def each_query_block(seg, live, length, size, step, work, empty):
    starts = document_starts(seg, length)

    @pl.loop(0, length // size)
    def _(i):
        first = pl.multiple_of(i * size, size)
        low, high = key_range(starts, live, first, size, length)
        base = low // 16 * 16
        steps = (high - base + step - 1) // step
        base = pl.multiple_of(jnp.maximum(jnp.minimum(base, length - steps * step), 0), 16)
        rows = pl.ds(first, size)
        for w in range(1, length // step + 1):

            @pl.when(steps == w)
            def _():
                work(rows, pl.ds(base, w * step))

        @pl.when(steps <= 0)
        def _():
            empty(rows)


def norm_stats(values):
    center = values - jnp.mean(values, axis=-1, keepdims=True)
    spread = jnp.mean(center * center, axis=-1, keepdims=True)
    inv = lax.rsqrt(spread + LAYER_EPS)
    return center * inv, inv


def norm_back(grad, normed, inv):
    return inv * (
        grad
        - jnp.mean(grad, axis=-1, keepdims=True)
        - normed * jnp.mean(grad * normed, axis=-1, keepdims=True)
    )


def half_swap(values, in_first):
    return jnp.where(in_first, pltpu.roll(values, PAIR - HEAD_DIM // 2, 1), pltpu.roll(values, HEAD_DIM // 2, 1))


def split3(values):
    a = values.astype(bf16)
    left = values - a.astype(f32)
    b = left.astype(bf16)
    return a, b, (left - b.astype(f32)).astype(bf16)


def forward_kernel(first, part_count, *refs):
    scal, seg, src = refs[:3]
    parts = refs[3 : 3 + part_count]
    cs, sn, fq, fk = refs[3 + part_count : 7 + part_count]
    outs = refs[7 + part_count :]
    if first:
        a1, gains = outs[:2]
        outs = outs[2:]
    w, q_out, k_out, v_out, o_out, lse_out, qx, kx, vx, sems = outs
    length, width = src.shape
    live, me = scal[0], scal[1]
    rows_each = width // max(16, 1) if part_count > 1 else width
    if part_count > 1:
        rows_each = parts[0].shape[1]
    copies = placed_copies(parts, w, sems, me, rows_each)
    for copy in copies:
        copy.start()
    for copy in copies:
        copy.wait()
    if first:
        turned = jnp.transpose(w[:, 4 * PAIR :].astype(f32))
        gains[0:8, :] = turned[0:8]
        gains[8:16, :] = turned[HEAD_DIM : HEAD_DIM + 8]
    lane = lax.broadcasted_iota(jnp.int32, (ROW_BLOCK, PAIR), 1)
    low_head = lane < HEAD_DIM
    in_first = (lane & (HEAD_DIM - 1)) < HEAD_DIM // 2
    zero = jnp.zeros((ROW_BLOCK, PAIR), bf16)

    @pl.loop(0, length // ROW_BLOCK)
    def _(b):
        rows = pl.ds(pl.multiple_of(b * ROW_BLOCK, ROW_BLOCK), ROW_BLOCK)
        if first:
            normed, _ = norm_stats(src[rows, :].astype(f32))
            a = (normed * gains[0:1, :]).astype(bf16)
            a1[rows, :] = a
        else:
            a = src[rows, :]
        qkv = jnp.dot(a, w[:, : 3 * PAIR], preferred_element_type=f32)
        cos, sin = cs[rows, :], sn[rows, :]
        u = qkv[:, :PAIR]
        q = (u * cos + half_swap(u, in_first) * sin).astype(bf16)
        u = qkv[:, PAIR : 2 * PAIR]
        k = (u * cos + half_swap(u, in_first) * sin).astype(bf16)
        v = qkv[:, 2 * PAIR :].astype(bf16)
        q_out[rows, :] = q
        k_out[rows, :] = k
        v_out[rows, :] = v
        scaled = q.astype(f32) * LOG2_SCALE
        high = scaled.astype(bf16)
        rest = (scaled - high.astype(f32)).astype(bf16)
        for h in (0, 1):
            mine = low_head if h == 0 else ~low_head
            qx[h, rows, :PAIR] = jnp.where(mine, high, zero)
            qx[h, rows, PAIR:] = jnp.where(mine, rest, fq[rows, :])
            kx[h, rows, :PAIR] = k
            kx[h, rows, PAIR:] = jnp.where(mine, k, fk[rows, :])
        vx[rows, :PAIR] = v
        vx[rows, PAIR:] = jnp.ones((ROW_BLOCK, PAIR), bf16)

    lane_q = lax.broadcasted_iota(jnp.int32, (FWD_BQ, PAIR), 1) < HEAD_DIM

    def work(rows, keys):
        values = vx[keys, :]
        scores = [
            lax.dot_general(qx[h, rows, :], kx[h, keys, :], NT, preferred_element_type=f32) for h in (0, 1)
        ]
        tops, sums = [], []
        for h in (0, 1):
            top = jnp.max(scores[h], axis=1, keepdims=True)
            probs = jnp.exp2(scores[h] - top).astype(bf16)
            tops.append(top)
            sums.append(jnp.dot(probs, values, preferred_element_type=f32))
        total = jnp.where(lane_q, sums[0][:, PAIR:], sums[1][:, PAIR:])
        out = jnp.where(lane_q, sums[0][:, :PAIR], sums[1][:, :PAIR])
        o_out[rows, :] = (out / total).astype(bf16)
        lse_out[rows, :] = jnp.maximum(jnp.where(lane_q, tops[0], tops[1]) + jnp.log2(total), -1e20)

    def empty(rows):
        o_out[rows, :] = jnp.zeros((FWD_BQ, PAIR), bf16)
        lse_out[rows, :] = jnp.zeros((FWD_BQ, PAIR), f32)

    each_query_block(seg[...], live, length, FWD_BQ, FWD_STEP, work, empty)


def forward_pair(first, scal, seg, src, parts, tables):
    length, width = src.shape
    cols = parts[0].shape[-1]
    shape = jax.ShapeDtypeStruct
    outs = [shape((width, cols), bf16)] + [shape((length, PAIR), bf16)] * 4 + [shape((length, PAIR), f32)]
    if first:
        outs = [shape((length, width), bf16), shape((16, width), f32)] + outs
    return pl.pallas_call(
        functools.partial(forward_kernel, first, len(parts)),
        out_shape=tuple(outs),
        in_specs=[smem(), vmem(), vmem()] + [hbm()] * len(parts) + [vmem()] * 4,
        out_specs=(vmem(),) * len(outs),
        scratch_shapes=[
            pltpu.VMEM((2, length, 2 * PAIR), bf16),
            pltpu.VMEM((2, length, 2 * PAIR), bf16),
            pltpu.VMEM((length, 2 * PAIR), bf16),
            pltpu.SemaphoreType.DMA((16,)),
        ],
        compiler_params=params(),
        name="attention_forward_first" if first else "attention_forward",
    )(scal, seg, src, *parts, *tables)


def backward_kernel(part_count, *refs):
    scal, seg, a1, near, far, w, q_in, k_in, v_in, o_in, lse, cs, sn, fq, fk, dqkv = refs[:16]
    parts = refs[16 : 16 + part_count]
    (grad_rows, qx, kx, dx, vx, qm, km, dq, dk, dv, grads, sems) = refs[16 + part_count :]
    length, width = a1.shape
    half = length // 2
    live, me, core = scal[0], scal[1], scal[2]
    loads = [
        pltpu.make_async_copy(near, grad_rows.at[pl.ds(pl.multiple_of(core * half, half), half)], sems.at[0]),
        pltpu.make_async_copy(far, grad_rows.at[pl.ds(pl.multiple_of((1 - core) * half, half), half)], sems.at[1]),
    ]
    for copy in loads:
        copy.start()
    for copy in loads:
        copy.wait()
    lane = lax.broadcasted_iota(jnp.int32, (ROW_BLOCK, PAIR), 1)
    in_head = lane & (HEAD_DIM - 1)
    low_head = lane < HEAD_DIM
    in_first = in_head < HEAD_DIM // 2
    zero = jnp.zeros((ROW_BLOCK, PAIR), bf16)
    minus = jnp.full((ROW_BLOCK, PAIR), -1, bf16)

    @pl.loop(0, length // ROW_BLOCK)
    def _(b):
        rows = pl.ds(pl.multiple_of(b * ROW_BLOCK, ROW_BLOCK), ROW_BLOCK)
        grad = jnp.dot(grad_rows[rows, :], w[:, 3 * PAIR : 4 * PAIR], preferred_element_type=f32).astype(bf16)
        q, k = q_in[rows, :], k_in[rows, :]
        scaled = q.astype(f32) * LOG2_SCALE
        high = scaled.astype(bf16)
        rest = (scaled - high.astype(f32)).astype(bf16)
        la, lb, lc = split3(lse[rows, :])
        fq_b = jnp.where(
            in_head == 5, la, jnp.where(in_head == 6, lb, jnp.where(in_head == 7, lc, fq[rows, :]))
        )
        fq_b = pltpu.roll(fq_b.astype(f32), HEAD_DIM, 1).astype(bf16)
        fk_b = jnp.where((in_head >= 5) & (in_head < 8), minus, fk[rows, :])
        inner = grad.astype(f32) * o_in[rows, :].astype(f32)
        for h in (0, 1):
            mine = low_head if h == 0 else ~low_head
            qx[h, rows, :PAIR] = jnp.where(mine, high, zero)
            qx[h, rows, PAIR:] = jnp.where(mine, rest, fq_b)
            kx[h, rows, :PAIR] = k
            kx[h, rows, PAIR:] = jnp.where(mine, k, fk_b)
            qm[h, rows, :] = jnp.where(mine, q, zero)
            km[h, rows, :] = jnp.where(mine, k, zero)
            dx[h, rows, :PAIR] = jnp.where(mine, grad, zero)
            delta = jnp.sum(jnp.where(mine, inner, 0.0), axis=1, keepdims=True)
            da, db, dc = split3(jnp.broadcast_to(delta, (ROW_BLOCK, PAIR)))
            dx[h, rows, PAIR:] = jnp.where(
                lane == 0, da, jnp.where(lane == 1, db, jnp.where(lane == 2, dc, zero))
            )
        vx[rows, :PAIR] = v_in[rows, :]
        vx[rows, PAIR:] = jnp.where(lane < 3, minus, zero)
        dk[rows, :] = jnp.zeros((ROW_BLOCK, PAIR), f32)
        dv[rows, :] = jnp.zeros((ROW_BLOCK, PAIR), f32)

    def work(rows, keys):
        grad_q = grad_k = grad_v = None
        for h in (0, 1):
            scores = lax.dot_general(qx[h, rows, :], kx[h, keys, :], NT, preferred_element_type=f32)
            pulled = lax.dot_general(dx[h, rows, :], vx[keys, :], NT, preferred_element_type=f32)
            probs = jnp.exp2(scores)
            grad_s = (probs * pulled).astype(bf16)
            one_q = jnp.dot(grad_s, km[h, keys, :], preferred_element_type=f32)
            one_v = lax.dot_general(probs.astype(bf16), dx[h, rows, :PAIR], TN, preferred_element_type=f32)
            one_k = lax.dot_general(grad_s, qm[h, rows, :], TN, preferred_element_type=f32)
            grad_q = one_q if h == 0 else grad_q + one_q
            grad_v = one_v if h == 0 else grad_v + one_v
            grad_k = one_k if h == 0 else grad_k + one_k
        dq[rows, :] = grad_q
        dv[keys, :] = dv[keys, :] + grad_v
        dk[keys, :] = dk[keys, :] + grad_k

    def empty(rows):
        dq[rows, :] = jnp.zeros((BWD_BQ, PAIR), f32)

    each_query_block(seg[...], live, length, BWD_BQ, BWD_STEP, work, empty)

    @pl.loop(0, length // ROW_BLOCK)
    def _(b):
        rows = pl.ds(pl.multiple_of(b * ROW_BLOCK, ROW_BLOCK), ROW_BLOCK)
        cos, sin = cs[rows, :], sn[rows, :]
        u = dq[rows, :] * SCORE_SCALE
        dqkv[rows, :PAIR] = (u * cos - half_swap(u, in_first) * sin).astype(bf16)
        u = dk[rows, :] * SCORE_SCALE
        dqkv[rows, PAIR : 2 * PAIR] = (u * cos - half_swap(u, in_first) * sin).astype(bf16)
        dqkv[rows, 2 * PAIR :] = dv[rows, :].astype(bf16)

    for m in range(width // ROW_BLOCK):
        part = slice(m * ROW_BLOCK, (m + 1) * ROW_BLOCK)
        grads[part, : 3 * PAIR] = lax.dot_general(
            a1[:, part], dqkv[...], TN, preferred_element_type=f32
        ).astype(bf16)
        grads[part, 3 * PAIR :] = lax.dot_general(
            grad_rows[:, part], o_in[...], TN, preferred_element_type=f32
        ).astype(bf16)
    if part_count == 1:
        stores = [pltpu.make_async_copy(grads, parts[0], sems.at[0])]
    else:
        rows_each = parts[0].shape[1]
        stores = []
        for h in range(parts[0].shape[0]):
            for j in range(part_count):
                own = jnp.bitwise_xor(me, h * part_count + j)
                stores.append(
                    pltpu.make_async_copy(
                        grads.at[pl.ds(pl.multiple_of(own * rows_each, 16), rows_each)],
                        parts[j].at[h],
                        sems.at[h * part_count + j],
                    )
                )
    for copy in stores:
        copy.start()
    for copy in stores:
        copy.wait()


def backward_pair(scal, seg, a1, near, far, w, saved, tables, part_shapes):
    length, width = a1.shape
    shape = jax.ShapeDtypeStruct
    outs = [shape((length, 3 * PAIR), bf16)] + [shape(s, bf16) for s in part_shapes]
    return pl.pallas_call(
        functools.partial(backward_kernel, len(part_shapes)),
        out_shape=tuple(outs),
        in_specs=[smem(), vmem(), vmem(), hbm(), hbm()] + [vmem()] * 10,
        out_specs=(vmem(),) + (hbm(),) * len(part_shapes),
        scratch_shapes=[
            pltpu.VMEM((length, width), bf16),
            pltpu.VMEM((2, length, 2 * PAIR), bf16),
            pltpu.VMEM((2, length, 2 * PAIR), bf16),
            pltpu.VMEM((2, length, 2 * PAIR), bf16),
            pltpu.VMEM((length, 2 * PAIR), bf16),
            pltpu.VMEM((2, length, PAIR), bf16),
            pltpu.VMEM((2, length, PAIR), bf16),
            pltpu.VMEM((length, PAIR), f32),
            pltpu.VMEM((length, PAIR), f32),
            pltpu.VMEM((length, PAIR), f32),
            pltpu.VMEM((width, 4 * PAIR), bf16),
            pltpu.SemaphoreType.DMA((16,)),
        ],
        compiler_params=params(),
        name="attention_backward",
    )(scal, seg, a1, near, far, w, *saved, *tables)


def project_kernel(count, low, high, scal, *refs):
    rows, weights, out = refs[:count], refs[count : 2 * count], refs[2 * count]
    total = None
    for one, w in zip(rows, weights):
        term = lax.dot_general(one[...], w[:, low:high], NT, preferred_element_type=f32)
        total = term if total is None else total + term
    out[...] = total.astype(out.dtype)


def project_far_half(scal, rows, weights, low, high):
    length, cols = rows[0].shape
    width = weights[0].shape[0]
    blocks = length // 2 // ROW_BLOCK
    return pl.pallas_call(
        functools.partial(project_kernel, len(rows), low, high),
        out_shape=jax.ShapeDtypeStruct((length // 2, width), bf16),
        grid_spec=pltpu.PrefetchScalarGridSpec(
            num_scalar_prefetch=1,
            grid=(blocks,),
            in_specs=[pl.BlockSpec((ROW_BLOCK, cols), lambda b, s: (b + (1 - s[2]) * blocks, 0))] * len(rows)
            + [pl.BlockSpec(w.shape, lambda b, s: (0, 0)) for w in weights],
            out_specs=pl.BlockSpec((ROW_BLOCK, width), lambda b, s: (b, 0)),
        ),
        compiler_params=params(),
        name="project_far_half",
    )(scal, *rows, *weights)


def final_kernel(count, scal, *refs):
    rows, weights = refs[:count], refs[count : 2 * count]
    tokens, far, grad_hidden, gains, out = refs[2 * count :]
    total = far[...].astype(f32)
    for one, w in zip(rows, weights):
        total = total + lax.dot_general(one[...], w[:, : 3 * PAIR], NT, preferred_element_type=f32)
    normed, inv = norm_stats(tokens[...].astype(f32))
    out[...] = grad_hidden[...] + norm_back(total * gains[0:1, :], normed, inv)


def final_rows(scal, rows, weights, tokens, far, grad_hidden, gains):
    length, cols = rows[0].shape
    width = tokens.shape[1]
    blocks = length // 2 // ROW_BLOCK
    whole = lambda a: pl.BlockSpec(a.shape, lambda b, s: (0, 0))
    near = lambda a: pl.BlockSpec((ROW_BLOCK, a.shape[1]), lambda b, s: (b + s[2] * blocks, 0))
    plain = pl.BlockSpec((ROW_BLOCK, width), lambda b, s: (b, 0))
    return pl.pallas_call(
        functools.partial(final_kernel, len(rows)),
        out_shape=jax.ShapeDtypeStruct((length // 2, width), f32),
        grid_spec=pltpu.PrefetchScalarGridSpec(
            num_scalar_prefetch=1,
            grid=(blocks,),
            in_specs=[near(r) for r in rows]
            + [whole(w) for w in weights]
            + [near(tokens), plain, plain, whole(gains)],
            out_specs=plain,
        ),
        compiler_params=params(),
        name="final_rows",
    )(scal, *rows, *weights, tokens, far, grad_hidden, gains)


def ffn_kernel(count, part_count, down_cols, scal, *refs):
    outs_of, weights = refs[:count], refs[count : 2 * count]
    tokens, far, cot, gains = refs[2 * count : 2 * count + 4]
    rest = refs[2 * count + 4 :]
    if part_count > 1:
        sources, rest = rest[: 2 * part_count], rest[2 * part_count :]
    else:
        sources, rest = rest[:2], rest[2:]
    result, dattn, grad_hidden, keep, send, w_in, w_down, z_all, pair_all, a2_all, dff_all, sems = rest
    width, ff = w_down.shape
    live, me, core = scal[0], scal[1], scal[2]
    step = pl.program_id(0)
    block = result.shape[0]

    @pl.when(step == 0)
    def _():
        copies = []
        if part_count == 1:
            copies.append(pltpu.make_async_copy(sources[0], w_in, sems.at[0]))
            copies.append(pltpu.make_async_copy(sources[1], w_down, sems.at[1]))
        else:
            offset = ff - down_cols
            rows_each = sources[0].shape[1]
            near_at = pl.multiple_of(core * offset, PAIR)
            far_from = pl.multiple_of(ff + (1 - core) * (down_cols - offset), PAIR)
            far_at = pl.multiple_of((1 - core) * down_cols, PAIR)
            for h in range(sources[0].shape[0]):
                for j in range(part_count):
                    own = jnp.bitwise_xor(me, h * part_count + j)
                    at = pl.ds(pl.multiple_of(own * rows_each, 16), rows_each)
                    number = 4 * (h * part_count + j)
                    mine, other = sources[j].at[h], sources[part_count + j].at[h]
                    copies += [
                        pltpu.make_async_copy(mine.at[:, :ff], w_in.at[core, at], sems.at[number]),
                        pltpu.make_async_copy(other.at[:, :ff], w_in.at[1 - core, at], sems.at[number + 1]),
                        pltpu.make_async_copy(
                            mine.at[:, ff:], w_down.at[at, pl.ds(near_at, down_cols)], sems.at[number + 2]
                        ),
                        pltpu.make_async_copy(
                            other.at[:, pl.ds(far_from, offset)],
                            w_down.at[at, pl.ds(far_at, offset)],
                            sems.at[number + 3],
                        ),
                    ]
        for copy in copies:
            copy.start()
        for copy in copies:
            copy.wait()

    here = core * (block * pl.num_programs(0)) + step * block
    position = here + lax.broadcasted_iota(jnp.int32, (block, 1), 0)
    valid = (position < live).astype(f32)
    attn = far[...].astype(f32)
    for one, w in zip(outs_of, weights):
        attn = attn + lax.dot_general(one[...], w[:, 3 * PAIR : 4 * PAIR], NT, preferred_element_type=f32)
    hidden = tokens[...].astype(f32) + valid * attn
    normed, inv = norm_stats(hidden)
    gain = gains[8:9, :]
    a2 = (normed * gain).astype(bf16)
    up = jnp.dot(a2, w_in[0], preferred_element_type=f32)
    gate = jnp.dot(a2, w_in[1], preferred_element_type=f32)
    below = 0.5 * (1.0 + lax.erf(up * math.sqrt(0.5)))
    act = up * below
    slope = below + up * jnp.exp(up * up * -0.5) * (1.0 / math.sqrt(2.0 * math.pi))
    z = (act * gate).astype(bf16)
    result[...] = (
        hidden + valid * lax.dot_general(z, w_down[...], NT, preferred_element_type=f32)
    ).astype(bf16)
    dy = cot[...].astype(f32)
    dff = (valid * dy).astype(bf16)
    dz = jnp.dot(dff, w_down[...], preferred_element_type=f32)
    du = (dz * gate * slope).astype(bf16)
    dg = (dz * act).astype(bf16)
    da2 = lax.dot_general(du, w_in[0], NT, preferred_element_type=f32) + lax.dot_general(
        dg, w_in[1], NT, preferred_element_type=f32
    )
    grad = dy + norm_back(da2 * gain, normed, inv)
    grad_hidden[...] = grad
    dattn[...] = (valid * grad).astype(bf16)
    rows = pl.ds(pl.multiple_of(step * block, block), block)
    z_all[rows, :] = z
    pair_all[0, rows, :] = du
    pair_all[1, rows, :] = dg
    a2_all[rows, :] = a2
    dff_all[rows, :] = dff

    @pl.when(step == pl.num_programs(0) - 1)
    def _():
        for m in range(width // ROW_BLOCK):
            part = slice(m * ROW_BLOCK, (m + 1) * ROW_BLOCK)
            left = a2_all[:, part]
            down = dff_all[:, part]
            if part_count == 1:
                for i in (0, 1):
                    keep[i, part, :] = lax.dot_general(
                        left, pair_all[i], TN, preferred_element_type=f32
                    ).astype(bf16)
                send[part, :] = lax.dot_general(down, z_all[...], TN, preferred_element_type=f32).astype(bf16)
            else:
                offset = ff - down_cols
                for out, who in ((send, 1 - core), (keep, core)):
                    out[part, :ff] = lax.dot_general(
                        left, pair_all[who], TN, preferred_element_type=f32
                    ).astype(bf16)
                    out[part, ff:] = lax.dot_general(
                        down,
                        z_all[:, pl.ds(pl.multiple_of(who * offset, PAIR), down_cols)],
                        TN,
                        preferred_element_type=f32,
                    ).astype(bf16)


def feed_forward(scal, outs_of, weights, tokens, far, cot, gains, sources, width, ff, down_cols):
    length = tokens.shape[0]
    half = length // 2
    blocks = half // ROW_BLOCK
    part_count = len(sources) // 2
    shape = jax.ShapeDtypeStruct
    whole = lambda a: pl.BlockSpec(a.shape, lambda b, s: (0,) * len(a.shape))
    near = lambda a: pl.BlockSpec((ROW_BLOCK, a.shape[1]), lambda b, s: (b + s[2] * blocks, 0))
    plain = pl.BlockSpec((ROW_BLOCK, width), lambda b, s: (b, 0))
    if part_count == 1:
        grads = (shape((2, width, ff), bf16), shape((width, ff), bf16))
    else:
        grads = (shape((width, ff + down_cols), bf16),) * 2
    return pl.pallas_call(
        functools.partial(ffn_kernel, len(outs_of), part_count, down_cols),
        out_shape=(shape((half, width), bf16), shape((half, width), bf16), shape((half, width), f32)) + grads,
        grid_spec=pltpu.PrefetchScalarGridSpec(
            num_scalar_prefetch=1,
            grid=(blocks,),
            in_specs=[near(o) for o in outs_of]
            + [whole(w) for w in weights]
            + [near(tokens), plain, plain, whole(gains)]
            + [hbm()] * len(sources),
            out_specs=(plain, plain, plain) + tuple(whole(g) for g in grads),
            scratch_shapes=[
                pltpu.VMEM((2, width, ff), bf16),
                pltpu.VMEM((width, ff), bf16),
                pltpu.VMEM((half, ff), bf16),
                pltpu.VMEM((2, half, ff), bf16),
                pltpu.VMEM((half, width), bf16),
                pltpu.VMEM((half, width), bf16),
                pltpu.SemaphoreType.DMA((64,)),
            ],
        ),
        compiler_params=params(),
        name="feed_forward",
    )(scal, *outs_of, *weights, tokens, far, cot, gains, *sources)


def pack_kernel(wide, scal, keep, got, *outs):
    me = scal[1]
    for j in range(wide):
        for h in range(outs[0].shape[0]):
            own = jnp.bitwise_xor(me, h * wide + j)
            outs[j][h] = (keep[own].astype(f32) + got[own].astype(f32)).astype(bf16)


def pack_parts(scal, keep, got, count):
    width, cols = keep.shape
    rows = width // count
    wide = 1 << bit_groups(count)[-1][1]
    shape = jax.ShapeDtypeStruct((count // wide, rows, cols), bf16)
    return pl.pallas_call(
        functools.partial(pack_kernel, wide),
        out_shape=(shape,) * wide,
        in_specs=[smem(), vmem(), vmem()],
        out_specs=(vmem(),) * wide,
        compiler_params=params(),
        name="pack_parts",
    )(scal, keep.reshape(count, rows, cols), got.reshape(count, rows, cols))


def rotary_tables(length):
    freqs = ROPE_THETA ** (-jnp.arange(0, HEAD_DIM, 2).astype(f32) / HEAD_DIM)
    angles = jnp.arange(length).astype(f32)[:, None] * freqs[None, :]
    cos, sin = jnp.cos(angles), jnp.sin(angles)
    return jnp.tile(cos, (1, 4)), jnp.tile(jnp.concatenate([-sin, sin], axis=1), (1, 2))


def mask_features(seg, live):
    column = jnp.arange(HEAD_DIM)[None, :]
    same = seg[:, None] == column
    position = jnp.arange(seg.shape[0])[:, None]
    query = jnp.where(column < 4, same.astype(f32), (column == 4).astype(f32))
    key = jnp.where(
        column < 4, jnp.where(same, 0.0, -BIG), jnp.where((column == 4) & (position >= live), -BIG, 0.0)
    )
    return jnp.tile(query, (1, 2)).astype(bf16), jnp.tile(key, (1, 2)).astype(bf16)


def local(tokens, segment_ids, counts, w_qkv, w_out, w_in, w_down, ln1_gain, ln2_gain, cotangent):
    count = lax.axis_size("dp")
    dp, core = lax.axis_index("dp"), lax.axis_index("head")
    length, width = tokens.shape[1:]
    ff = w_in.shape[2]
    rows_each = width // count
    fast = rows_each % 16 == 0 and count & (count - 1) == 0 and count >= 16
    pairs = w_qkv.shape[2] // PAIR
    first_core = core == 0
    pick = lambda a, b: jnp.where(first_core, a, b)
    join = lambda mine, other: jnp.concatenate([pick(mine, other), pick(other, mine)], axis=0)
    row, cot = tokens[0], cotangent[0]
    seg = segment_ids[0]
    live = counts[0]
    scal = jnp.stack([live, dp, core]).astype(jnp.int32)
    seg_tile = seg.reshape(-1, 128)

    out_turned = w_out.T
    both = jnp.stack([ln1_gain, ln2_gain], axis=1)
    both = join(both, core_swap(both))
    gain_cols = jnp.repeat(both, HEAD_DIM, axis=1)
    payloads = []
    for i in range(pairs):
        cols = slice(i * PAIR, (i + 1) * PAIR)
        payload = [w_qkv[0][:, cols], w_qkv[1][:, cols], w_qkv[2][:, cols], out_turned[:, cols]]
        payloads.append(jnp.concatenate(payload + ([gain_cols] if i == 0 else []), axis=1))
    if fast:
        pair_parts = [gather_parts(p, count) for p in payloads]
    else:
        pair_parts = [[lax.all_gather(p, "dp", axis=0, tiled=True)] for p in payloads]

    down_turned = w_down.T
    down_cols = -(-(ff // 2) // 128) * 128
    offset = ff - down_cols
    if fast:
        zero_one = jnp.concatenate([w_in[0], down_turned[:, :down_cols]], axis=1)
        one_two = jnp.concatenate([w_in[1], down_turned[:, offset:]], axis=1)
        got = core_swap(pick(one_two, zero_one))
        ffn_parts = gather_parts(join(pick(zero_one, one_two), got), count)
        sources = ffn_parts + [core_swap(p) for p in ffn_parts]
    else:
        sources = [
            lax.all_gather(w_in, ("dp", "head"), axis=1, tiled=True),
            lax.all_gather(down_turned, ("dp", "head"), axis=0, tiled=True),
        ]

    tables = rotary_tables(length) + mask_features(seg, live)
    a1, gains, *kept = forward_pair(True, scal, seg_tile, row, pair_parts[0], tables)
    saved = [kept]
    for i in range(1, pairs):
        saved.append(forward_pair(False, scal, seg_tile, a1, pair_parts[i], tables))
    weights = [s[0] for s in saved]
    outs_of = [s[4] for s in saved]

    far = core_swap(project_far_half(scal, outs_of, weights, 3 * PAIR, 4 * PAIR))
    result, near_grad, grad_hidden, keep, send = feed_forward(
        scal, outs_of, weights, row, far, cot, gains, sources, width, ff, down_cols
    )
    far_grad = core_swap(near_grad)

    if fast:
        parts = pack_parts(scal, keep, core_swap(send), count)
        done = reduce_parts(parts, count)
        rows_here = w_in.shape[1]
        low, high = done[:rows_here], done[rows_here:]
        mine = pick(low, high)
        other = core_swap(pick(high, low))
        grad_w_in = jnp.stack(
            [pick(mine[:, :ff], other[:, :ff]), pick(other[:, :ff], mine[:, :ff])]
        )
        grad_down = jnp.concatenate(
            [pick(mine[:, ff:], other[:, ff:]), pick(other[:, ff:], mine[:, ff:])[:, down_cols - offset :]],
            axis=1,
        ).T
    else:
        grad_w_in = lax.psum_scatter(keep.astype(f32), ("dp", "head"), scatter_dimension=1, tiled=True)
        grad_down = lax.psum_scatter(
            send.astype(f32), ("dp", "head"), scatter_dimension=0, tiled=True
        ).T
    grad_two = jnp.sum(grad_w_in * w_in.astype(f32), axis=(0, 2)) / ln2_gain.astype(f32)

    if fast:
        wide = len(pair_parts[0])
        part_shapes = [(count // wide, rows_each, 4 * PAIR)] * wide
    else:
        part_shapes = [(width, 4 * PAIR)]
    dqkv, shards = [], []
    for i in range(pairs):
        _, q, k, v, o, lse = saved[i]
        one, *parts = backward_pair(
            scal, seg_tile, a1, near_grad, far_grad, weights[i], (q, k, v, o, lse), tables, part_shapes
        )
        dqkv.append(one)
        if fast:
            shards.append(reduce_parts(parts, count))
        else:
            shards.append(lax.psum_scatter(parts[0].astype(f32), "dp", scatter_dimension=0, tiled=True))

    far_da = core_swap(project_far_half(scal, dqkv, weights, 0, 3 * PAIR))
    grad_tokens = final_rows(scal, dqkv, weights, row, far_da, grad_hidden, gains)

    grad_qkv = jnp.stack(
        [jnp.concatenate([s[:, c * PAIR : (c + 1) * PAIR] for s in shards], axis=1) for c in range(3)]
    )
    grad_out = jnp.concatenate([s[:, 3 * PAIR :] for s in shards], axis=1).T
    partial = jnp.sum(grad_qkv * w_qkv.astype(f32), axis=(0, 2))
    rows_here = ln1_gain.shape[0]
    low, high = partial[:rows_here], partial[rows_here:]
    grad_one = (pick(low, high) + core_swap(pick(high, low))) / ln1_gain.astype(f32)
    return (
        result[None],
        grad_tokens[None],
        grad_qkv,
        grad_out,
        grad_w_in,
        grad_down,
        grad_one,
        grad_two,
    )


def solution(mesh):
    placed = (
        P("dp", None, None),
        P("dp", None),
        P("dp"),
        P(None, "dp", "head"),
        P("head", "dp"),
        P(None, ("dp", "head"), None),
        P(None, ("dp", "head")),
        P(("dp", "head")),
        P(("dp", "head")),
        P("dp", "head", None),
    )
    return jax.shard_map(
        local,
        mesh=mesh,
        in_specs=placed,
        out_specs=(
            P("dp", "head", None),
            P("dp", "head", None),
            P(None, "dp", "head"),
            P("head", "dp"),
            P(None, ("dp", "head"), None),
            P(None, ("dp", "head")),
            P(("dp", "head")),
            P(("dp", "head")),
        ),
        check_vma=False,
    )
```

time: 1380 us -> 424 us (0.31)
  matrix products: 430 us -> 0 us
  waiting for transfers between devices: 395 us -> 96.5 us
  other arithmetic: 236 us -> 12.6 us
  Pallas kernels: 0 us -> 222 us
  local copies, waits for them, and re-layouts: 160 us -> 14.2 us
  blocking collectives: 129 us -> 0 us
  starting transfers between devices: 0.87 us -> 67.7 us
  between operations: 16.5 us -> 2.45 us
    dot_general x40 -> x0, matrix products: 430 us -> none  [the longest x4 72.6 us: backward_one_block(): jnp.einsum('qhe,khe->hqk', grad_blk, v_row, preferred_element_type=jnp.fl...]
    pallas_call x0 -> x15, Pallas kernels: none -> 222 us  [the longest x3 93.9 us: backward_pair(): pl.pallas_call(functools.partial(backward_kernel, len(part_shapes)), out_...]
    unnamed x13 -> x0, waiting for transfers between devices: 192 us -> none
    reduce_scatter x2 -> x0, waiting for transfers between devices: 138 us -> none  [the longest x1 128 us: local(): lax.psum_scatter(grad_out_local, 'dp', scatter_dimension=1, tiled=True)]
    convert_element_type x13 -> x3, other arithmetic: 99.6 us -> 1.66 us  [the longest x1 0.85 us: mask_features(): jnp.tile(key, (1, 2)).astype(bf16)]
    ppermute x0 -> x60, waiting for transfers between devices: none -> 96.5 us  [the longest x48 89.8 us: xor_permute(): return lax.ppermute(value, 'dp', [(i, i ^ mask) for i in range(count)])]
    unnamed x2 -> x0, blocking collectives: 82.7 us -> none
    ppermute x0 -> x60, starting transfers between devices: none -> 67.7 us  [the longest x48 66.4 us: xor_permute(): return lax.ppermute(value, 'dp', [(i, i ^ mask) for i in range(count)])]
  transfers between devices with their start and end apart: 10 -> 60, of which waited for: 6 -> 21; matrix products, arithmetic and copies ran while one was open for 57% -> 4% of each run, Pallas kernels for 0% -> 45%
where the time goes in v1:
time: 424 us; the launch traced here: 415 us
  Pallas kernels  222 us (52%)
  waiting for transfers between devices  96.5 us (23%)
  starting transfers between devices  67.7 us (16%)
  local copies, waits for them, and re-layouts  14.2 us (3%)
  other arithmetic  12.6 us (3%)
    pallas_call x3, Pallas kernels, backward_pair(): pl.pallas_call(functools.partial(backward_kernel, len(part_shapes)), out_...  93.9 us
    ppermute x48, waiting for transfers between devices, xor_permute(): return lax.ppermute(value, 'dp', [(i, i ^ mask) for i in range(count)])  89.8 us
    ppermute x48, starting transfers between devices, xor_permute(): return lax.ppermute(value, 'dp', [(i, i ^ mask) for i in range(count)])  66.4 us
    pallas_call x3, Pallas kernels, forward_pair(): pl.pallas_call(functools.partial(forward_kernel, first, len(parts)), out_...  56.5 us
    pallas_call x1, Pallas kernels, feed_forward(): pl.pallas_call(functools.partial(ffn_kernel, len(outs_of), part_count, do...  35.5 us
    pallas_call x2, Pallas kernels, project_far_half(): pl.pallas_call(functools.partial(project_kernel, len(rows), low, high), o...  13.2 us
    pallas_call x1, Pallas kernels, final_rows(): pl.pallas_call(functools.partial(final_kernel, len(rows)), out_shape=jax....  9.44 us
    pallas_call x4, Pallas kernels, sum_parts(): pl.pallas_call(functools.partial(sum_kernel, len(arrays)), out_shape=tupl...  8.57 us
  transfers between devices with their start and end apart: 60, of which 21 were waited for; matrix products, arithmetic and copies ran while one was open for 4% of the time, Pallas kernels for 45%

profile of v1, /device:TPU:0, one launch (start us, length us, event | category | flops | bytes accessed | tf_op | source)
XLA Modules:
  0.0 415.3 jit_solution(11140996248908098400)
XLA Ops:
  2.3 5.1 %collective-permute-start.15 = (bf16[1,48,512]{2,1,0:T(8,128)(2,1)S(1)}, bf16[1,48,512]{2,1,0:T(8,128)(2,1)S(1)}, u32[]{:S(2)}, u32[]{:S(2)}) collective-permute-start(bf16[1,48,512]{2,1,0:T(8,128)(2,1)S(1)} %get-tuple-element.163), channel_id=1, source_target_pairs={{0,24},{2,26},{4,28},{6,30},{8,16},{10,18},{12,20},{14,22},{16,8},... | collective-permute-start | bytes 147464 | tf_op jit(solution)/shard_map/ppermute | solution.py:56
  39.6 11.0 %collective-permute-done.17.refs_5_ = bf16[4,48,512]{2,1,0:T(8,128)(2,1)S(1)} collective-permute-done((bf16[4,48,512]{2,1,0:T(8,128)(2,1)S(1)}, bf16[4,48,512]{2,1,0:T(8,128)(2,1)S(1)}, u32[]{:S(2)}, u32[]{:S(2)}) %collective-permute-start.17) | collective-permute-done | bytes 196640 | tf_op jit(solution)/shard_map/ppermute | solution.py:56
  63.7 20.6 %attention_forward_first.1 = (bf16[2048,768]{1,0:T(8,128)(2,1)}, f32[16,768]{1,0:T(8,128)}, bf16[768,640]{1,0:T(8,128)(2,1)}, bf16[2048,128]{1,0:T(8,128)(2,1)},...) custom-call(s32[3]{0:T(128)} %pad_add_fusion.refs_0_.scal, ...), custom_call_target="tpu_custom_call" | custom-call | tf_op jit(solution)/shard_map/attention_forward_first/pallas_call | solution.py:284
  84.3 17.7 %attention_forward.3 = (bf16[768,512]{1,0:T(8,128)(2,1)}, bf16[2048,128]{1,0:T(8,128)(2,1)}, bf16[2048,128]{1,0:T(8,128)(2,1)}, bf16[2048,128]{1,0:T(8,128)(2,1)...) custom-call(s32[3]{0:T(128)} %pad_add_fusion.refs_0_.scal, s32[16,128]{1,0:T(8,128)} %bitcast.91, ...), custom_call_target="tpu_custom_call" | custom-call | tf_op jit(solution)/shard_map/attention_forward/pallas_call | solution.py:284
  102.1 18.2 %attention_forward.2 = (bf16[768,512]{1,0:T(8,128)(2,1)}, bf16[2048,128]{1,0:T(8,128)(2,1)}, bf16[2048,128]{1,0:T(8,128)(2,1)}, bf16[2048,128]{1,0:T(8,128)(2,1)...) custom-call(s32[3]{0:T(128)} %pad_add_fusion.refs_0_.scal, s32[16,128]{1,0:T(8,128)} %bitcast.92, ...), custom_call_target="tpu_custom_call" | custom-call | tf_op jit(solution)/shard_map/attention_forward/pallas_call | solution.py:284
  120.3 5.8 %project_far_half.2 = bf16[1024,768]{1,0:T(8,128)(2,1)} custom-call(s32[3]{0:T(128)} %pad_add_fusion.refs_0_.scal, bf16[2048,128]{1,0:T(8,128)(2,1)} %get-tuple-element.68.refs_0_.refs_9_, bf16[2048,128]{1,0:T(8,128)(2,1)} %get-tuple-element.70.refs_1_.refs_9_, bf16[2048,128]{1,0:T(8,128)(2,1)} %get-tuple-element.71.refs_2_.refs_9_, ...), custom_call_target="tpu_custom_call" | custom-call | tf_op jit(solution)/shard_map/project_far_half/pallas_call | solution.py:458
  130.9 15.7 %collective-permute-done.26.refs_13_ = bf16[4,48,1792]{2,1,0:T(8,128)(2,1)S(1)} collective-permute-done((bf16[4,48,1792]{2,1,0:T(8,128)(2,1)S(1)}, bf16[4,48,1792]{2,1,0:T(8,128)(2,1)S(1)}, u32[]{:S(2)}, u32[]{:S(2)}) %collective-permute-start.26) | collective-permute-done | bytes 688160 | tf_op jit(solution)/shard_map/ppermute | solution.py:56
  146.6 13.5 %collective-permute-done.25.refs_12_ = bf16[4,48,1792]{2,1,0:T(8,128)(2,1)S(1)} collective-permute-done((bf16[4,48,1792]{2,1,0:T(8,128)(2,1)S(1)}, bf16[4,48,1792]{2,1,0:T(8,128)(2,1)S(1)}, u32[]{:S(2)}, u32[]{:S(2)}) %collective-permute-start.25) | collective-permute-done | bytes 688160 | tf_op jit(solution)/shard_map/ppermute | solution.py:56
  164.7 35.5 %feed_forward.1 = (bf16[1024,768]{1,0:T(8,128)(2,1)}, bf16[1024,768]{1,0:T(8,128)(2,1)}, f32[1024,768]{1,0:T(8,128)}, bf16[768,1792]{1,0:T(8,128)(2,1)}, bf16[768,1792]{1,0:T(8,128)(2,1)}) custom-call(s32[3]{0:T(128)} %pad_add_fusion.refs_0_.scal, bf16[2048,128]{1,0:T(8,128)(2,1)} %get-tuple-element.68.refs_0_.refs_9_, ...), custom_call_target="tpu_custom_call" | custom-call | tf_op jit(solution)/shard_map/feed_forward/pallas_call | solution.py:631
  200.8 4.1 collective-permute-done.31.refs_4_
  206.0 31.4 %attention_backward.5 = (bf16[2048,384]{1,0:T(8,128)(2,1)}, bf16[4,48,512]{2,1,0:T(8,128)(2,1)}, bf16[4,48,512]{2,1,0:T(8,128)(2,1)}, bf16[4,48,512]{2,1,0:T(8,128)(2,1)}, bf16[4,48,512]{2,1,0:T(8,128)(2,1)}) custom-call(s32[3]{0:T(128)} %pad_add_fusion.refs_0_.scal, s32[16,128]{1,0:T(8,128)} %bitcast.93, bf16[2048,768]{1,0:T(8,128)(2,1)} %get-tuple-element.69.refs_2_, ...), custom_call_target="tpu_custom_call" | custom-call | tf_op jit(solution)/shard_map/attention_backward/pallas_call | solution.py:421
  241.0 31.2 %attention_backward.4 = (bf16[2048,384]{1,0:T(8,128)(2,1)}, bf16[4,48,512]{2,1,0:T(8,128)(2,1)}, bf16[4,48,512]{2,1,0:T(8,128)(2,1)}, bf16[4,48,512]{2,1,0:T(8,128)(2,1)}, bf16[4,48,512]{2,1,0:T(8,128)(2,1)}) custom-call(s32[3]{0:T(128)} %pad_add_fusion.refs_0_.scal, s32[16,128]{1,0:T(8,128)} %bitcast.94, bf16[2048,768]{1,0:T(8,128)(2,1)} %get-tuple-element.69.refs_2_, ...), custom_call_target="tpu_custom_call" | custom-call | tf_op jit(solution)/shard_map/attention_backward/pallas_call | solution.py:421
  272.9 31.2 %attention_backward.3 = (bf16[2048,384]{1,0:T(8,128)(2,1)}, bf16[4,48,512]{2,1,0:T(8,128)(2,1)}, bf16[4,48,512]{2,1,0:T(8,128)(2,1)}, bf16[4,48,512]{2,1,0:T(8,128)(2,1)}, bf16[4,48,512]{2,1,0:T(8,128)(2,1)}) custom-call(s32[3]{0:T(128)} %pad_add_fusion.refs_0_.scal, s32[16,128]{1,0:T(8,128)} %bitcast.95, bf16[2048,768]{1,0:T(8,128)(2,1)} %get-tuple-element.69.refs_2_, ...), custom_call_target="tpu_custom_call" | custom-call | tf_op jit(solution)/shard_map/attention_backward/pallas_call | solution.py:421
  314.0 3.4 collective-permute-done.33.refs_1_
  317.4 4.0 collective-permute-start.50
  321.4 7.4 %project_far_half.3 = bf16[1024,768]{1,0:T(8,128)(2,1)} custom-call(s32[3]{0:T(128)} %pad_add_fusion.refs_0_.scal, bf16[2048,384]{1,0:T(8,128)(2,1)} %get-tuple-element.82.refs_0_, bf16[2048,384]{1,0:T(8,128)(2,1)} %get-tuple-element.87.refs_1_, bf16[2048,384]{1,0:T(8,128)(2,1)} %get-tuple-element.92.refs_2_, ...), custom_call_target="tpu_custom_call" | custom-call | tf_op jit(solution)/shard_map/project_far_half/pallas_call | solution.py:458
  334.0 3.8 collective-permute-start.44
  341.0 3.3 collective-permute-start.38
  348.0 4.8 %pack_parts.1 = (bf16[4,48,1792]{2,1,0:T(8,128)(2,1)}, bf16[4,48,1792]{2,1,0:T(8,128)(2,1)}, bf16[4,48,1792]{2,1,0:T(8,128)(2,1)}, bf16[4,48,1792]{2,1,0:T(8,128)(2,1)}) custom-call(s32[3]{0:T(128)} %pad_add_fusion.refs_0_.scal, bf16[16,48,1792]{2,1,0:T(8,128)(2,1)} %bitcast.84, bf16[16,48,1792]{2,1,0:T(8,128)(2,1)} %bitcast.51.got), custom_call_target="tpu_custom_call" | custom-call | tf_op jit(solution)/shard_map/pack_parts/pallas_call | solution.py:670
  357.2 14.1 %collective-permute-done.52.refs_1_ = bf16[4,48,1792]{2,1,0:T(8,128)(2,1)S(1)} collective-permute-done((bf16[4,48,1792]{2,1,0:T(8,128)(2,1)}, bf16[4,48,1792]{2,1,0:T(8,128)(2,1)S(1)}, u32[]{:S(2)}, u32[]{:S(2)}) %collective-permute-start.52) | collective-permute-done | bytes 688160 | tf_op jit(solution)/shard_map/ppermute | solution.py:56
  371.3 12.3 %collective-permute-done.53.refs_2_ = bf16[4,48,1792]{2,1,0:T(8,128)(2,1)S(1)} collective-permute-done((bf16[4,48,1792]{2,1,0:T(8,128)(2,1)}, bf16[4,48,1792]{2,1,0:T(8,128)(2,1)S(1)}, u32[]{:S(2)}, u32[]{:S(2)}) %collective-permute-start.53) | collective-permute-done | bytes 688160 | tf_op jit(solution)/shard_map/ppermute | solution.py:56
  387.5 3.6 collective-permute-start.56
  395.8 4.7 %collective-permute-done.56 = bf16[48,1792]{1,0:T(8,128)(2,1)S(1)} collective-permute-done((bf16[48,1792]{1,0:T(8,128)(2,1)}, bf16[48,1792]{1,0:T(8,128)(2,1)S(1)}, u32[]{:S(2)}, u32[]{:S(2)}) %collective-permute-start.56) | collective-permute-done | bytes 172064 | tf_op jit(solution)/shard_map/ppermute | solution.py:56
  403.5 9.4 %final_rows.1 = f32[1024,768]{1,0:T(8,128)} custom-call(s32[3]{0:T(128)} %pad_add_fusion.refs_0_.scal, bf16[2048,384]{1,0:T(8,128)(2,1)} %get-tuple-element.82.refs_0_, bf16[2048,384]{1,0:T(8,128)(2,1)} %get-tuple-element.87.refs_1_, bf16[2048,384]{1,0:T(8,128)(2,1)} %get-tuple-element.92.refs_2_, bf16[768,640]{1,0:T(8,128)(2,1)} %get-tuple-element.72.refs_3_.refs_5_, ...), custom_call_target="tpu_custom_call" | custom-call | tf_op jit(solution)/shard_map/final_rows/pallas_call | solution.py:490
  (255 shorter events, 101.0 us)
Async XLA Ops:
  2.3 21.5 %collective-permute-start.15 = (bf16[1,48,512]{2,1,0:T(8,128)(2,1)S(1)}, bf16[1,48,512]{2,1,0:T(8,128)(2,1)S(1)}, u32[]{:S(2)}, u32[]{:S(2)}) collective-permute-start(bf16[1,48,512]{2,1,0:T(8,128)(2,1)S(1)} %get-tuple-element.163), channel_id=1, source_target_pairs={{0,24},{2,26},{4,28},{6,30},{8,16},{10,18},{12,20},{14,22},{16,8},... | collective-permute-start | bytes 147464 | tf_op jit(solution)/shard_map/ppermute | solution.py:56
  29.5 24.1 %collective-permute-start.6 = (bf16[4,48,640]{2,1,0:T(8,128)(2,1)S(1)}, bf16[4,48,640]{2,1,0:T(8,128)(2,1)S(1)}, u32[]{:S(2)}, u32[]{:S(2)}) collective-permute-start(bf16[4,48,640]{2,1,0:T(8,128)(2,1)S(1)} %maximum_bitcast_fusion.1.refs_3_), channel_id=1, source_target_pairs={{0,6},{2,4},{4,2},{6,0},{8,14},{10,12},{12,10},{14,8},{16,22},{18,... | collective-permute-start | bytes 737288 | tf_op jit(solution)/shard_map/ppermute | solution.py:56
  32.0 24.5 %collective-permute-start.5 = (bf16[4,48,640]{2,1,0:T(8,128)(2,1)S(1)}, bf16[4,48,640]{2,1,0:T(8,128)(2,1)S(1)}, u32[]{:S(2)}, u32[]{:S(2)}) collective-permute-start(bf16[4,48,640]{2,1,0:T(8,128)(2,1)S(1)} %maximum_bitcast_fusion.1.refs_3_), channel_id=1, source_target_pairs={{0,4},{2,6},{4,0},{6,2},{8,12},{10,14},{12,8},{14,10},{16,20},{18,... | collective-permute-start | bytes 737288 | tf_op jit(solution)/shard_map/ppermute | solution.py:56
  32.5 24.0 %collective-permute-start.4 = (bf16[4,48,640]{2,1,0:T(8,128)(2,1)S(1)}, bf16[4,48,640]{2,1,0:T(8,128)(2,1)S(1)}, u32[]{:S(2)}, u32[]{:S(2)}) collective-permute-start(bf16[4,48,640]{2,1,0:T(8,128)(2,1)S(1)} %maximum_bitcast_fusion.1.refs_3_), channel_id=1, source_target_pairs={{0,2},{2,0},{4,6},{6,4},{8,10},{10,8},{12,14},{14,12},{16,18},{18,... | collective-permute-start | bytes 737288 | tf_op jit(solution)/shard_map/ppermute | solution.py:56
  50.6 51.4 %collective-permute-start.11 = (bf16[4,48,512]{2,1,0:T(8,128)(2,1)S(1)}, bf16[4,48,512]{2,1,0:T(8,128)(2,1)}, u32[]{:S(2)}, u32[]{:S(2)}) collective-permute-start(bf16[4,48,512]{2,1,0:T(8,128)(2,1)S(1)} %maximum_bitcast_fusion.2.refs_3_), channel_id=1, source_target_pairs={{0,4},{2,6},{4,0},{6,2},{8,12},{10,14},{12,8},{14,10},{16,20},{18,... | collective-permute-start | bytes 589832 | tf_op jit(solution)/shard_map/ppermute | solution.py:56
  52.1 49.9 %collective-permute-start.10 = (bf16[4,48,512]{2,1,0:T(8,128)(2,1)S(1)}, bf16[4,48,512]{2,1,0:T(8,128)(2,1)}, u32[]{:S(2)}, u32[]{:S(2)}) collective-permute-start(bf16[4,48,512]{2,1,0:T(8,128)(2,1)S(1)} %maximum_bitcast_fusion.2.refs_3_), channel_id=1, source_target_pairs={{0,2},{2,0},{4,6},{6,4},{8,10},{10,8},{12,14},{14,12},{16,18},{18,... | collective-permute-start | bytes 589832 | tf_op jit(solution)/shard_map/ppermute | solution.py:56
  53.6 72.5 %collective-permute-start.23 = (bf16[1,48,1792]{2,1,0:T(8,128)(2,1)S(1)}, bf16[1,48,1792]{2,1,0:T(8,128)(2,1)}, u32[]{:S(2)}, u32[]{:S(2)}) collective-permute-start(bf16[1,48,1792]{2,1,0:T(8,128)(2,1)S(1)} %get-tuple-element.142), channel_id=1, source_target_pairs={{0,24},{2,26},{4,28},{6,30},{8,16},{10,18},{12,20},{14,22},{16,8},... | collective-permute-start | bytes 516104 | tf_op jit(solution)/shard_map/ppermute | solution.py:56
  56.5 69.7 %collective-permute-start.22 = (bf16[1,48,1792]{2,1,0:T(8,128)(2,1)S(1)}, bf16[1,48,1792]{2,1,0:T(8,128)(2,1)}, u32[]{:S(2)}, u32[]{:S(2)}) collective-permute-start(bf16[1,48,1792]{2,1,0:T(8,128)(2,1)S(1)} %get-tuple-element.142), channel_id=1, source_target_pairs={{0,16},{2,18},{4,20},{6,22},{8,24},{10,26},{12,28},{14,30},{16,0},... | collective-permute-start | bytes 516104 | tf_op jit(solution)/shard_map/ppermute | solution.py:56
  56.5 69.7 %collective-permute-start.21 = (bf16[1,48,1792]{2,1,0:T(8,128)(2,1)S(1)}, bf16[1,48,1792]{2,1,0:T(8,128)(2,1)}, u32[]{:S(2)}, u32[]{:S(2)}) collective-permute-start(bf16[1,48,1792]{2,1,0:T(8,128)(2,1)S(1)} %get-tuple-element.142), channel_id=1, source_target_pairs={{0,8},{2,10},{4,12},{6,14},{8,0},{10,2},{12,4},{14,6},{16,24},{18,... | collective-permute-start | bytes 516104 | tf_op jit(solution)/shard_map/ppermute | solution.py:56
  126.1 37.1 %collective-permute-start.19 = (bf16[1024,768]{1,0:T(8,128)(2,1)}, bf16[1024,768]{1,0:T(8,128)(2,1)S(1)}, u32[]{:S(2)}, u32[]{:S(2)}) collective-permute-start(bf16[1024,768]{1,0:T(8,128)(2,1)} %project_far_half.2), channel_id=1, source_target_pairs={{0,1},{1,0},{2,3},{3,2},{4,5},{5,4},{6,7},{7,6},{8,9},{9,8},{10,11... | collective-permute-start | bytes 4718600 | tf_op jit(solution)/shard_map/ppermute | solution.py:60
  127.4 32.6 %collective-permute-start.25 = (bf16[4,48,1792]{2,1,0:T(8,128)(2,1)S(1)}, bf16[4,48,1792]{2,1,0:T(8,128)(2,1)S(1)}, u32[]{:S(2)}, u32[]{:S(2)}) collective-permute-start(bf16[4,48,1792]{2,1,0:T(8,128)(2,1)S(1)} %maximum_bitcast_fusion.refs_10_), channel_id=1, source_target_pairs={{0,4},{2,6},{4,0},{6,2},{8,12},{10,14},{12,8},{14,10},{16,20},{18,... | collective-permute-start | bytes 2064392 | tf_op jit(solution)/shard_map/ppermute | solution.py:56
  127.9 32.2 %collective-permute-start.24 = (bf16[4,48,1792]{2,1,0:T(8,128)(2,1)S(1)}, bf16[4,48,1792]{2,1,0:T(8,128)(2,1)S(1)}, u32[]{:S(2)}, u32[]{:S(2)}) collective-permute-start(bf16[4,48,1792]{2,1,0:T(8,128)(2,1)S(1)} %maximum_bitcast_fusion.refs_10_), channel_id=1, source_target_pairs={{0,2},{2,0},{4,6},{6,4},{8,10},{10,8},{12,14},{14,12},{16,18},{18,... | collective-permute-start | bytes 2064392 | tf_op jit(solution)/shard_map/ppermute | solution.py:56
  130.9 29.7 %collective-permute-start.27 = (bf16[4,48,1792]{2,1,0:T(8,128)(2,1)S(1)}, bf16[4,48,1792]{2,1,0:T(8,128)(2,1)S(1)}, u32[]{:S(2)}, u32[]{:S(2)}) collective-permute-start(bf16[4,48,1792]{2,1,0:T(8,128)(2,1)S(1)} %maximum_bitcast_fusion.refs_10_), channel_id=1, source_target_pairs={{0,1},{1,0},{2,3},{3,2},{4,5},{5,4},{6,7},{7,6},{8,9},{9,8},{10,11... | collective-permute-start | bytes 2064392 | tf_op jit(solution)/shard_map/ppermute | solution.py:60
  200.4 147.6 %collective-permute-start.51 = (bf16[768,1792]{1,0:T(8,128)(2,1)}, bf16[768,1792]{1,0:T(8,128)(2,1)}, u32[]{:S(2)}, u32[]{:S(2)}) collective-permute-start(bf16[768,1792]{1,0:T(8,128)(2,1)} %get-tuple-element.119), channel_id=1, source_target_pairs={{0,1},{1,0},{2,3},{3,2},{4,5},{5,4},{6,7},{7,6},{8,9},{9,8},{10,11... | collective-permute-start | bytes 8257544 | tf_op jit(solution)/shard_map/ppermute | solution.py:60
  237.5 34.9 %collective-permute-start.45 = (bf16[4,48,512]{2,1,0:T(8,128)(2,1)}, bf16[4,48,512]{2,1,0:T(8,128)(2,1)S(1)}, u32[]{:S(2)}, u32[]{:S(2)}) collective-permute-start(bf16[4,48,512]{2,1,0:T(8,128)(2,1)} %get-tuple-element.111), channel_id=1, source_target_pairs={{0,2},{2,0},{4,6},{6,4},{8,10},{10,8},{12,14},{14,12},{16,18},{18,... | collective-permute-start | bytes 589832 | tf_op jit(solution)/shard_map/ppermute | solution.py:56
  237.5 66.6 %collective-permute-start.46 = (bf16[4,48,512]{2,1,0:T(8,128)(2,1)}, bf16[4,48,512]{2,1,0:T(8,128)(2,1)S(1)}, u32[]{:S(2)}, u32[]{:S(2)}) collective-permute-start(bf16[4,48,512]{2,1,0:T(8,128)(2,1)} %get-tuple-element.112), channel_id=1, source_target_pairs={{0,4},{2,6},{4,0},{6,2},{8,12},{10,14},{12,8},{14,10},{16,20},{18,... | collective-permute-start | bytes 589832 | tf_op jit(solution)/shard_map/ppermute | solution.py:56
  238.0 66.3 %collective-permute-start.47 = (bf16[4,48,512]{2,1,0:T(8,128)(2,1)}, bf16[4,48,512]{2,1,0:T(8,128)(2,1)S(1)}, u32[]{:S(2)}, u32[]{:S(2)}) collective-permute-start(bf16[4,48,512]{2,1,0:T(8,128)(2,1)} %get-tuple-element.113), channel_id=1, source_target_pairs={{0,6},{2,4},{4,2},{6,0},{8,14},{10,12},{12,10},{14,8},{16,22},{18,... | collective-permute-start | bytes 589832 | tf_op jit(solution)/shard_map/ppermute | solution.py:56
  272.3 35.1 %collective-permute-start.39 = (bf16[4,48,512]{2,1,0:T(8,128)(2,1)}, bf16[4,48,512]{2,1,0:T(8,128)(2,1)S(1)}, u32[]{:S(2)}, u32[]{:S(2)}) collective-permute-start(bf16[4,48,512]{2,1,0:T(8,128)(2,1)} %get-tuple-element.103), channel_id=1, source_target_pairs={{0,2},{2,0},{4,6},{6,4},{8,10},{10,8},{12,14},{14,12},{16,18},{18,... | collective-permute-start | bytes 589832 | tf_op jit(solution)/shard_map/ppermute | solution.py:56
  272.4 35.4 %collective-permute-start.40 = (bf16[4,48,512]{2,1,0:T(8,128)(2,1)}, bf16[4,48,512]{2,1,0:T(8,128)(2,1)S(1)}, u32[]{:S(2)}, u32[]{:S(2)}) collective-permute-start(bf16[4,48,512]{2,1,0:T(8,128)(2,1)} %get-tuple-element.104), channel_id=1, source_target_pairs={{0,4},{2,6},{4,0},{6,2},{8,12},{10,14},{12,8},{14,10},{16,20},{18,... | collective-permute-start | bytes 589832 | tf_op jit(solution)/shard_map/ppermute | solution.py:56
  307.8 23.0 %collective-permute-start.35 = (bf16[4,48,512]{2,1,0:T(8,128)(2,1)}, bf16[4,48,512]{2,1,0:T(8,128)(2,1)S(1)}, u32[]{:S(2)}, u32[]{:S(2)}) collective-permute-start(bf16[4,48,512]{2,1,0:T(8,128)(2,1)} %get-tuple-element.97), channel_id=1, source_target_pairs={{0,6},{2,4},{4,2},{6,0},{8,14},{10,12},{12,10},{14,8},{16,22},{18,... | collective-permute-start | bytes 589832 | tf_op jit(solution)/shard_map/ppermute | solution.py:56
  313.0 20.4 %collective-permute-start.48 = (bf16[48,512]{1,0:T(8,128)(2,1)}, bf16[48,512]{1,0:T(8,128)(2,1)S(1)}, u32[]{:S(2)}, u32[]{:S(2)}) collective-permute-start(bf16[48,512]{1,0:T(8,128)(2,1)} %get-tuple-element.115), channel_id=1, source_target_pairs={{0,8},{2,10},{4,12},{6,14},{8,0},{10,2},{12,4},{14,6},{16,24},{18,... | collective-permute-start | bytes 147464 | tf_op jit(solution)/shard_map/ppermute | solution.py:56
  330.8 71.6 %collective-permute-start.32 = (bf16[1024,768]{1,0:T(8,128)(2,1)}, bf16[1024,768]{1,0:T(8,128)(2,1)S(1)}, u32[]{:S(2)}, u32[]{:S(2)}) collective-permute-start(bf16[1024,768]{1,0:T(8,128)(2,1)} %project_far_half.3), channel_id=1, source_target_pairs={{0,1},{1,0},{2,3},{3,2},{4,5},{5,4},{6,7},{7,6},{8,9},{9,8},{10,11... | collective-permute-start | bytes 4718600 | tf_op jit(solution)/shard_map/ppermute | solution.py:60
  354.0 29.7 %collective-permute-start.53 = (bf16[4,48,1792]{2,1,0:T(8,128)(2,1)}, bf16[4,48,1792]{2,1,0:T(8,128)(2,1)S(1)}, u32[]{:S(2)}, u32[]{:S(2)}) collective-permute-start(bf16[4,48,1792]{2,1,0:T(8,128)(2,1)} %get-tuple-element.122), channel_id=1, source_target_pairs={{0,4},{2,6},{4,0},{6,2},{8,12},{10,14},{12,8},{14,10},{16,20},{18,... | collective-permute-start | bytes 2064392 | tf_op jit(solution)/shard_map/ppermute | solution.py:56
  356.3 27.4 %collective-permute-start.54 = (bf16[4,48,1792]{2,1,0:T(8,128)(2,1)}, bf16[4,48,1792]{2,1,0:T(8,128)(2,1)S(1)}, u32[]{:S(2)}, u32[]{:S(2)}) collective-permute-start(bf16[4,48,1792]{2,1,0:T(8,128)(2,1)} %get-tuple-element.123), channel_id=1, source_target_pairs={{0,6},{2,4},{4,2},{6,0},{8,14},{10,12},{12,10},{14,8},{16,22},{18,... | collective-permute-start | bytes 2064392 | tf_op jit(solution)/shard_map/ppermute | solution.py:56
  (77 other events, 840.0 us)

commit v2 on v1

v2 whole, which is shorter than its diff:
```python
import functools
import math

import jax
import jax.numpy as jnp
import numpy as np
from jax import lax
from jax.experimental import pallas as pl
from jax.experimental.pallas import tpu as pltpu
from jax.sharding import PartitionSpec as P

HEAD_DIM = 64
PAIR = 2 * HEAD_DIM
LAYER_EPS = 1e-05
ROPE_THETA = 160000.0
BIG = 1e30
LOG2_SCALE = math.log2(math.e) / math.sqrt(HEAD_DIM)
SCORE_SCALE = 1.0 / math.sqrt(HEAD_DIM)
ROW_BLOCK = 256
FWD_MIB, BWD_MIB, FFN_MIB = 32, 40, 44
FWD_BQ, FWD_STEP = 512, 256
BWD_BQ, BWD_STEP = 256, 512
NT = (((1,), (1,)), ((), ()))
TN = (((0,), (0,)), ((), ()))
bf16 = jnp.bfloat16
f32 = jnp.float32


def vmem():
    return pl.BlockSpec(memory_space=pltpu.VMEM)


def smem():
    return pl.BlockSpec(memory_space=pltpu.SMEM)


def hbm():
    return pl.BlockSpec(memory_space=pltpu.HBM)


def anywhere():
    return pl.BlockSpec(memory_space=pl.ANY)


def params(mib=16):
    return pltpu.CompilerParams(vmem_limit_bytes=mib << 20)


def lasts(micros):
    return pl.CostEstimate(flops=int(micros * 1e8), bytes_accessed=0, transcendentals=0)


def passing(kernel, inputs, deps):
    def run(*refs):
        kernel(*refs[:inputs], *refs[inputs + deps :])

    return run


def bit_groups(count):
    bits = count.bit_length() - 1
    shifts = []
    low = 0
    while low < bits:
        wide = min(2, bits - low)
        shifts.append((low, wide))
        low += wide
    return shifts[::-1]


def xor_permute(value, count, mask):
    return lax.ppermute(value, "dp", [(i, i ^ mask) for i in range(count)])


def core_swap(value):
    return lax.ppermute(value, "head", [(0, 1), (1, 0)])


def stack_kernel(*refs):
    ins, out = refs[:-1], refs[-1]
    wide = len(ins)
    for j, one in enumerate(ins):
        for h in range(one.shape[0]):
            out[h * wide + j] = one[h]


def stack_parts(parts, deps=()):
    m, rows, cols = parts[0].shape
    return pl.pallas_call(
        passing(stack_kernel, len(parts), len(deps)),
        out_shape=jax.ShapeDtypeStruct((m * len(parts), rows, cols), parts[0].dtype),
        in_specs=[vmem()] * len(parts) + [anywhere()] * len(deps),
        out_specs=vmem(),
        compiler_params=params(),
        cost_estimate=lasts(1),
        name="stack_parts",
    )(*parts, *deps)


def gather_step(current, count, group):
    shift, wide = group
    return [current] + [xor_permute(current, count, j << shift) for j in range(1, 1 << wide)]


def sum_kernel(count, *refs):
    ins, outs = refs[:count], refs[count:]
    for i, out in enumerate(outs):
        total = ins[0][i].astype(f32)
        for one in ins[1:]:
            total = total + one[i].astype(f32)
        out[...] = total.astype(out.dtype)


def sum_parts(arrays, deps=()):
    m, rows, cols = arrays[0].shape
    return pl.pallas_call(
        passing(functools.partial(sum_kernel, len(arrays)), len(arrays), len(deps)),
        out_shape=tuple(
            jax.ShapeDtypeStruct((rows, cols), f32 if i == 0 else bf16) for i in range(m)
        ),
        in_specs=[vmem()] * len(arrays) + [anywhere()] * len(deps),
        out_specs=(vmem(),) * m,
        compiler_params=params(),
        cost_estimate=lasts(2),
        name="sum_parts",
    )(*arrays, *deps)


def reduce_near(parts, count):
    return [parts[0]] + [xor_permute(parts[j], count, j) for j in range(1, len(parts))]


def reduce_far(pieces, count, wide):
    shift = wide.bit_length() - 1
    total = pieces[0]
    for h in range(1, len(pieces)):
        total = total + xor_permute(pieces[h], count, h << shift).astype(f32)
    return total


def load_kernel(pairs, scal, w_qkv, out_turned, mine, other, head, rest):
    for c in range(3):
        head[:, c * PAIR : (c + 1) * PAIR] = w_qkv[c, :, :PAIR]
        for i in range(1, pairs):
            at = (3 * (i - 1) + c) * PAIR
            rest[:, at : at + PAIR] = w_qkv[c, :, i * PAIR : (i + 1) * PAIR]
    rest[:, 3 * PAIR * (pairs - 1) :] = out_turned[...]
    mine, other = mine[...].astype(f32), other[...].astype(f32)
    first = scal[2] == 0
    gains = jnp.concatenate([jnp.where(first, mine, other), jnp.where(first, other, mine)], axis=0)
    low = lax.broadcasted_iota(jnp.int32, (gains.shape[0], PAIR), 1) < HEAD_DIM
    head[:, 3 * PAIR :] = jnp.where(low, gains[:, 0:1], gains[:, 1:2]).astype(bf16)


def attention_loads(scal, w_qkv, out_turned, mine, other):
    rows, cols = w_qkv.shape[1:]
    pairs = cols // PAIR
    shape = jax.ShapeDtypeStruct
    return pl.pallas_call(
        functools.partial(load_kernel, pairs),
        out_shape=(shape((rows, 4 * PAIR), bf16), shape((rows, 3 * PAIR * (pairs - 1) + cols), bf16)),
        in_specs=[smem()] + [vmem()] * 4,
        out_specs=(vmem(),) * 2,
        compiler_params=params(),
        cost_estimate=lasts(1),
        name="attention_loads",
    )(scal, w_qkv, out_turned, mine, other)


def placed_copies(parts, target, sems, me, rows):
    if len(parts) == 1:
        return [pltpu.make_async_copy(parts[0], target, sems.at[0])]
    copies = []
    wide = len(parts)
    for h in range(parts[0].shape[0]):
        for j in range(wide):
            own = jnp.bitwise_xor(me, h * wide + j)
            copies.append(
                pltpu.make_async_copy(
                    parts[j].at[h],
                    target.at[pl.ds(pl.multiple_of(own * rows, 16), rows)],
                    sems.at[h * wide + j],
                )
            )
    return copies


def document_starts(seg, length):
    starts = [jnp.int32(0)]
    for d in (1, 2, 3):
        starts.append(jnp.sum((seg < d).astype(jnp.int32)))
    return starts + [jnp.int32(length)]


def key_range(starts, live, first, size, length):
    last = jnp.minimum(first + size, live) - 1
    low = jnp.int32(0)
    high = jnp.int32(length)
    for d in (1, 2, 3):
        low = jnp.where(starts[d] <= first, starts[d], low)
    for d in (3, 2, 1):
        high = jnp.where(starts[d] > last, starts[d], high)
    high = jnp.minimum(high, live)
    return low, jnp.where(first < live, high, low)


def each_query_block(starts, live, length, size, step, work, empty):
    @pl.loop(0, length // size)
    def _(i):
        first = pl.multiple_of(i * size, size)
        low, high = key_range(starts, live, first, size, length)
        base = low // 16 * 16
        steps = (high - base + step - 1) // step
        base = pl.multiple_of(jnp.maximum(jnp.minimum(base, length - steps * step), 0), 16)
        rows = pl.ds(first, size)
        for w in range(1, length // step + 1):

            @pl.when(steps == w)
            def _():
                work(rows, pl.ds(base, w * step))

        @pl.when(steps <= 0)
        def _():
            empty(rows)


def lane_bounds(starts, live, length):
    column = lax.broadcasted_iota(jnp.int32, (1, PAIR), 1) & (HEAD_DIM - 1)
    low = jnp.zeros((1, PAIR), jnp.int32)
    high = jnp.where(column == 4, live, length)
    for d in range(4):
        low = jnp.where(column == d, starts[d], low)
        high = jnp.where(column == d, starts[d + 1], high)
    return column, low, high


def mask_features(bounds, first, size):
    column, low, high = bounds
    position = first + lax.broadcasted_iota(jnp.int32, (size, PAIR), 0)
    inside = (position >= low) & (position < high)
    column = jnp.broadcast_to(column, (size, PAIR))
    query = jnp.where((inside & (column < 4)) | (column == 4), 1.0, 0.0)
    return query, jnp.where(inside, 0.0, -BIG)


def rotary_block(table, turns, block):
    cos, sin = table[0], table[1]
    cos_at, sin_at = turns[0, pl.ds(block, 1), :], turns[1, pl.ds(block, 1), :]
    return cos * cos_at - sin * sin_at, sin * cos_at + cos * sin_at


def norm_stats(values):
    center = values - jnp.mean(values, axis=-1, keepdims=True)
    spread = jnp.mean(center * center, axis=-1, keepdims=True)
    inv = lax.rsqrt(spread + LAYER_EPS)
    return center * inv, inv


def norm_back(grad, normed, inv):
    return inv * (
        grad
        - jnp.mean(grad, axis=-1, keepdims=True)
        - normed * jnp.mean(grad * normed, axis=-1, keepdims=True)
    )


def half_swap(values, in_first):
    return jnp.where(in_first, pltpu.roll(values, PAIR - HEAD_DIM // 2, 1), pltpu.roll(values, HEAD_DIM // 2, 1))


def split3(values):
    a = values.astype(bf16)
    left = values - a.astype(f32)
    b = left.astype(bf16)
    return a, b, (left - b.astype(f32)).astype(bf16)


def forward_kernel(first, part_count, at, *refs):
    scal, seg, src, table, turns = refs[:5]
    parts = refs[5 : 5 + max(part_count, 1)]
    outs = refs[5 + max(part_count, 1) :]
    if first:
        a1, gains = outs[:2]
        outs = outs[2:]
    if part_count:
        w, outs = outs[0], outs[1:]
    else:
        w = parts[0]
    q_out, k_out, v_out, o_out, lse_out, qx, kx, vx, sems = outs
    length, width = src.shape
    live, me = scal[0], scal[1]

    copies = placed_copies(parts, w, sems, me, parts[0].shape[-2]) if part_count else []
    for copy in copies:
        copy.start()
    starts = document_starts(seg[...], length)
    bounds = lane_bounds(starts, live, length)
    for copy in copies:
        copy.wait()
    if first:
        turned = jnp.transpose(w[:, 3 * PAIR : 4 * PAIR].astype(f32))
        gains[0:8, :] = turned[0:8]
        gains[8:16, :] = turned[HEAD_DIM : HEAD_DIM + 8]
    lane = lax.broadcasted_iota(jnp.int32, (ROW_BLOCK, PAIR), 1)
    low_head = lane < HEAD_DIM
    in_first = (lane & (HEAD_DIM - 1)) < HEAD_DIM // 2
    zero = jnp.zeros((ROW_BLOCK, PAIR), bf16)

    @pl.loop(0, length // ROW_BLOCK)
    def _(b):
        rows = pl.ds(pl.multiple_of(b * ROW_BLOCK, ROW_BLOCK), ROW_BLOCK)
        if first:
            normed, _ = norm_stats(src[rows, :].astype(f32))
            a = (normed * gains[0:1, :]).astype(bf16)
            a1[rows, :] = a
        else:
            a = src[rows, :]
        qkv = jnp.dot(a, w[:, at : at + 3 * PAIR], preferred_element_type=f32)
        cos, sin = rotary_block(table, turns, b)
        query_mask, key_mask = mask_features(bounds, b * ROW_BLOCK, ROW_BLOCK)
        query_mask, key_mask = query_mask.astype(bf16), key_mask.astype(bf16)
        u = qkv[:, :PAIR]
        q = (u * cos + half_swap(u, in_first) * sin).astype(bf16)
        u = qkv[:, PAIR : 2 * PAIR]
        k = (u * cos + half_swap(u, in_first) * sin).astype(bf16)
        v = qkv[:, 2 * PAIR :].astype(bf16)
        q_out[rows, :] = q
        k_out[rows, :] = k
        v_out[rows, :] = v
        scaled = q.astype(f32) * LOG2_SCALE
        high = scaled.astype(bf16)
        rest = (scaled - high.astype(f32)).astype(bf16)
        for h in (0, 1):
            mine = low_head if h == 0 else ~low_head
            qx[h, rows, :PAIR] = jnp.where(mine, high, zero)
            qx[h, rows, PAIR:] = jnp.where(mine, rest, query_mask)
            kx[h, rows, :PAIR] = k
            kx[h, rows, PAIR:] = jnp.where(mine, k, key_mask)
        vx[rows, :PAIR] = v
        vx[rows, PAIR:] = jnp.ones((ROW_BLOCK, PAIR), bf16)

    lane_q = lax.broadcasted_iota(jnp.int32, (FWD_BQ, PAIR), 1) < HEAD_DIM

    def work(rows, keys):
        values = vx[keys, :]
        scores = [
            lax.dot_general(qx[h, rows, :], kx[h, keys, :], NT, preferred_element_type=f32) for h in (0, 1)
        ]
        tops, sums = [], []
        for h in (0, 1):
            top = jnp.max(scores[h], axis=1, keepdims=True)
            probs = jnp.exp2(scores[h] - top).astype(bf16)
            tops.append(top)
            sums.append(jnp.dot(probs, values, preferred_element_type=f32))
        total = jnp.where(lane_q, sums[0][:, PAIR:], sums[1][:, PAIR:])
        out = jnp.where(lane_q, sums[0][:, :PAIR], sums[1][:, :PAIR])
        o_out[rows, :] = (out / total).astype(bf16)
        lse_out[rows, :] = jnp.maximum(jnp.where(lane_q, tops[0], tops[1]) + jnp.log2(total), -1e20)

    def empty(rows):
        o_out[rows, :] = jnp.zeros((FWD_BQ, PAIR), bf16)
        lse_out[rows, :] = jnp.zeros((FWD_BQ, PAIR), f32)

    each_query_block(starts, live, length, FWD_BQ, FWD_STEP, work, empty)


def forward_pair(first, scal, seg, src, tables, parts, at, deps=()):
    length, width = src.shape
    shape = jax.ShapeDtypeStruct
    outs = [shape((length, PAIR), bf16)] * 4 + [shape((length, PAIR), f32)]
    pieces = isinstance(parts, list)
    operands = parts if pieces else [parts]
    if pieces:
        outs = [shape((width, parts[0].shape[-1]), bf16)] + outs
    if first:
        outs = [shape((length, width), bf16), shape((16, width), f32)] + outs
    kernel = functools.partial(forward_kernel, first, len(parts) if pieces else 0, at)
    return pl.pallas_call(
        passing(kernel, 5 + len(operands), len(deps)),
        out_shape=tuple(outs),
        in_specs=[smem(), vmem(), vmem(), vmem(), vmem()]
        + [hbm() if pieces else vmem()] * len(operands)
        + [anywhere()] * len(deps),
        out_specs=(vmem(),) * len(outs),
        scratch_shapes=[
            pltpu.VMEM((2, length, 2 * PAIR), bf16),
            pltpu.VMEM((2, length, 2 * PAIR), bf16),
            pltpu.VMEM((length, 2 * PAIR), bf16),
            pltpu.SemaphoreType.DMA((16,)),
        ],
        compiler_params=params(FWD_MIB),
        cost_estimate=lasts(18),
        name="attention_forward_first" if first else "attention_forward",
    )(scal, seg, src, *tables, *operands, *deps)


def backward_kernel(part_count, *refs):
    scal, seg, a1, near, far, w, q_in, k_in, v_in, o_in, lse, table, turns, dqkv = refs[:14]
    parts = refs[14 : 14 + part_count]
    (qx, kx, dx, vx, qm, km, dq, dk, dv, grads, sems) = refs[14 + part_count :]
    length, width = a1.shape
    half = length // 2
    live, me, core = scal[0], scal[1], scal[2]
    starts = document_starts(seg[...], length)
    bounds = lane_bounds(starts, live, length)
    halves = ((near, core), (far, 1 - core))
    lane = lax.broadcasted_iota(jnp.int32, (ROW_BLOCK, PAIR), 1)
    in_head = lane & (HEAD_DIM - 1)
    low_head = lane < HEAD_DIM
    in_first = in_head < HEAD_DIM // 2
    zero = jnp.zeros((ROW_BLOCK, PAIR), bf16)
    minus = jnp.full((ROW_BLOCK, PAIR), -1, bf16)

    def prepare(source, at, b):
        first = pl.multiple_of(at * half + b * ROW_BLOCK, ROW_BLOCK)
        rows = pl.ds(first, ROW_BLOCK)
        grad = jnp.dot(source[pl.ds(pl.multiple_of(b * ROW_BLOCK, ROW_BLOCK), ROW_BLOCK), :], w[...], preferred_element_type=f32).astype(bf16)
        query_mask, key_mask = mask_features(bounds, first, ROW_BLOCK)
        q, k = q_in[rows, :], k_in[rows, :]
        scaled = q.astype(f32) * LOG2_SCALE
        high = scaled.astype(bf16)
        rest = (scaled - high.astype(f32)).astype(bf16)
        la, lb, lc = split3(pltpu.roll(lse[rows, :], HEAD_DIM, 1))
        fq_b = jnp.where(
            in_head == 5, la, jnp.where(in_head == 6, lb, jnp.where(in_head == 7, lc, query_mask.astype(bf16)))
        )
        fk_b = jnp.where((in_head >= 5) & (in_head < 8), minus, key_mask.astype(bf16))
        inner = grad.astype(f32) * o_in[rows, :].astype(f32)
        for h in (0, 1):
            mine = low_head if h == 0 else ~low_head
            qx[h, rows, :PAIR] = jnp.where(mine, high, zero)
            qx[h, rows, PAIR:] = jnp.where(mine, rest, fq_b)
            kx[h, rows, :PAIR] = k
            kx[h, rows, PAIR:] = jnp.where(mine, k, fk_b)
            qm[h, rows, :] = jnp.where(mine, q, zero)
            km[h, rows, :] = jnp.where(mine, k, zero)
            dx[h, rows, :PAIR] = jnp.where(mine, grad, zero)
            delta = jnp.sum(jnp.where(mine, inner, 0.0), axis=1, keepdims=True)
            da, db, dc = split3(jnp.broadcast_to(delta, (ROW_BLOCK, PAIR)))
            dx[h, rows, PAIR:] = jnp.where(
                lane == 0, da, jnp.where(lane == 1, db, jnp.where(lane == 2, dc, zero))
            )
        vx[rows, :PAIR] = v_in[rows, :]
        vx[rows, PAIR:] = jnp.where(lane < 3, minus, zero)
        dk[rows, :] = jnp.zeros((ROW_BLOCK, PAIR), f32)
        dv[rows, :] = jnp.zeros((ROW_BLOCK, PAIR), f32)

    for source, at in halves:

        @pl.loop(0, half // ROW_BLOCK)
        def _(b):
            prepare(source, at, b)

    def work(rows, keys):
        grad_q = grad_k = grad_v = None
        for h in (0, 1):
            scores = lax.dot_general(qx[h, rows, :], kx[h, keys, :], NT, preferred_element_type=f32)
            pulled = lax.dot_general(dx[h, rows, :], vx[keys, :], NT, preferred_element_type=f32)
            probs = jnp.exp2(scores)
            grad_s = (probs * pulled).astype(bf16)
            one_q = jnp.dot(grad_s, km[h, keys, :], preferred_element_type=f32)
            one_v = lax.dot_general(probs.astype(bf16), dx[h, rows, :PAIR], TN, preferred_element_type=f32)
            one_k = lax.dot_general(grad_s, qm[h, rows, :], TN, preferred_element_type=f32)
            grad_q = one_q if h == 0 else grad_q + one_q
            grad_v = one_v if h == 0 else grad_v + one_v
            grad_k = one_k if h == 0 else grad_k + one_k
        dq[rows, :] = grad_q
        dv[keys, :] = dv[keys, :] + grad_v
        dk[keys, :] = dk[keys, :] + grad_k

    def empty(rows):
        dq[rows, :] = jnp.zeros((BWD_BQ, PAIR), f32)

    each_query_block(starts, live, length, BWD_BQ, BWD_STEP, work, empty)

    @pl.loop(0, length // ROW_BLOCK)
    def _(b):
        rows = pl.ds(pl.multiple_of(b * ROW_BLOCK, ROW_BLOCK), ROW_BLOCK)
        cos, sin = rotary_block(table, turns, b)
        u = dq[rows, :] * SCORE_SCALE
        dqkv[rows, :PAIR] = (u * cos - half_swap(u, in_first) * sin).astype(bf16)
        u = dk[rows, :] * SCORE_SCALE
        dqkv[rows, PAIR : 2 * PAIR] = (u * cos - half_swap(u, in_first) * sin).astype(bf16)
        dqkv[rows, 2 * PAIR :] = dv[rows, :].astype(bf16)

    for m in range(width // ROW_BLOCK):
        part = slice(m * ROW_BLOCK, (m + 1) * ROW_BLOCK)
        grads[part, : 3 * PAIR] = lax.dot_general(
            a1[:, part], dqkv[...], TN, preferred_element_type=f32
        ).astype(bf16)
        total = None
        for source, at in halves:
            rows = pl.ds(pl.multiple_of(at * half, half), half)
            term = lax.dot_general(source[:, part], o_in[rows, :], TN, preferred_element_type=f32)
            total = term if total is None else total + term
        grads[part, 3 * PAIR :] = total.astype(bf16)
    if part_count == 1:
        stores = [pltpu.make_async_copy(grads, parts[0], sems.at[0])]
    else:
        rows_each = parts[0].shape[1]
        stores = []
        for h in range(parts[0].shape[0]):
            for j in range(part_count):
                own = jnp.bitwise_xor(me, h * part_count + j)
                stores.append(
                    pltpu.make_async_copy(
                        grads.at[pl.ds(pl.multiple_of(own * rows_each, 16), rows_each)],
                        parts[j].at[h],
                        sems.at[h * part_count + j],
                    )
                )
    for copy in stores:
        copy.start()
    for copy in stores:
        copy.wait()


def backward_pair(scal, seg, a1, near, far, w, saved, tables, part_shapes, deps=()):
    length, width = a1.shape
    shape = jax.ShapeDtypeStruct
    outs = [shape((length, 3 * PAIR), bf16)] + [shape(s, bf16) for s in part_shapes]
    return pl.pallas_call(
        passing(functools.partial(backward_kernel, len(part_shapes)), 13, len(deps)),
        out_shape=tuple(outs),
        in_specs=[smem()] + [vmem()] * 12 + [anywhere()] * len(deps),
        out_specs=(vmem(),) + (anywhere(),) * len(part_shapes),
        scratch_shapes=[
            pltpu.VMEM((2, length, 2 * PAIR), bf16),
            pltpu.VMEM((2, length, 2 * PAIR), bf16),
            pltpu.VMEM((2, length, 2 * PAIR), bf16),
            pltpu.VMEM((length, 2 * PAIR), bf16),
            pltpu.VMEM((2, length, PAIR), bf16),
            pltpu.VMEM((2, length, PAIR), bf16),
            pltpu.VMEM((length, PAIR), f32),
            pltpu.VMEM((length, PAIR), f32),
            pltpu.VMEM((length, PAIR), f32),
            pltpu.VMEM((width, 4 * PAIR), bf16),
            pltpu.SemaphoreType.DMA((16,)),
        ],
        compiler_params=params(BWD_MIB),
        cost_estimate=lasts(30),
        name="attention_backward",
    )(scal, seg, a1, near, far, w, *saved, *tables, *deps)


def project_kernel(count, scal, *refs):
    rows, weights, out = refs[:count], refs[count : 2 * count], refs[2 * count]
    total = None
    for one, w in zip(rows, weights):
        term = lax.dot_general(one[...], w[...], NT, preferred_element_type=f32)
        total = term if total is None else total + term
    out[...] = total.astype(out.dtype)


def columns_of(weight, at, cols):
    return pl.BlockSpec((weight.shape[0], cols), lambda b, s: (0, at // cols))


def project_far_half(scal, rows, weights, deps=()):
    length, cols = rows[0].shape
    width = weights[0][0].shape[0]
    blocks = length // 2 // ROW_BLOCK
    count = len(rows)
    return pl.pallas_call(
        passing(functools.partial(project_kernel, count), 1 + 2 * count, len(deps)),
        out_shape=jax.ShapeDtypeStruct((length // 2, width), bf16),
        grid_spec=pltpu.PrefetchScalarGridSpec(
            num_scalar_prefetch=1,
            grid=(blocks,),
            in_specs=[pl.BlockSpec((ROW_BLOCK, cols), lambda b, s: (b + (1 - s[2]) * blocks, 0))] * count
            + [columns_of(w, at, cols) for w, at in weights]
            + [anywhere()] * len(deps),
            out_specs=pl.BlockSpec((ROW_BLOCK, width), lambda b, s: (b, 0)),
        ),
        compiler_params=params(),
        cost_estimate=lasts(4),
        name="project_far_half",
    )(scal, *rows, *[w for w, _ in weights], *deps)


def final_kernel(count, scal, *refs):
    rows, weights = refs[:count], refs[count : 2 * count]
    tokens, far, grad_hidden, gains, out = refs[2 * count :]
    total = far[...].astype(f32)
    for one, w in zip(rows, weights):
        total = total + lax.dot_general(one[...], w[...], NT, preferred_element_type=f32)
    normed, inv = norm_stats(tokens[...].astype(f32))
    out[...] = grad_hidden[...] + norm_back(total * gains[0:1, :], normed, inv)


def final_rows(scal, rows, weights, tokens, far, grad_hidden, gains):
    length, cols = rows[0].shape
    width = tokens.shape[1]
    blocks = length // 2 // ROW_BLOCK
    whole = lambda a: pl.BlockSpec(a.shape, lambda b, s: (0, 0))
    near = lambda a: pl.BlockSpec((ROW_BLOCK, a.shape[1]), lambda b, s: (b + s[2] * blocks, 0))
    plain = pl.BlockSpec((ROW_BLOCK, width), lambda b, s: (b, 0))
    return pl.pallas_call(
        functools.partial(final_kernel, len(rows)),
        out_shape=jax.ShapeDtypeStruct((length // 2, width), f32),
        grid_spec=pltpu.PrefetchScalarGridSpec(
            num_scalar_prefetch=1,
            grid=(blocks,),
            in_specs=[near(r) for r in rows]
            + [columns_of(w, at, cols) for w, at in weights]
            + [near(tokens), plain, plain, whole(gains)],
            out_specs=plain,
        ),
        compiler_params=params(),
        cost_estimate=lasts(7),
        name="final_rows",
    )(scal, *rows, *[w for w, _ in weights], tokens, far, grad_hidden, gains)


def ffn_kernel(count, split, down_cols, scal, *refs):
    outs_of, weights = refs[:count], refs[count : 2 * count]
    tokens, far, cot, gains, ffn_w = refs[2 * count : 2 * count + 5]
    result, dattn, grad_hidden, keep, send, z_all, pair_all, a2_all, dff_all = refs[2 * count + 5 :]
    width, ff = ffn_w.shape[1:]
    live, me, core = scal[0], scal[1], scal[2]
    step = pl.program_id(0)
    block = result.shape[0]

    here = core * (block * pl.num_programs(0)) + step * block
    position = here + lax.broadcasted_iota(jnp.int32, (block, 1), 0)
    valid = (position < live).astype(f32)
    attn = far[...].astype(f32)
    for one, w in zip(outs_of, weights):
        attn = attn + lax.dot_general(one[...], w[...], NT, preferred_element_type=f32)
    hidden = tokens[...].astype(f32) + valid * attn
    normed, inv = norm_stats(hidden)
    gain = gains[8:9, :]
    a2 = (normed * gain).astype(bf16)
    up = jnp.dot(a2, ffn_w[0], preferred_element_type=f32)
    gate = jnp.dot(a2, ffn_w[1], preferred_element_type=f32)
    below = 0.5 * (1.0 + lax.erf(up * math.sqrt(0.5)))
    act = up * below
    slope = below + up * jnp.exp(up * up * -0.5) * (1.0 / math.sqrt(2.0 * math.pi))
    z = (act * gate).astype(bf16)
    result[...] = (
        hidden + valid * lax.dot_general(z, ffn_w[2], NT, preferred_element_type=f32)
    ).astype(bf16)
    dy = cot[...].astype(f32)
    dff = (valid * dy).astype(bf16)
    dz = jnp.dot(dff, ffn_w[2], preferred_element_type=f32)
    du = (dz * gate * slope).astype(bf16)
    dg = (dz * act).astype(bf16)
    da2 = lax.dot_general(du, ffn_w[0], NT, preferred_element_type=f32) + lax.dot_general(
        dg, ffn_w[1], NT, preferred_element_type=f32
    )
    grad = dy + norm_back(da2 * gain, normed, inv)
    grad_hidden[...] = grad
    dattn[...] = (valid * grad).astype(bf16)
    rows = pl.ds(pl.multiple_of(step * block, block), block)
    z_all[rows, :] = z
    pair_all[0, rows, :] = du
    pair_all[1, rows, :] = dg
    a2_all[rows, :] = a2
    dff_all[rows, :] = dff

    @pl.when(step == pl.num_programs(0) - 1)
    def _():
        for m in range(width // ROW_BLOCK):
            part = slice(m * ROW_BLOCK, (m + 1) * ROW_BLOCK)
            left = a2_all[:, part]
            down = dff_all[:, part]
            if not split:
                for i in (0, 1):
                    keep[i, part, :] = lax.dot_general(
                        left, pair_all[i], TN, preferred_element_type=f32
                    ).astype(bf16)
                send[part, :] = lax.dot_general(down, z_all[...], TN, preferred_element_type=f32).astype(bf16)
            else:
                offset = ff - down_cols
                for out, who in ((send, 1 - core), (keep, core)):
                    out[part, :ff] = lax.dot_general(
                        left, pair_all[who], TN, preferred_element_type=f32
                    ).astype(bf16)
                    out[part, ff:] = lax.dot_general(
                        down,
                        z_all[:, pl.ds(pl.multiple_of(who * offset, PAIR), down_cols)],
                        TN,
                        preferred_element_type=f32,
                    ).astype(bf16)


def feed_forward(scal, outs_of, weights, tokens, far, cot, gains, ffn_w, down_cols, split):
    length = tokens.shape[0]
    half = length // 2
    blocks = half // ROW_BLOCK
    width, ff = ffn_w.shape[1:]
    shape = jax.ShapeDtypeStruct
    whole = lambda a: pl.BlockSpec(a.shape, lambda b, s: (0,) * len(a.shape))
    near = lambda a: pl.BlockSpec((ROW_BLOCK, a.shape[1]), lambda b, s: (b + s[2] * blocks, 0))
    plain = pl.BlockSpec((ROW_BLOCK, width), lambda b, s: (b, 0))
    if not split:
        grads = (shape((2, width, ff), bf16), shape((width, ff), bf16))
    else:
        grads = (shape((width, ff + down_cols), bf16),) * 2
    return pl.pallas_call(
        functools.partial(ffn_kernel, len(outs_of), split, down_cols),
        out_shape=(shape((half, width), bf16), shape((half, width), bf16), shape((half, width), f32)) + grads,
        grid_spec=pltpu.PrefetchScalarGridSpec(
            num_scalar_prefetch=1,
            grid=(blocks,),
            in_specs=[near(o) for o in outs_of]
            + [columns_of(w, at, PAIR) for w, at in weights]
            + [near(tokens), plain, plain, whole(gains)]
            + [vmem()],
            out_specs=(plain, plain, plain) + tuple(whole(g) for g in grads),
            scratch_shapes=[
                pltpu.VMEM((half, ff), bf16),
                pltpu.VMEM((2, half, ff), bf16),
                pltpu.VMEM((half, width), bf16),
                pltpu.VMEM((half, width), bf16),
            ],
        ),
        compiler_params=params(FFN_MIB),
        cost_estimate=lasts(35),
        name="feed_forward",
    )(scal, *outs_of, *[w for w, _ in weights], tokens, far, cot, gains, ffn_w)


def pack_kernel(wide, scal, keep, got, *outs):
    me = scal[1]
    for j in range(wide):
        for h in range(outs[0].shape[0]):
            own = jnp.bitwise_xor(me, h * wide + j)
            outs[j][h] = (keep[own].astype(f32) + got[own].astype(f32)).astype(bf16)


def pack_parts(scal, keep, got, count, deps=()):
    width, cols = keep.shape
    rows = width // count
    wide = 1 << bit_groups(count)[-1][1]
    shape = jax.ShapeDtypeStruct((count // wide, rows, cols), bf16)
    return pl.pallas_call(
        passing(functools.partial(pack_kernel, wide), 3, len(deps)),
        out_shape=(shape,) * wide,
        in_specs=[smem(), vmem(), vmem()] + [anywhere()] * len(deps),
        out_specs=(vmem(),) * wide,
        compiler_params=params(),
        cost_estimate=lasts(4),
        name="pack_parts",
    )(scal, keep.reshape(count, rows, cols), got.reshape(count, rows, cols), *deps)


def rotary_tables(length):
    freqs = ROPE_THETA ** (-np.arange(0, HEAD_DIM, 2) / HEAD_DIM)
    freqs = np.tile(np.float32(freqs).astype(np.float64), 4)
    sign = np.where(np.arange(PAIR) % HEAD_DIM < HEAD_DIM // 2, -1.0, 1.0)

    def both(positions):
        angles = positions[:, None] * freqs[None, :]
        return jnp.asarray(np.stack([np.cos(angles), np.sin(angles) * sign]), f32)

    return both(np.arange(ROW_BLOCK)), both(np.arange(0, length, ROW_BLOCK))


def local(tokens, segment_ids, counts, w_qkv, w_out, w_in, w_down, ln1_gain, ln2_gain, cotangent):
    count = lax.axis_size("dp")
    dp, core = lax.axis_index("dp"), lax.axis_index("head")
    length, width = tokens.shape[1:]
    ff = w_in.shape[2]
    rows_each = width // count
    fast = rows_each % 16 == 0 and count & (count - 1) == 0 and len(bit_groups(count)) == 2
    pairs = w_qkv.shape[2] // PAIR
    first_core = core == 0
    pick = lambda a, b: jnp.where(first_core, a, b)
    join = lambda mine, other: jnp.concatenate([pick(mine, other), pick(other, mine)], axis=0)
    row, cot = tokens[0], cotangent[0]
    seg = segment_ids[0]
    live = counts[0]
    scal = jnp.stack([live, dp, core]).astype(jnp.int32)
    seg_tile = seg.reshape(-1, 128)

    both = jnp.stack([ln1_gain, ln2_gain], axis=1)
    head_load, rest_load = attention_loads(scal, w_qkv, w_out.T, both, core_swap(both))
    down_turned = w_down.T
    down_cols = -(-(ff // 2) // 128) * 128
    offset = ff - down_cols
    tables = rotary_tables(length)
    out_at = 3 * PAIR * (pairs - 1)
    everyone = ("dp", "head")
    ffn_w = lax.all_gather(jnp.concatenate([w_in, down_turned[None]]), everyone, axis=1, tiled=True)

    if fast:
        high_bits, low_bits = bit_groups(count)
        head_high = gather_step(head_load[None], count, high_bits)
        rest_load = stack_parts([rest_load[None]], head_high[1:])
        head_parts = gather_step(stack_parts(head_high), count, low_bits)
        rest_high = gather_step(rest_load, count, high_bits)
        rest_all = stack_parts(rest_high, head_parts[1:])
        a1, gains, *kept = forward_pair(
            True, scal, seg_tile, row, tables, head_parts, 0, [rest_all]
        )
        rest_parts = gather_step(rest_all, count, low_bits)
    else:
        head_parts = [lax.all_gather(head_load, "dp", axis=0, tiled=True)]
        rest_parts = [lax.all_gather(rest_load, "dp", axis=0, tiled=True)]
        a1, gains, *kept = forward_pair(True, scal, seg_tile, row, tables, head_parts, 0)

    head_w, saved = kept[0], [kept[1:]]
    rest_w, *kept = forward_pair(False, scal, seg_tile, a1, tables, rest_parts, 0)
    saved.append(kept)
    for i in range(2, pairs):
        saved.append(forward_pair(False, scal, seg_tile, a1, tables, rest_w, 3 * PAIR * (i - 1)))
    qkv_w = [(head_w, 0)] + [(rest_w, 3 * PAIR * (i - 1)) for i in range(1, pairs)]
    out_w = [(rest_w, out_at + i * PAIR) for i in range(pairs)]
    outs_of = [s[3] for s in saved]

    far = core_swap(project_far_half(scal, outs_of, out_w))
    result, near_grad, grad_hidden, keep, send = feed_forward(
        scal, outs_of, out_w, row, far, cot, gains, ffn_w, down_cols, fast
    )
    far_grad = core_swap(near_grad)

    def backward(i, deps):
        w, at = out_w[i]
        return backward_pair(
            scal, seg_tile, a1, near_grad, far_grad, w[:, at : at + PAIR], saved[i], tables, part_shapes, deps
        )

    if fast:
        wide = 1 << low_bits[1]
        part_shapes = [(count // wide, rows_each, 4 * PAIR)] * wide
        got = core_swap(send)
        dqkv, near_parts, shards = [], [], []
        deps = []
        ffn_pieces = None
        for i in range(pairs):
            one, *parts = backward(i, deps)
            dqkv.append(one)
            near_parts.append(reduce_near(parts, count))
            if i == 0:
                ffn_near = pack_parts(scal, keep, got, count, [one])
                deps = list(ffn_near)
                ffn_near = reduce_near(ffn_near, count)
            elif i < pairs - 1:
                ffn_pieces = sum_parts(ffn_near, [one])
                pieces = sum_parts(near_parts[i - 1], [one])
                deps = list(ffn_pieces) + list(pieces)
                shards.append(reduce_far(pieces, count, wide))
        done = reduce_far(ffn_pieces, count, wide)
        pieces = sum_parts(near_parts[-2], dqkv[-1:])
        shards.append(reduce_far(pieces, count, wide))
        far_da = core_swap(project_far_half(scal, dqkv, qkv_w, pieces))
        pieces = sum_parts(near_parts[-1])
        shards.append(reduce_far(pieces, count, wide))
        rows_here = w_in.shape[1]
        low, high = done[:rows_here], done[rows_here:]
        mine = pick(low, high)
        other = core_swap(pick(high, low))
        grad_w_in = jnp.stack(
            [pick(mine[:, :ff], other[:, :ff]), pick(other[:, :ff], mine[:, :ff])]
        )
        grad_down = jnp.concatenate(
            [pick(mine[:, ff:], other[:, ff:]), pick(other[:, ff:], mine[:, ff:])[:, down_cols - offset :]],
            axis=1,
        ).T
    else:
        part_shapes = [(width, 4 * PAIR)]
        grad_w_in = lax.psum_scatter(keep.astype(f32), everyone, scatter_dimension=1, tiled=True)
        grad_down = lax.psum_scatter(send.astype(f32), everyone, scatter_dimension=0, tiled=True).T
        dqkv, shards = [], []
        for i in range(pairs):
            one, parts = backward(i, ())
            dqkv.append(one)
            shards.append(lax.psum_scatter(parts.astype(f32), "dp", scatter_dimension=0, tiled=True))
        far_da = core_swap(project_far_half(scal, dqkv, qkv_w))

    grad_two = jnp.sum(grad_w_in * w_in.astype(f32), axis=(0, 2)) / ln2_gain.astype(f32)
    grad_tokens = final_rows(scal, dqkv, qkv_w, row, far_da, grad_hidden, gains)

    grad_qkv = jnp.stack(
        [jnp.concatenate([s[:, c * PAIR : (c + 1) * PAIR] for s in shards], axis=1) for c in range(3)]
    )
    grad_out = jnp.concatenate([s[:, 3 * PAIR :] for s in shards], axis=1).T
    partial = jnp.sum(grad_qkv * w_qkv.astype(f32), axis=(0, 2))
    rows_here = ln1_gain.shape[0]
    low, high = partial[:rows_here], partial[rows_here:]
    grad_one = (pick(low, high) + core_swap(pick(high, low))) / ln1_gain.astype(f32)
    return (
        result[None],
        grad_tokens[None],
        grad_qkv,
        grad_out,
        grad_w_in,
        grad_down,
        grad_one,
        grad_two,
    )


def solution(mesh):
    placed = (
        P("dp", None, None),
        P("dp", None),
        P("dp"),
        P(None, "dp", "head"),
        P("head", "dp"),
        P(None, ("dp", "head"), None),
        P(None, ("dp", "head")),
        P(("dp", "head")),
        P(("dp", "head")),
        P("dp", "head", None),
    )
    return jax.shard_map(
        local,
        mesh=mesh,
        in_specs=placed,
        out_specs=(
            P("dp", "head", None),
            P("dp", "head", None),
            P(None, "dp", "head"),
            P("head", "dp"),
            P(None, ("dp", "head"), None),
            P(None, ("dp", "head")),
            P(("dp", "head")),
            P(("dp", "head")),
        ),
        check_vma=False,
    )
```

time: 424 us -> 320 us (0.75); the launches traced: 415 us -> 317 us
  Pallas kernels: 222 us -> 160 us
  waiting for transfers between devices: 96.5 us -> 52.4 us
  between operations: 2.45 us -> 15.9 us
  starting transfers between devices: 67.7 us -> 58.1 us
  local copies, waits for them, and re-layouts: 14.2 us -> 23.5 us
  other arithmetic: 12.6 us -> 7.74 us
    pallas_call x14 -> x18, Pallas kernels: 212 us -> 154 us  [the longest x3 67 us: backward_pair(): pl.pallas_call(passing(functools.partial(backward_kernel, len(part_shapes...]
    ppermute x48 -> x36, waiting for transfers between devices: 89.8 us -> 43.7 us  [xor_permute(): return lax.ppermute(value, 'dp', [(i, i ^ mask) for i in range(count)])]
    unnamed x82 -> x144, local copies, waits for them, and re-layouts: 5.58 us -> 22.6 us
    ppermute x48 -> x36, starting transfers between devices: 66.4 us -> 56.9 us  [xor_permute(): return lax.ppermute(value, 'dp', [(i, i ^ mask) for i in range(count)])]
    ppermute x12 -> x7, waiting for transfers between devices: 6.75 us -> 8.75 us  [core_swap(): return lax.ppermute(value, 'head', [(0, 1), (1, 0)])]
  transfers between devices with their start and end apart: 60 -> 44, of which waited for: 21 -> 17; matrix products, arithmetic and copies ran while one was open for 4% -> 2% of each run, Pallas kernels for 45% -> 38%
where the time goes in v2:
time: 320 us; the launch traced here: 317 us
  Pallas kernels  160 us (50%)
  starting transfers between devices  58.1 us (18%)
  waiting for transfers between devices  52.4 us (16%)
  local copies, waits for them, and re-layouts  23.5 us (7%)
  between operations  15.9 us (5%)
  other arithmetic  7.74 us (2%)
    pallas_call x3, Pallas kernels, backward_pair(): pl.pallas_call(passing(functools.partial(backward_kernel, len(part_shapes...  67 us
    ppermute x36, starting transfers between devices, xor_permute(): return lax.ppermute(value, 'dp', [(i, i ^ mask) for i in range(count)])  56.9 us
    ppermute x36, waiting for transfers between devices, xor_permute(): return lax.ppermute(value, 'dp', [(i, i ^ mask) for i in range(count)])  43.7 us
    pallas_call x3, Pallas kernels, forward_pair(): pl.pallas_call(passing(kernel, 5 + len(operands), len(deps)), out_shape=t...  41.7 us
    pallas_call x1, Pallas kernels, feed_forward(): pl.pallas_call(functools.partial(ffn_kernel, len(outs_of), split, down_co...  32.8 us
    unnamed x144, local copies, waits for them, and re-layouts  22.6 us
    ppermute x7, waiting for transfers between devices, core_swap(): return lax.ppermute(value, 'head', [(0, 1), (1, 0)])  8.75 us
    pallas_call x2, Pallas kernels, project_far_half(): pl.pallas_call(passing(functools.partial(project_kernel, count), 1 + 2 *...  6.56 us
  transfers between devices with their start and end apart: 44, of which 17 were waited for; matrix products, arithmetic and copies ran while one was open for 2% of the time, Pallas kernels for 38%

profile of v2, /device:TPU:0, one launch (start us, length us, event | category | flops | bytes accessed | tf_op | source)
XLA Modules:
  0.0 317.4 jit_solution(12016646087906655046)
XLA Ops:
  13.4 2.9 collective-permute-start.1
  18.9 3.3 %collective-permute-done.2.refs_2_ = bf16[1,48,512]{2,1,0:T(8,128)(2,1)S(1)} collective-permute-done((bf16[1,48,512]{2,1,0:T(8,128)(2,1)S(1)}, bf16[1,48,512]{2,1,0:T(8,128)(2,1)S(1)}, u32[]{:S(2)}, u32[]{:S(2)}) %collective-permute-start.2) | collective-permute-done | bytes 49184 | tf_op jit(solution)/shard_map/ppermute | solution.py:72
  32.8 7.3 %collective-permute-done.8.refs_2_ = bf16[1,48,1152]{2,1,0:T(8,128)(2,1)S(1)} collective-permute-done((bf16[1,48,1152]{2,1,0:T(8,128)(2,1)S(1)}, bf16[1,48,1152]{2,1,0:T(8,128)(2,1)S(1)}, u32[]{:S(2)}, u32[]{:S(2)}) %collective-permute-start.8) | collective-permute-done | bytes 110624 | tf_op jit(solution)/shard_map/ppermute | solution.py:72
  45.4 17.8 %attention_forward_first.1 = (bf16[2048,768]{1,0:T(8,128)(2,1)S(1)}, f32[16,768]{1,0:T(8,128)S(1)}, bf16[768,512]{1,0:T(8,128)(2,1)S(1)}, bf16[2048,128]{1,0:T(8...) custom-call(s32[3]{0:T(128)S(1)} %pad_add_fusion.scal.refs_0_, ...), custom_call_target="tpu_custom_call" | custom-call | flops 1800000000 | tf_op jit(solution)/shard_map/attention_forward_first/pallas_call | solution.py:378
  65.5 13.1 %attention_forward.2 = (bf16[768,1152]{1,0:T(8,128)(2,1)S(1)}, bf16[2048,128]{1,0:T(8,128)(2,1)S(1)}, bf16[2048,128]{1,0:T(8,128)(2,1)S(1)}, bf16[2048,128]{1,0:...) custom-call(s32[3]{0:T(128)S(1)} %pad_add_fusion.scal.refs_0_, s32[16,128]{1,0:T(8,128)S(1)} %bitcast.42, ...), custom_call_target="tpu_custom_call" | custom-call | flops 1800000000 | tf_op jit(solution)/shard_map/attention_forward/pallas_call | solution.py:378
  78.7 10.8 %attention_forward.3 = (bf16[2048,128]{1,0:T(8,128)(2,1)S(1)}, bf16[2048,128]{1,0:T(8,128)(2,1)S(1)}, bf16[2048,128]{1,0:T(8,128)(2,1)S(1)}, bf16[2048,128]{1,0:T(8,128)(2,1)S(1)}, f32[2048,128]{1,0:T(8,128)S(1)}) custom-call(s32[3]{0:T(128)S(1)} %pad_add_fusion.scal.refs_0_, s32[16,128]{1,0:T(8,128)S(1)} %bitcast.43, ...), custom_call_target="tpu_custom_call" | custom-call | flops 1800000000 | tf_op jit(solution)/shard_map/attention_forward/pallas_call | solution.py:378
  89.5 2.6 project_far_half.2
  92.3 3.4 %collective-permute-done.13.refs_7_ = bf16[1024,768]{1,0:T(8,128)(2,1)S(1)} collective-permute-done((bf16[1024,768]{1,0:T(8,128)(2,1)S(1)}, bf16[1024,768]{1,0:T(8,128)(2,1)S(1)}, u32[]{:S(2)}, u32[]{:S(2)}) %collective-permute-start.13) | collective-permute-done | bytes 1572896 | tf_op jit(solution)/shard_map/ppermute | solution.py:76
  100.7 32.8 %feed_forward.1 = (bf16[1024,768]{1,0:T(8,128)(2,1)}, bf16[1024,768]{1,0:T(8,128)(2,1)S(1)}, f32[1024,768]{1,0:T(8,128)}, bf16[768,1792]{1,0:T(8,128)(2,1)}, bf16[768,1792]{1,0:T(8,128)(2,1)}) custom-call(s32[3]{0:T(128)S(1)} %pad_add_fusion.scal.refs_0_, bf16[2048,128]{1,0:T(8,128)(2,1)S(1)} %copy-done.18, ...), custom_call_target="tpu_custom_call" | custom-call | flops 3500000000 | tf_op jit(solution)/shard_map/feed_forward/pallas_call | solution.py:700
  136.0 4.8 %collective-permute-done.14.refs_4_ = bf16[1024,768]{1,0:T(8,128)(2,1)S(1)} collective-permute-done((bf16[1024,768]{1,0:T(8,128)(2,1)S(1)}, bf16[1024,768]{1,0:T(8,128)(2,1)S(1)}, u32[]{:S(2)}, u32[]{:S(2)}) %collective-permute-start.14) | collective-permute-done | bytes 1572896 | tf_op jit(solution)/shard_map/ppermute | solution.py:76
  142.8 22.0 %attention_backward.3 = (bf16[2048,384]{1,0:T(8,128)(2,1)S(1)}, bf16[4,48,512]{2,1,0:T(8,128)(2,1)S(1)}, bf16[4,48,512]{2,1,0:T(8,128)(2,1)S(1)}, bf16[4,48,512]{2,1,0:T(8,128)(2,1)S(1)}, bf16[4,48,512]{2,1,0:T(8,128)(2,1)S(1)}) custom-call(s32[3]{0:T(128)S(1)} %pad_add_fusion.scal.refs_0_, s32[16,128]{1,0:T(8,128)S(1)} %bitcast.44, ...), custom_call_target="tpu_custom_call" | custom-call | flops 3000000000 | tf_op jit(solution)/shard_map/attention_backward/pallas_call | solution.py:522
  169.3 10.7 %collective-permute-start.17 = (bf16[4,48,1792]{2,1,0:T(8,128)(2,1)}, bf16[4,48,1792]{2,1,0:T(8,128)(2,1)}, u32[]{:S(2)}, u32[]{:S(2)}) collective-permute-start(bf16[4,48,1792]{2,1,0:T(8,128)(2,1)} %get-tuple-element.92.refs_15_), channel_id=1, source_target_pairs={{0,4},{2,6},{4,0},{6,2},{8,12},{10,14},{12,8},{14,10},{16,20},{18,... | collective-permute-start | bytes 2064392 | tf_op jit(solution)/shard_map/ppermute | solution.py:72
  183.0 23.3 %attention_backward.4 = (bf16[2048,384]{1,0:T(8,128)(2,1)S(1)}, bf16[4,48,512]{2,1,0:T(8,128)(2,1)S(1)}, bf16[4,48,512]{2,1,0:T(8,128)(2,1)S(1)}, bf16[4,48,512]{2,1,0:T(8,128)(2,1)S(1)}, bf16[4,48,512]{2,1,0:T(8,128)(2,1)S(1)}) custom-call(s32[3]{0:T(128)S(1)} %pad_add_fusion.scal.refs_0_, s32[16,128]{1,0:T(8,128)S(1)} %bitcast.45, ...), custom_call_target="tpu_custom_call" | custom-call | flops 3000000000 | tf_op jit(solution)/shard_map/attention_backward/pallas_call | solution.py:522
  206.9 11.8 %collective-permute-done.20.refs_2_ = bf16[4,48,512]{2,1,0:T(8,128)(2,1)S(1)} collective-permute-done((bf16[4,48,512]{2,1,0:T(8,128)(2,1)S(1)}, bf16[4,48,512]{2,1,0:T(8,128)(2,1)S(1)}, u32[]{:S(2)}, u32[]{:S(2)}) %collective-permute-start.20) | collective-permute-done | bytes 196640 | tf_op jit(solution)/shard_map/ppermute | solution.py:72
  220.1 3.5 %collective-permute-done.26 = bf16[48,512]{1,0:T(8,128)(2,1)} collective-permute-done((bf16[48,512]{1,0:T(8,128)(2,1)S(1)}, bf16[48,512]{1,0:T(8,128)(2,1)}, u32[]{:S(2)}, u32[]{:S(2)}) %collective-permute-start.26) | collective-permute-done | bytes 49184 | tf_op jit(solution)/shard_map/ppermute | solution.py:72
  225.6 4.1 %collective-permute-done.28 = bf16[48,512]{1,0:T(8,128)(2,1)} collective-permute-done((bf16[48,512]{1,0:T(8,128)(2,1)}, bf16[48,512]{1,0:T(8,128)(2,1)}, u32[]{:S(2)}, u32[]{:S(2)}) %collective-permute-start.28) | collective-permute-done | bytes 49184 | tf_op jit(solution)/shard_map/ppermute | solution.py:72
  243.3 21.7 %attention_backward.5 = (bf16[2048,384]{1,0:T(8,128)(2,1)S(1)}, bf16[4,48,512]{2,1,0:T(8,128)(2,1)S(1)}, bf16[4,48,512]{2,1,0:T(8,128)(2,1)S(1)}, bf16[4,48,512]{2,1,0:T(8,128)(2,1)S(1)}, bf16[4,48,512]{2,1,0:T(8,128)(2,1)S(1)}) custom-call(s32[3]{0:T(128)S(1)} %pad_add_fusion.scal.refs_0_, s32[16,128]{1,0:T(8,128)S(1)} %bitcast.46, ...), custom_call_target="tpu_custom_call" | custom-call | flops 3000000000 | tf_op jit(solution)/shard_map/attention_backward/pallas_call | solution.py:522
  265.4 4.3 %collective-permute-start.31 = (bf16[48,512]{1,0:T(8,128)(2,1)S(1)}, bf16[48,512]{1,0:T(8,128)(2,1)S(1)}, u32[]{:S(2)}, u32[]{:S(2)}) collective-permute-start(bf16[48,512]{1,0:T(8,128)(2,1)S(1)} %get-tuple-element.120.refs_10_), channel_id=1, source_target_pairs={{0,24},{2,26},{4,28},{6,30},{8,16},{10,18},{12,20},{14,22},{16,8},... | collective-permute-start | bytes 147464 | tf_op jit(solution)/shard_map/ppermute | solution.py:72
  270.3 3.9 %project_far_half.3 = bf16[1024,768]{1,0:T(8,128)(2,1)S(1)} custom-call(s32[3]{0:T(128)S(1)} %pad_add_fusion.scal.refs_0_, bf16[2048,384]{1,0:T(8,128)(2,1)S(1)} %copy-done.1, bf16[2048,384]{1,0:T(8,128)(2,1)S(1)} %get-tuple-element.94.refs_4_.refs_2_.refs_1_, bf16[2048,384]{1,0:T(8,128)(2,1)S(1)} %get-tuple-element.111.refs_4_.refs_3_.refs_2_, ...), custom_call_target="tpu_custom_call" | custom-call | flops 400000000 | tf_op jit(solution)/shard_map/project_far_half/pallas_call | solution.py:564
  274.3 3.9 %collective-permute-start.40 = (bf16[48,1792]{1,0:T(8,128)(2,1)S(1)}, bf16[48,1792]{1,0:T(8,128)(2,1)S(1)}, u32[]{:S(2)}, u32[]{:S(2)}) collective-permute-start(bf16[48,1792]{1,0:T(8,128)(2,1)S(1)} %get-tuple-element.102.refs_16_), channel_id=1, source_target_pairs={{0,24},{2,26},{4,28},{6,30},{8,16},{10,18},{12,20},{14,22},{16,8},... | collective-permute-start | bytes 516104 | tf_op jit(solution)/shard_map/ppermute | solution.py:72
  280.2 5.0 %collective-permute-start.33 = (bf16[4,48,512]{2,1,0:T(8,128)(2,1)S(1)}, bf16[4,48,512]{2,1,0:T(8,128)(2,1)S(1)}, u32[]{:S(2)}, u32[]{:S(2)}) collective-permute-start(bf16[4,48,512]{2,1,0:T(8,128)(2,1)S(1)} %get-tuple-element.124), channel_id=1, source_target_pairs={{0,4},{2,6},{4,0},{6,2},{8,12},{10,14},{12,8},{14,10},{16,20},{18,... | collective-permute-start | bytes 589832 | tf_op jit(solution)/shard_map/ppermute | solution.py:72
  286.9 3.7 %collective-permute-done.33.refs_2_ = bf16[4,48,512]{2,1,0:T(8,128)(2,1)S(1)} collective-permute-done((bf16[4,48,512]{2,1,0:T(8,128)(2,1)S(1)}, bf16[4,48,512]{2,1,0:T(8,128)(2,1)S(1)}, u32[]{:S(2)}, u32[]{:S(2)}) %collective-permute-start.33) | collective-permute-done | bytes 196640 | tf_op jit(solution)/shard_map/ppermute | solution.py:72
  293.2 3.7 %collective-permute-start.37 = (bf16[48,512]{1,0:T(8,128)(2,1)S(1)}, bf16[48,512]{1,0:T(8,128)(2,1)S(1)}, u32[]{:S(2)}, u32[]{:S(2)}) collective-permute-start(bf16[48,512]{1,0:T(8,128)(2,1)S(1)} %get-tuple-element.129), channel_id=1, source_target_pairs={{0,24},{2,26},{4,28},{6,30},{8,16},{10,18},{12,20},{14,22},{16,8},... | collective-permute-start | bytes 147464 | tf_op jit(solution)/shard_map/ppermute | solution.py:72
  304.3 6.0 %final_rows.1 = f32[1024,768]{1,0:T(8,128)} custom-call(s32[3]{0:T(128)S(1)} %pad_add_fusion.scal.refs_0_, bf16[2048,384]{1,0:T(8,128)(2,1)S(1)} %copy-done.1, bf16[2048,384]{1,0:T(8,128)(2,1)S(1)} %get-tuple-element.94.refs_4_.refs_2_.refs_1_, bf16[2048,384]{1,0:T(8,128)(2,1)S(1)} %get-tuple-element.111.refs_4_.refs_3_.refs_2_, ...), custom_call_target="tpu_custom_call" | custom-call | flops 700000000 | tf_op jit(solution)/shard_map/final_rows/pallas_call | solution.py:598
  (253 shorter events, 75.0 us)
Async XLA Ops:
  7.2 89.7 %all-gather.2.cloned.1.call-start = ((), (), s32[]{:S(2)}) async-start(), calls=%async_computation | async-start | bytes 5474304 | tf_op jit(solution)/shard_map/all_gather | solution.py:785
  24.9 15.2 %collective-permute-start.4 = (bf16[4,48,512]{2,1,0:T(8,128)(2,1)S(1)}, bf16[4,48,512]{2,1,0:T(8,128)(2,1)S(1)}, u32[]{:S(2)}, u32[]{:S(2)}) collective-permute-start(bf16[4,48,512]{2,1,0:T(8,128)(2,1)S(1)} %stack_parts.3.refs_5_), channel_id=1, source_target_pairs={{0,2},{2,0},{4,6},{6,4},{8,10},{10,8},{12,14},{14,12},{16,18},{18,... | collective-permute-start | bytes 589832 | tf_op jit(solution)/shard_map/ppermute | solution.py:72
  26.4 13.7 %collective-permute-start.5 = (bf16[4,48,512]{2,1,0:T(8,128)(2,1)S(1)}, bf16[4,48,512]{2,1,0:T(8,128)(2,1)S(1)}, u32[]{:S(2)}, u32[]{:S(2)}) collective-permute-start(bf16[4,48,512]{2,1,0:T(8,128)(2,1)S(1)} %stack_parts.3.refs_5_), channel_id=1, source_target_pairs={{0,4},{2,6},{4,0},{6,2},{8,12},{10,14},{12,8},{14,10},{16,20},{18,... | collective-permute-start | bytes 589832 | tf_op jit(solution)/shard_map/ppermute | solution.py:72
  28.0 12.2 %collective-permute-start.6 = (bf16[4,48,512]{2,1,0:T(8,128)(2,1)S(1)}, bf16[4,48,512]{2,1,0:T(8,128)(2,1)S(1)}, u32[]{:S(2)}, u32[]{:S(2)}) collective-permute-start(bf16[4,48,512]{2,1,0:T(8,128)(2,1)S(1)} %stack_parts.3.refs_5_), channel_id=1, source_target_pairs={{0,6},{2,4},{4,2},{6,0},{8,14},{10,12},{12,10},{14,8},{16,22},{18,... | collective-permute-start | bytes 589832 | tf_op jit(solution)/shard_map/ppermute | solution.py:72
  28.4 11.7 %collective-permute-start.8 = (bf16[1,48,1152]{2,1,0:T(8,128)(2,1)S(1)}, bf16[1,48,1152]{2,1,0:T(8,128)(2,1)S(1)}, u32[]{:S(2)}, u32[]{:S(2)}) collective-permute-start(bf16[1,48,1152]{2,1,0:T(8,128)(2,1)S(1)} %stack_parts.4.refs_0_), channel_id=1, source_target_pairs={{0,16},{2,18},{4,20},{6,22},{8,24},{10,26},{12,28},{14,30},{16,0},... | collective-permute-start | bytes 331784 | tf_op jit(solution)/shard_map/ppermute | solution.py:72
  40.2 24.9 %collective-permute-start.10 = (bf16[4,48,1152]{2,1,0:T(8,128)(2,1)S(1)}, bf16[4,48,1152]{2,1,0:T(8,128)(2,1)S(1)}, u32[]{:S(2)}, u32[]{:S(2)}) collective-permute-start(bf16[4,48,1152]{2,1,0:T(8,128)(2,1)S(1)} %stack_parts.5.refs_9_.refs_5_), channel_id=1, source_target_pairs={{0,2},{2,0},{4,6},{6,4},{8,10},{10,8},{12,14},{14,12},{16,18},{18,... | collective-permute-start | bytes 1327112 | tf_op jit(solution)/shard_map/ppermute | solution.py:72
  41.7 23.4 %collective-permute-start.11 = (bf16[4,48,1152]{2,1,0:T(8,128)(2,1)S(1)}, bf16[4,48,1152]{2,1,0:T(8,128)(2,1)S(1)}, u32[]{:S(2)}, u32[]{:S(2)}) collective-permute-start(bf16[4,48,1152]{2,1,0:T(8,128)(2,1)S(1)} %stack_parts.5.refs_9_.refs_5_), channel_id=1, source_target_pairs={{0,4},{2,6},{4,0},{6,2},{8,12},{10,14},{12,8},{14,10},{16,20},{18,... | collective-permute-start | bytes 1327112 | tf_op jit(solution)/shard_map/ppermute | solution.py:72
  42.7 22.7 %collective-permute-start.12 = (bf16[4,48,1152]{2,1,0:T(8,128)(2,1)S(1)}, bf16[4,48,1152]{2,1,0:T(8,128)(2,1)S(1)}, u32[]{:S(2)}, u32[]{:S(2)}) collective-permute-start(bf16[4,48,1152]{2,1,0:T(8,128)(2,1)S(1)} %stack_parts.5.refs_9_.refs_5_), channel_id=1, source_target_pairs={{0,6},{2,4},{4,2},{6,0},{8,14},{10,12},{12,10},{14,8},{16,22},{18,... | collective-permute-start | bytes 1327112 | tf_op jit(solution)/shard_map/ppermute | solution.py:72
  133.5 31.4 %collective-permute-start.15 = (bf16[768,1792]{1,0:T(8,128)(2,1)}, bf16[768,1792]{1,0:T(8,128)(2,1)S(1)}, u32[]{:S(2)}, u32[]{:S(2)}) collective-permute-start(bf16[768,1792]{1,0:T(8,128)(2,1)} %get-tuple-element.89), channel_id=1, source_target_pairs={{0,1},{1,0},{2,3},{3,2},{4,5},{5,4},{6,7},{7,6},{8,9},{9,8},{10,11... | collective-permute-start | bytes 8257544 | tf_op jit(solution)/shard_map/ppermute | solution.py:76
  164.9 16.7 %collective-permute-start.19 = (bf16[4,48,512]{2,1,0:T(8,128)(2,1)S(1)}, bf16[4,48,512]{2,1,0:T(8,128)(2,1)S(1)}, u32[]{:S(2)}, u32[]{:S(2)}) collective-permute-start(bf16[4,48,512]{2,1,0:T(8,128)(2,1)S(1)} %get-tuple-element.104), channel_id=1, source_target_pairs={{0,2},{2,0},{4,6},{6,4},{8,10},{10,8},{12,14},{14,12},{16,18},{18,... | collective-permute-start | bytes 589832 | tf_op jit(solution)/shard_map/ppermute | solution.py:72
  167.3 65.1 %collective-permute-start.16 = (bf16[4,48,1792]{2,1,0:T(8,128)(2,1)}, bf16[4,48,1792]{2,1,0:T(8,128)(2,1)}, u32[]{:S(2)}, u32[]{:S(2)}) collective-permute-start(bf16[4,48,1792]{2,1,0:T(8,128)(2,1)} %get-tuple-element.91.refs_14_), channel_id=1, source_target_pairs={{0,2},{2,0},{4,6},{6,4},{8,10},{10,8},{12,14},{14,12},{16,18},{18,... | collective-permute-start | bytes 2064392 | tf_op jit(solution)/shard_map/ppermute | solution.py:72
  169.3 63.5 %collective-permute-start.17 = (bf16[4,48,1792]{2,1,0:T(8,128)(2,1)}, bf16[4,48,1792]{2,1,0:T(8,128)(2,1)}, u32[]{:S(2)}, u32[]{:S(2)}) collective-permute-start(bf16[4,48,1792]{2,1,0:T(8,128)(2,1)} %get-tuple-element.92.refs_15_), channel_id=1, source_target_pairs={{0,4},{2,6},{4,0},{6,2},{8,12},{10,14},{12,8},{14,10},{16,20},{18,... | collective-permute-start | bytes 2064392 | tf_op jit(solution)/shard_map/ppermute | solution.py:72
  180.0 52.8 %collective-permute-start.18 = (bf16[4,48,1792]{2,1,0:T(8,128)(2,1)}, bf16[4,48,1792]{2,1,0:T(8,128)(2,1)}, u32[]{:S(2)}, u32[]{:S(2)}) collective-permute-start(bf16[4,48,1792]{2,1,0:T(8,128)(2,1)} %get-tuple-element.93.refs_16_), channel_id=1, source_target_pairs={{0,6},{2,4},{4,2},{6,0},{8,14},{10,12},{12,10},{14,8},{16,22},{18,... | collective-permute-start | bytes 2064392 | tf_op jit(solution)/shard_map/ppermute | solution.py:72
  180.0 38.7 %collective-permute-start.20 = (bf16[4,48,512]{2,1,0:T(8,128)(2,1)S(1)}, bf16[4,48,512]{2,1,0:T(8,128)(2,1)S(1)}, u32[]{:S(2)}, u32[]{:S(2)}) collective-permute-start(bf16[4,48,512]{2,1,0:T(8,128)(2,1)S(1)} %get-tuple-element.105), channel_id=1, source_target_pairs={{0,4},{2,6},{4,0},{6,2},{8,12},{10,14},{12,8},{14,10},{16,20},{18,... | collective-permute-start | bytes 589832 | tf_op jit(solution)/shard_map/ppermute | solution.py:72
  181.5 37.2 %collective-permute-start.21 = (bf16[4,48,512]{2,1,0:T(8,128)(2,1)S(1)}, bf16[4,48,512]{2,1,0:T(8,128)(2,1)S(1)}, u32[]{:S(2)}, u32[]{:S(2)}) collective-permute-start(bf16[4,48,512]{2,1,0:T(8,128)(2,1)S(1)} %get-tuple-element.106), channel_id=1, source_target_pairs={{0,6},{2,4},{4,2},{6,0},{8,14},{10,12},{12,10},{14,8},{16,22},{18,... | collective-permute-start | bytes 589832 | tf_op jit(solution)/shard_map/ppermute | solution.py:72
  225.3 39.8 %collective-permute-start.22 = (bf16[4,48,512]{2,1,0:T(8,128)(2,1)}, bf16[4,48,512]{2,1,0:T(8,128)(2,1)S(1)}, u32[]{:S(2)}, u32[]{:S(2)}) collective-permute-start(bf16[4,48,512]{2,1,0:T(8,128)(2,1)} %copy-done.51), channel_id=1, source_target_pairs={{0,2},{2,0},{4,6},{6,4},{8,10},{10,8},{12,14},{14,12},{16,18},{18,... | collective-permute-start | bytes 589832 | tf_op jit(solution)/shard_map/ppermute | solution.py:72
  229.8 35.3 %collective-permute-start.23 = (bf16[4,48,512]{2,1,0:T(8,128)(2,1)}, bf16[4,48,512]{2,1,0:T(8,128)(2,1)S(1)}, u32[]{:S(2)}, u32[]{:S(2)}) collective-permute-start(bf16[4,48,512]{2,1,0:T(8,128)(2,1)} %copy-done.50), channel_id=1, source_target_pairs={{0,4},{2,6},{4,0},{6,2},{8,12},{10,14},{12,8},{14,10},{16,20},{18,... | collective-permute-start | bytes 589832 | tf_op jit(solution)/shard_map/ppermute | solution.py:72
  232.4 32.7 %collective-permute-start.24 = (bf16[4,48,512]{2,1,0:T(8,128)(2,1)}, bf16[4,48,512]{2,1,0:T(8,128)(2,1)S(1)}, u32[]{:S(2)}, u32[]{:S(2)}) collective-permute-start(bf16[4,48,512]{2,1,0:T(8,128)(2,1)} %copy-done.49), channel_id=1, source_target_pairs={{0,6},{2,4},{4,2},{6,0},{8,14},{10,12},{12,10},{14,8},{16,22},{18,... | collective-permute-start | bytes 589832 | tf_op jit(solution)/shard_map/ppermute | solution.py:72
  265.3 12.9 %collective-permute-start.30 = (bf16[48,512]{1,0:T(8,128)(2,1)S(1)}, bf16[48,512]{1,0:T(8,128)(2,1)S(1)}, u32[]{:S(2)}, u32[]{:S(2)}) collective-permute-start(bf16[48,512]{1,0:T(8,128)(2,1)S(1)} %get-tuple-element.119.refs_9_), channel_id=1, source_target_pairs={{0,16},{2,18},{4,20},{6,22},{8,24},{10,26},{12,28},{14,30},{16,0},... | collective-permute-start | bytes 147464 | tf_op jit(solution)/shard_map/ppermute | solution.py:72
  265.4 14.8 %collective-permute-start.31 = (bf16[48,512]{1,0:T(8,128)(2,1)S(1)}, bf16[48,512]{1,0:T(8,128)(2,1)S(1)}, u32[]{:S(2)}, u32[]{:S(2)}) collective-permute-start(bf16[48,512]{1,0:T(8,128)(2,1)S(1)} %get-tuple-element.120.refs_10_), channel_id=1, source_target_pairs={{0,24},{2,26},{4,28},{6,30},{8,16},{10,18},{12,20},{14,22},{16,8},... | collective-permute-start | bytes 147464 | tf_op jit(solution)/shard_map/ppermute | solution.py:72
  269.7 15.6 %collective-permute-start.38 = (bf16[48,1792]{1,0:T(8,128)(2,1)S(1)}, bf16[48,1792]{1,0:T(8,128)(2,1)S(1)}, u32[]{:S(2)}, u32[]{:S(2)}) collective-permute-start(bf16[48,1792]{1,0:T(8,128)(2,1)S(1)} %get-tuple-element.100.refs_14_), channel_id=1, source_target_pairs={{0,8},{2,10},{4,12},{6,14},{8,0},{10,2},{12,4},{14,6},{16,24},{18,... | collective-permute-start | bytes 516104 | tf_op jit(solution)/shard_map/ppermute | solution.py:72
  269.8 17.0 %collective-permute-start.39 = (bf16[48,1792]{1,0:T(8,128)(2,1)S(1)}, bf16[48,1792]{1,0:T(8,128)(2,1)S(1)}, u32[]{:S(2)}, u32[]{:S(2)}) collective-permute-start(bf16[48,1792]{1,0:T(8,128)(2,1)S(1)} %get-tuple-element.101.refs_15_), channel_id=1, source_target_pairs={{0,16},{2,18},{4,20},{6,22},{8,24},{10,26},{12,28},{14,30},{16,0},... | collective-permute-start | bytes 516104 | tf_op jit(solution)/shard_map/ppermute | solution.py:72
  274.3 12.5 %collective-permute-start.40 = (bf16[48,1792]{1,0:T(8,128)(2,1)S(1)}, bf16[48,1792]{1,0:T(8,128)(2,1)S(1)}, u32[]{:S(2)}, u32[]{:S(2)}) collective-permute-start(bf16[48,1792]{1,0:T(8,128)(2,1)S(1)} %get-tuple-element.102.refs_16_), channel_id=1, source_target_pairs={{0,24},{2,26},{4,28},{6,30},{8,16},{10,18},{12,20},{14,22},{16,8},... | collective-permute-start | bytes 516104 | tf_op jit(solution)/shard_map/ppermute | solution.py:72
  286.8 17.5 %collective-permute-start.25 = (bf16[1024,768]{1,0:T(8,128)(2,1)S(1)}, bf16[1024,768]{1,0:T(8,128)(2,1)S(1)}, u32[]{:S(2)}, u32[]{:S(2)}) collective-permute-start(bf16[1024,768]{1,0:T(8,128)(2,1)S(1)} %project_far_half.3), channel_id=1, source_target_pairs={{0,1},{1,0},{2,3},{3,2},{4,5},{5,4},{6,7},{7,6},{8,9},{9,8},{10,11... | collective-permute-start | bytes 4718600 | tf_op jit(solution)/shard_map/ppermute | solution.py:76
  (92 other events, 1016.2 us)
Sparse Core Ops, SparseCore 0:
  11.5 74.7 all-gather.1

commit v3 on v2

--- a/solution.py
+++ b/solution.py
@@ -17,9 +17,9 @@
 LOG2_SCALE = math.log2(math.e) / math.sqrt(HEAD_DIM)
 SCORE_SCALE = 1.0 / math.sqrt(HEAD_DIM)
 ROW_BLOCK = 256
-FWD_MIB, BWD_MIB, FFN_MIB = 32, 40, 44
+FWD_MIB, BWD_MIB, FFN_MIB = 20, 23, 18
 FWD_BQ, FWD_STEP = 512, 256
-BWD_BQ, BWD_STEP = 256, 512
+BWD_BQ, BWD_STEP, BWD_CHUNK = 256, 128, 12
 NT = (((1,), (1,)), ((), ()))
 TN = (((0,), (0,)), ((), ()))
 bf16 = jnp.bfloat16
@@ -42,7 +42,7 @@
     return pl.BlockSpec(memory_space=pl.ANY)
 
 
-def params(mib=16):
+def params(mib=10):
     return pltpu.CompilerParams(vmem_limit_bytes=mib << 20)
 
 
@@ -130,11 +130,15 @@
     return [parts[0]] + [xor_permute(parts[j], count, j) for j in range(1, len(parts))]
 
 
+def far_pieces(pieces, count, wide):
+    shift = wide.bit_length() - 1
+    return [pieces[0]] + [xor_permute(pieces[h], count, h << shift) for h in range(1, len(pieces))]
+
+
 def reduce_far(pieces, count, wide):
-    shift = wide.bit_length() - 1
-    total = pieces[0]
-    for h in range(1, len(pieces)):
-        total = total + xor_permute(pieces[h], count, h << shift).astype(f32)
+    total, *others = far_pieces(pieces, count, wide)
+    for one in others:
+        total = total + one.astype(f32)
     return total
 
 
@@ -146,7 +150,7 @@
             rest[:, at : at + PAIR] = w_qkv[c, :, i * PAIR : (i + 1) * PAIR]
     rest[:, 3 * PAIR * (pairs - 1) :] = out_turned[...]
     mine, other = mine[...].astype(f32), other[...].astype(f32)
-    first = scal[2] == 0
+    first = scal[0] == 0
     gains = jnp.concatenate([jnp.where(first, mine, other), jnp.where(first, other, mine)], axis=0)
     low = lax.broadcasted_iota(jnp.int32, (gains.shape[0], PAIR), 1) < HEAD_DIM
     head[:, 3 * PAIR :] = jnp.where(low, gains[:, 0:1], gains[:, 1:2]).astype(bf16)
@@ -167,9 +171,9 @@
     )(scal, w_qkv, out_turned, mine, other)
 
 
-def placed_copies(parts, target, sems, me, rows):
+def placed_copies(parts, target, sems, me, rows, cols):
     if len(parts) == 1:
-        return [pltpu.make_async_copy(parts[0], target, sems.at[0])]
+        return [pltpu.make_async_copy(parts[0].at[:, cols], target.at[:, cols], sems.at[0])]
     copies = []
     wide = len(parts)
     for h in range(parts[0].shape[0]):
@@ -177,19 +181,16 @@
             own = jnp.bitwise_xor(me, h * wide + j)
             copies.append(
                 pltpu.make_async_copy(
-                    parts[j].at[h],
-                    target.at[pl.ds(pl.multiple_of(own * rows, 16), rows)],
+                    parts[j].at[h, :, cols],
+                    target.at[pl.ds(pl.multiple_of(own * rows, 16), rows), cols],
                     sems.at[h * wide + j],
                 )
             )
     return copies
 
 
-def document_starts(seg, length):
-    starts = [jnp.int32(0)]
-    for d in (1, 2, 3):
-        starts.append(jnp.sum((seg < d).astype(jnp.int32)))
-    return starts + [jnp.int32(length)]
+def document_starts(scal, length):
+    return [jnp.int32(0), scal[3], scal[4], scal[5], jnp.int32(length)]
 
 
 def key_range(starts, live, first, size, length):
@@ -201,7 +202,8 @@
     for d in (3, 2, 1):
         high = jnp.where(starts[d] > last, starts[d], high)
     high = jnp.minimum(high, live)
-    return low, jnp.where(first < live, high, low)
+    seen = first < live
+    return jnp.where(seen, low, 0), jnp.where(seen, high, 0)
 
 
 def each_query_block(starts, live, length, size, step, work, empty):
@@ -224,6 +226,27 @@
             empty(rows)
 
 
+def each_key_chunk(starts, live, length, size, step, most, work):
+    @pl.loop(0, length // size)
+    def _(i):
+        first = pl.multiple_of(i * size, size)
+        low, high = key_range(starts, live, first, size, length)
+        base = low // 16 * 16
+        steps = (high - base + step - 1) // step
+        base = jnp.maximum(jnp.minimum(base, length - steps * step), 0)
+        rows = pl.ds(first, size)
+
+        @pl.loop(0, (steps + most - 1) // most)
+        def _(c):
+            at = pl.multiple_of(base + c * (most * step), 16)
+            left = jnp.minimum(steps - c * most, most)
+            for w in range(1, most + 1):
+
+                @pl.when(left == w)
+                def _():
+                    work(rows, pl.ds(at, w * step))
+
+
 def lane_bounds(starts, live, length):
     column = lax.broadcasted_iota(jnp.int32, (1, PAIR), 1) & (HEAD_DIM - 1)
     low = jnp.zeros((1, PAIR), jnp.int32)
@@ -276,9 +299,9 @@
 
 
 def forward_kernel(first, part_count, at, *refs):
-    scal, seg, src, table, turns = refs[:5]
-    parts = refs[5 : 5 + max(part_count, 1)]
-    outs = refs[5 + max(part_count, 1) :]
+    scal, src, table, turns = refs[:4]
+    parts = refs[4 : 4 + max(part_count, 1)]
+    outs = refs[4 + max(part_count, 1) :]
     if first:
         a1, gains = outs[:2]
         outs = outs[2:]
@@ -290,10 +313,15 @@
     length, width = src.shape
     live, me = scal[0], scal[1]
 
-    copies = placed_copies(parts, w, sems, me, parts[0].shape[-2]) if part_count else []
-    for copy in copies:
+    copies, later = [], []
+    if part_count:
+        soon = 4 * PAIR if first else 3 * PAIR
+        copies = placed_copies(parts, w, sems.at[0], me, parts[0].shape[-2], slice(0, soon))
+        if w.shape[1] > soon:
+            later = placed_copies(parts, w, sems.at[1], me, parts[0].shape[-2], slice(soon, w.shape[1]))
+    for copy in copies + later:
         copy.start()
-    starts = document_starts(seg[...], length)
+    starts = document_starts(scal, length)
     bounds = lane_bounds(starts, live, length)
     for copy in copies:
         copy.wait()
@@ -362,9 +390,11 @@
         lse_out[rows, :] = jnp.zeros((FWD_BQ, PAIR), f32)
 
     each_query_block(starts, live, length, FWD_BQ, FWD_STEP, work, empty)
-
-
-def forward_pair(first, scal, seg, src, tables, parts, at, deps=()):
+    for copy in later:
+        copy.wait()
+
+
+def forward_pair(first, scal, src, tables, parts, at, deps=()):
     length, width = src.shape
     shape = jax.ShapeDtypeStruct
     outs = [shape((length, PAIR), bf16)] * 4 + [shape((length, PAIR), f32)]
@@ -376,9 +406,9 @@
         outs = [shape((length, width), bf16), shape((16, width), f32)] + outs
     kernel = functools.partial(forward_kernel, first, len(parts) if pieces else 0, at)
     return pl.pallas_call(
-        passing(kernel, 5 + len(operands), len(deps)),
+        passing(kernel, 4 + len(operands), len(deps)),
         out_shape=tuple(outs),
-        in_specs=[smem(), vmem(), vmem(), vmem(), vmem()]
+        in_specs=[smem(), vmem(), vmem(), vmem()]
         + [hbm() if pieces else vmem()] * len(operands)
         + [anywhere()] * len(deps),
         out_specs=(vmem(),) * len(outs),
@@ -386,22 +416,24 @@
             pltpu.VMEM((2, length, 2 * PAIR), bf16),
             pltpu.VMEM((2, length, 2 * PAIR), bf16),
             pltpu.VMEM((length, 2 * PAIR), bf16),
-            pltpu.SemaphoreType.DMA((16,)),
+            pltpu.SemaphoreType.DMA((2, 16)),
         ],
         compiler_params=params(FWD_MIB),
         cost_estimate=lasts(18),
         name="attention_forward_first" if first else "attention_forward",
-    )(scal, seg, src, *tables, *operands, *deps)
-
-
-def backward_kernel(part_count, *refs):
-    scal, seg, a1, near, far, w, q_in, k_in, v_in, o_in, lse, table, turns, dqkv = refs[:14]
-    parts = refs[14 : 14 + part_count]
-    (qx, kx, dx, vx, qm, km, dq, dk, dv, grads, sems) = refs[14 + part_count :]
+    )(scal, src, *tables, *operands, *deps)
+
+
+def backward_kernel(part_count, carried, *refs):
+    scal, a1, near, far, w, q_in, k_in, v_in, o_in, lse, table, turns = refs[:12]
+    before = refs[12 : 12 + carried]
+    refs = refs[12 + carried :]
+    dqkv, parts = refs[0], refs[1 : 1 + part_count]
+    (qx, kx, dx, vx, qm, km, dq, dk, dv, grads, sems) = refs[1 + part_count :]
     length, width = a1.shape
     half = length // 2
     live, me, core = scal[0], scal[1], scal[2]
-    starts = document_starts(seg[...], length)
+    starts = document_starts(scal, length)
     bounds = lane_bounds(starts, live, length)
     halves = ((near, core), (far, 1 - core))
     lane = lax.broadcasted_iota(jnp.int32, (ROW_BLOCK, PAIR), 1)
@@ -442,6 +474,7 @@
             )
         vx[rows, :PAIR] = v_in[rows, :]
         vx[rows, PAIR:] = jnp.where(lane < 3, minus, zero)
+        dq[rows, :] = jnp.zeros((ROW_BLOCK, PAIR), f32)
         dk[rows, :] = jnp.zeros((ROW_BLOCK, PAIR), f32)
         dv[rows, :] = jnp.zeros((ROW_BLOCK, PAIR), f32)
 
@@ -452,7 +485,8 @@
             prepare(source, at, b)
 
     def work(rows, keys):
-        grad_q = grad_k = grad_v = None
+        grad_q = dq[rows, :]
+        grad_k = grad_v = None
         for h in (0, 1):
             scores = lax.dot_general(qx[h, rows, :], kx[h, keys, :], NT, preferred_element_type=f32)
             pulled = lax.dot_general(dx[h, rows, :], vx[keys, :], NT, preferred_element_type=f32)
@@ -461,17 +495,14 @@
             one_q = jnp.dot(grad_s, km[h, keys, :], preferred_element_type=f32)
             one_v = lax.dot_general(probs.astype(bf16), dx[h, rows, :PAIR], TN, preferred_element_type=f32)
             one_k = lax.dot_general(grad_s, qm[h, rows, :], TN, preferred_element_type=f32)
-            grad_q = one_q if h == 0 else grad_q + one_q
+            grad_q = grad_q + one_q
             grad_v = one_v if h == 0 else grad_v + one_v
             grad_k = one_k if h == 0 else grad_k + one_k
         dq[rows, :] = grad_q
         dv[keys, :] = dv[keys, :] + grad_v
         dk[keys, :] = dk[keys, :] + grad_k
 
-    def empty(rows):
-        dq[rows, :] = jnp.zeros((BWD_BQ, PAIR), f32)
-
-    each_query_block(starts, live, length, BWD_BQ, BWD_STEP, work, empty)
+    each_key_chunk(starts, live, length, BWD_BQ, BWD_STEP, BWD_CHUNK, work)
 
     @pl.loop(0, length // ROW_BLOCK)
     def _(b):
@@ -494,19 +525,23 @@
             term = lax.dot_general(source[:, part], o_in[rows, :], TN, preferred_element_type=f32)
             total = term if total is None else total + term
         grads[part, 3 * PAIR :] = total.astype(bf16)
-    if part_count == 1:
-        stores = [pltpu.make_async_copy(grads, parts[0], sems.at[0])]
-    else:
+    made = [*before, grads]
+    cols = grads.shape[1]
+    stores = []
+    for n, one in enumerate(made):
+        at = slice(n * cols, (n + 1) * cols)
+        if part_count == 1:
+            stores.append(pltpu.make_async_copy(one, parts[0].at[:, at], sems.at[n, 0]))
+            continue
         rows_each = parts[0].shape[1]
-        stores = []
         for h in range(parts[0].shape[0]):
             for j in range(part_count):
                 own = jnp.bitwise_xor(me, h * part_count + j)
                 stores.append(
                     pltpu.make_async_copy(
-                        grads.at[pl.ds(pl.multiple_of(own * rows_each, 16), rows_each)],
-                        parts[j].at[h],
-                        sems.at[h * part_count + j],
+                        one.at[pl.ds(pl.multiple_of(own * rows_each, 16), rows_each)],
+                        parts[j].at[h, :, at],
+                        sems.at[n, h * part_count + j],
                     )
                 )
     for copy in stores:
@@ -515,14 +550,14 @@
         copy.wait()
 
 
-def backward_pair(scal, seg, a1, near, far, w, saved, tables, part_shapes, deps=()):
+def backward_pair(scal, a1, near, far, w, saved, tables, part_shapes, before=(), deps=()):
     length, width = a1.shape
     shape = jax.ShapeDtypeStruct
     outs = [shape((length, 3 * PAIR), bf16)] + [shape(s, bf16) for s in part_shapes]
     return pl.pallas_call(
-        passing(functools.partial(backward_kernel, len(part_shapes)), 13, len(deps)),
+        passing(functools.partial(backward_kernel, len(part_shapes), len(before)), 12 + len(before), len(deps)),
         out_shape=tuple(outs),
-        in_specs=[smem()] + [vmem()] * 12 + [anywhere()] * len(deps),
+        in_specs=[smem()] + [vmem()] * 11 + [anywhere()] * (len(before) + len(deps)),
         out_specs=(vmem(),) + (anywhere(),) * len(part_shapes),
         scratch_shapes=[
             pltpu.VMEM((2, length, 2 * PAIR), bf16),
@@ -535,12 +570,12 @@
             pltpu.VMEM((length, PAIR), f32),
             pltpu.VMEM((length, PAIR), f32),
             pltpu.VMEM((width, 4 * PAIR), bf16),
-            pltpu.SemaphoreType.DMA((16,)),
+            pltpu.SemaphoreType.DMA((len(before) + 1, 16)),
         ],
         compiler_params=params(BWD_MIB),
         cost_estimate=lasts(30),
         name="attention_backward",
-    )(scal, seg, a1, near, far, w, *saved, *tables, *deps)
+    )(scal, a1, near, far, w, *saved, *tables, *before, *deps)
 
 
 def project_kernel(count, scal, *refs):
@@ -588,7 +623,7 @@
     out[...] = grad_hidden[...] + norm_back(total * gains[0:1, :], normed, inv)
 
 
-def final_rows(scal, rows, weights, tokens, far, grad_hidden, gains):
+def final_rows(scal, rows, weights, tokens, far, grad_hidden, gains, deps=()):
     length, cols = rows[0].shape
     width = tokens.shape[1]
     blocks = length // 2 // ROW_BLOCK
@@ -596,26 +631,67 @@
     near = lambda a: pl.BlockSpec((ROW_BLOCK, a.shape[1]), lambda b, s: (b + s[2] * blocks, 0))
     plain = pl.BlockSpec((ROW_BLOCK, width), lambda b, s: (b, 0))
     return pl.pallas_call(
-        functools.partial(final_kernel, len(rows)),
+        passing(functools.partial(final_kernel, len(rows)), 5 + 2 * len(rows), len(deps)),
         out_shape=jax.ShapeDtypeStruct((length // 2, width), f32),
         grid_spec=pltpu.PrefetchScalarGridSpec(
             num_scalar_prefetch=1,
             grid=(blocks,),
             in_specs=[near(r) for r in rows]
             + [columns_of(w, at, cols) for w, at in weights]
-            + [near(tokens), plain, plain, whole(gains)],
+            + [near(tokens), plain, plain, whole(gains)]
+            + [anywhere()] * len(deps),
             out_specs=plain,
         ),
         compiler_params=params(),
         cost_estimate=lasts(7),
         name="final_rows",
-    )(scal, *rows, *[w for w, _ in weights], tokens, far, grad_hidden, gains)
-
-
-def ffn_kernel(count, split, down_cols, scal, *refs):
+    )(scal, *rows, *[w for w, _ in weights], tokens, far, grad_hidden, gains, *deps)
+
+
+def finish_kernel(sizes, *refs):
+    groups, at = [], 0
+    for size in sizes:
+        groups.append(refs[at : at + size])
+        at += size
+    w_qkv, grad_qkv, grad_out, partial = refs[at:]
+    pair = 0
+    inner = None
+    for group in groups:
+        total = group[0][...]
+        for one in group[1:]:
+            total = total + one[...].astype(f32)
+        for i in range(total.shape[1] // (4 * PAIR)):
+            cols = slice(pair * PAIR, (pair + 1) * PAIR)
+            for c in range(3):
+                grad = total[:, (4 * i + c) * PAIR : (4 * i + c + 1) * PAIR]
+                grad_qkv[c, :, cols] = grad
+                term = grad * w_qkv[c, :, cols].astype(f32)
+                inner = term if inner is None else inner + term
+            grad_out[:, cols] = total[:, (4 * i + 3) * PAIR : (4 * i + 4) * PAIR]
+            pair += 1
+    partial[...] = jnp.broadcast_to(jnp.sum(inner, axis=1, keepdims=True), partial.shape)
+
+
+def finish(groups, w_qkv, deps):
+    rows, cols = w_qkv.shape[1:]
+    shape = jax.ShapeDtypeStruct
+    sizes = [len(g) for g in groups]
+    flat = [x for g in groups for x in g]
+    return pl.pallas_call(
+        passing(functools.partial(finish_kernel, sizes), len(flat) + 1, len(deps)),
+        out_shape=(shape((3, rows, cols), f32), shape((rows, cols), f32), shape((rows, PAIR), f32)),
+        in_specs=[vmem()] * (len(flat) + 1) + [anywhere()] * len(deps),
+        out_specs=(vmem(),) * 3,
+        compiler_params=params(),
+        cost_estimate=lasts(2),
+        name="finish",
+    )(*flat, w_qkv, *deps)
+
+
+def ffn_kernel(count, scal, *refs):
     outs_of, weights = refs[:count], refs[count : 2 * count]
     tokens, far, cot, gains, ffn_w = refs[2 * count : 2 * count + 5]
-    result, dattn, grad_hidden, keep, send, z_all, pair_all, a2_all, dff_all = refs[2 * count + 5 :]
+    result, dattn, grad_hidden, z_all, pair_all, a2_all, dff_all = refs[2 * count + 5 :]
     width, ff = ffn_w.shape[1:]
     live, me, core = scal[0], scal[1], scal[2]
     step = pl.program_id(0)
@@ -651,72 +727,91 @@
     grad = dy + norm_back(da2 * gain, normed, inv)
     grad_hidden[...] = grad
     dattn[...] = (valid * grad).astype(bf16)
-    rows = pl.ds(pl.multiple_of(step * block, block), block)
-    z_all[rows, :] = z
-    pair_all[0, rows, :] = du
-    pair_all[1, rows, :] = dg
-    a2_all[rows, :] = a2
-    dff_all[rows, :] = dff
-
-    @pl.when(step == pl.num_programs(0) - 1)
-    def _():
-        for m in range(width // ROW_BLOCK):
-            part = slice(m * ROW_BLOCK, (m + 1) * ROW_BLOCK)
-            left = a2_all[:, part]
-            down = dff_all[:, part]
-            if not split:
-                for i in (0, 1):
-                    keep[i, part, :] = lax.dot_general(
-                        left, pair_all[i], TN, preferred_element_type=f32
-                    ).astype(bf16)
-                send[part, :] = lax.dot_general(down, z_all[...], TN, preferred_element_type=f32).astype(bf16)
-            else:
-                offset = ff - down_cols
-                for out, who in ((send, 1 - core), (keep, core)):
-                    out[part, :ff] = lax.dot_general(
-                        left, pair_all[who], TN, preferred_element_type=f32
-                    ).astype(bf16)
-                    out[part, ff:] = lax.dot_general(
-                        down,
-                        z_all[:, pl.ds(pl.multiple_of(who * offset, PAIR), down_cols)],
-                        TN,
-                        preferred_element_type=f32,
-                    ).astype(bf16)
-
-
-def feed_forward(scal, outs_of, weights, tokens, far, cot, gains, ffn_w, down_cols, split):
+    z_all[...] = z
+    pair_all[0] = du
+    pair_all[1] = dg
+    a2_all[...] = a2
+    dff_all[...] = dff
+
+
+def weight_grad_kernel(split, own, down_cols, scal, z, pair, a2, dff, *outs):
+    width, ff = a2.shape[1], z.shape[1]
+    core = scal[2]
+    for m in range(width // ROW_BLOCK):
+        part = slice(m * ROW_BLOCK, (m + 1) * ROW_BLOCK)
+        left, down = a2[:, part], dff[:, part]
+        if split:
+            who = core if own else 1 - core
+            at = pl.multiple_of(who * (ff - down_cols), PAIR)
+            outs[0][part, :ff] = lax.dot_general(left, pair[who], TN, preferred_element_type=f32).astype(bf16)
+            outs[0][part, ff:] = lax.dot_general(
+                down, z[:, pl.ds(at, down_cols)], TN, preferred_element_type=f32
+            ).astype(bf16)
+        else:
+            for i in (0, 1):
+                outs[0][i, part, :] = lax.dot_general(
+                    left, pair[i], TN, preferred_element_type=f32
+                ).astype(bf16)
+            outs[1][part, :] = lax.dot_general(down, z[...], TN, preferred_element_type=f32).astype(bf16)
+
+
+def weight_grads(split, own, down_cols, scal, z, pair, a2, dff, deps=()):
+    width, ff = a2.shape[1], z.shape[1]
+    shape = jax.ShapeDtypeStruct
+    if split:
+        outs = (shape((width, ff + down_cols), bf16),)
+    else:
+        outs = (shape((2, width, ff), bf16), shape((width, ff), bf16))
+    return pl.pallas_call(
+        passing(functools.partial(weight_grad_kernel, split, own, down_cols), 5, len(deps)),
+        out_shape=outs,
+        in_specs=[smem()] + [vmem()] * 4 + [anywhere()] * len(deps),
+        out_specs=(vmem(),) * len(outs),
+        compiler_params=params(10 if split else 32),
+        cost_estimate=lasts(5),
+        name="weight_grads",
+    )(scal, z, pair, a2, dff, *deps)
+
+
+def feed_forward(scal, outs_of, weights, tokens, far, cot, gains, ffn_w):
     length = tokens.shape[0]
+    width, ff = ffn_w.shape[1:]
     half = length // 2
     blocks = half // ROW_BLOCK
-    width, ff = ffn_w.shape[1:]
     shape = jax.ShapeDtypeStruct
     whole = lambda a: pl.BlockSpec(a.shape, lambda b, s: (0,) * len(a.shape))
     near = lambda a: pl.BlockSpec((ROW_BLOCK, a.shape[1]), lambda b, s: (b + s[2] * blocks, 0))
-    plain = pl.BlockSpec((ROW_BLOCK, width), lambda b, s: (b, 0))
-    if not split:
-        grads = (shape((2, width, ff), bf16), shape((width, ff), bf16))
-    else:
-        grads = (shape((width, ff + down_cols), bf16),) * 2
+    plain = lambda cols: pl.BlockSpec((ROW_BLOCK, cols), lambda b, s: (b, 0))
     return pl.pallas_call(
-        functools.partial(ffn_kernel, len(outs_of), split, down_cols),
-        out_shape=(shape((half, width), bf16), shape((half, width), bf16), shape((half, width), f32)) + grads,
+        functools.partial(ffn_kernel, len(outs_of)),
+        out_shape=(
+            shape((half, width), bf16),
+            shape((half, width), bf16),
+            shape((half, width), f32),
+            shape((half, ff), bf16),
+            shape((2, half, ff), bf16),
+            shape((half, width), bf16),
+            shape((half, width), bf16),
+        ),
         grid_spec=pltpu.PrefetchScalarGridSpec(
             num_scalar_prefetch=1,
             grid=(blocks,),
             in_specs=[near(o) for o in outs_of]
             + [columns_of(w, at, PAIR) for w, at in weights]
-            + [near(tokens), plain, plain, whole(gains)]
+            + [near(tokens), plain(width), plain(width), whole(gains)]
             + [vmem()],
-            out_specs=(plain, plain, plain) + tuple(whole(g) for g in grads),
-            scratch_shapes=[
-                pltpu.VMEM((half, ff), bf16),
-                pltpu.VMEM((2, half, ff), bf16),
-                pltpu.VMEM((half, width), bf16),
-                pltpu.VMEM((half, width), bf16),
-            ],
+            out_specs=(
+                plain(width),
+                plain(width),
+                plain(width),
+                plain(ff),
+                pl.BlockSpec((2, ROW_BLOCK, ff), lambda b, s: (0, b, 0)),
+                plain(width),
+                plain(width),
+            ),
         ),
         compiler_params=params(FFN_MIB),
-        cost_estimate=lasts(35),
+        cost_estimate=lasts(25),
         name="feed_forward",
     )(scal, *outs_of, *[w for w, _ in weights], tokens, far, cot, gains, ffn_w)
 
@@ -771,11 +866,11 @@
     row, cot = tokens[0], cotangent[0]
     seg = segment_ids[0]
     live = counts[0]
-    scal = jnp.stack([live, dp, core]).astype(jnp.int32)
-    seg_tile = seg.reshape(-1, 128)
+    begins = jnp.sum(seg[None, :] < jnp.arange(1, 4)[:, None], axis=1)
+    scal = jnp.concatenate([jnp.stack([live, dp, core]), begins]).astype(jnp.int32)
 
     both = jnp.stack([ln1_gain, ln2_gain], axis=1)
-    head_load, rest_load = attention_loads(scal, w_qkv, w_out.T, both, core_swap(both))
+    head_load, rest_load = attention_loads(core.astype(jnp.int32)[None], w_qkv, w_out.T, both, core_swap(both))
     down_turned = w_down.T
     down_cols = -(-(ff // 2) // 128) * 128
     offset = ff - down_cols
@@ -792,61 +887,66 @@
         rest_high = gather_step(rest_load, count, high_bits)
         rest_all = stack_parts(rest_high, head_parts[1:])
         a1, gains, *kept = forward_pair(
-            True, scal, seg_tile, row, tables, head_parts, 0, [rest_all]
+            True, scal, row, tables, head_parts, 0, [rest_all]
         )
         rest_parts = gather_step(rest_all, count, low_bits)
     else:
         head_parts = [lax.all_gather(head_load, "dp", axis=0, tiled=True)]
         rest_parts = [lax.all_gather(rest_load, "dp", axis=0, tiled=True)]
-        a1, gains, *kept = forward_pair(True, scal, seg_tile, row, tables, head_parts, 0)
+        a1, gains, *kept = forward_pair(True, scal, row, tables, head_parts, 0)
 
     head_w, saved = kept[0], [kept[1:]]
-    rest_w, *kept = forward_pair(False, scal, seg_tile, a1, tables, rest_parts, 0)
+    rest_w, *kept = forward_pair(False, scal, a1, tables, rest_parts, 0)
     saved.append(kept)
     for i in range(2, pairs):
-        saved.append(forward_pair(False, scal, seg_tile, a1, tables, rest_w, 3 * PAIR * (i - 1)))
+        saved.append(forward_pair(False, scal, a1, tables, rest_w, 3 * PAIR * (i - 1)))
     qkv_w = [(head_w, 0)] + [(rest_w, 3 * PAIR * (i - 1)) for i in range(1, pairs)]
     out_w = [(rest_w, out_at + i * PAIR) for i in range(pairs)]
     outs_of = [s[3] for s in saved]
 
     far = core_swap(project_far_half(scal, outs_of, out_w))
-    result, near_grad, grad_hidden, keep, send = feed_forward(
-        scal, outs_of, out_w, row, far, cot, gains, ffn_w, down_cols, fast
-    )
+    result, near_grad, grad_hidden, *kept = feed_forward(scal, outs_of, out_w, row, far, cot, gains, ffn_w)
     far_grad = core_swap(near_grad)
 
-    def backward(i, deps):
+    def backward(i, part_shapes, before=(), deps=()):
+        q, k, v, o, lse = saved[i]
         w, at = out_w[i]
+        w = w[:, at : at + PAIR]
         return backward_pair(
-            scal, seg_tile, a1, near_grad, far_grad, w[:, at : at + PAIR], saved[i], tables, part_shapes, deps
+            scal, a1, near_grad, far_grad, w, (q, k, v, o, lse), tables, part_shapes, before, deps
         )
 
     if fast:
         wide = 1 << low_bits[1]
-        part_shapes = [(count // wide, rows_each, 4 * PAIR)] * wide
-        got = core_swap(send)
-        dqkv, near_parts, shards = [], [], []
-        deps = []
-        ffn_pieces = None
-        for i in range(pairs):
-            one, *parts = backward(i, deps)
+        parts_of = lambda n: [(count // wide, rows_each, n * 4 * PAIR)] * wide
+        got = core_swap(weight_grads(True, False, down_cols, scal, *kept)[0])
+        keep = weight_grads(True, True, down_cols, scal, *kept)[0]
+        deps = pack_parts(scal, keep, got, count)
+        ffn_near = reduce_near(deps, count)
+        dqkv, before = [], []
+        pieces = None
+        for i in range(pairs - 1):
+            last = i == pairs - 2
+            one, *parts = backward(
+                i, parts_of(pairs - 1) if last else [(width, 4 * PAIR)], before if last else [], deps
+            )
             dqkv.append(one)
-            near_parts.append(reduce_near(parts, count))
+            before += parts
             if i == 0:
-                ffn_near = pack_parts(scal, keep, got, count, [one])
-                deps = list(ffn_near)
-                ffn_near = reduce_near(ffn_near, count)
-            elif i < pairs - 1:
-                ffn_pieces = sum_parts(ffn_near, [one])
-                pieces = sum_parts(near_parts[i - 1], [one])
-                deps = list(ffn_pieces) + list(pieces)
-                shards.append(reduce_far(pieces, count, wide))
-        done = reduce_far(ffn_pieces, count, wide)
-        pieces = sum_parts(near_parts[-2], dqkv[-1:])
-        shards.append(reduce_far(pieces, count, wide))
-        far_da = core_swap(project_far_half(scal, dqkv, qkv_w, pieces))
-        pieces = sum_parts(near_parts[-1])
-        shards.append(reduce_far(pieces, count, wide))
+                pieces = sum_parts(ffn_near, [one])
+                deps = pieces
+        done = reduce_far(pieces, count, wide)
+        early_near = reduce_near(parts, count)
+        one, *parts = backward(pairs - 1, parts_of(1), (), [done])
+        dqkv.append(one)
+        late_near = reduce_near(parts, count)
+        pieces = sum_parts(early_near, [one])
+        early = far_pieces(pieces, count, wide)
+        far_da = project_far_half(scal, dqkv, qkv_w, pieces)
+        pieces = sum_parts(late_near, [far_da])
+        shards = [early, far_pieces(pieces, count, wide)]
+        far_da = core_swap(far_da)
+        grad_tokens = final_rows(scal, dqkv, qkv_w, row, far_da, grad_hidden, gains, pieces)
         rows_here = w_in.shape[1]
         low, high = done[:rows_here], done[rows_here:]
         mine = pick(low, high)
@@ -859,32 +959,29 @@
             axis=1,
         ).T
     else:
-        part_shapes = [(width, 4 * PAIR)]
+        keep, send = weight_grads(False, True, down_cols, scal, *kept)
         grad_w_in = lax.psum_scatter(keep.astype(f32), everyone, scatter_dimension=1, tiled=True)
         grad_down = lax.psum_scatter(send.astype(f32), everyone, scatter_dimension=0, tiled=True).T
         dqkv, shards = [], []
         for i in range(pairs):
-            one, parts = backward(i, ())
+            one, parts = backward(i, [(width, 4 * PAIR)])
             dqkv.append(one)
-            shards.append(lax.psum_scatter(parts.astype(f32), "dp", scatter_dimension=0, tiled=True))
+            shards.append([lax.psum_scatter(parts.astype(f32), "dp", scatter_dimension=0, tiled=True)])
         far_da = core_swap(project_far_half(scal, dqkv, qkv_w))
+        grad_tokens = final_rows(scal, dqkv, qkv_w, row, far_da, grad_hidden, gains)
 
     grad_two = jnp.sum(grad_w_in * w_in.astype(f32), axis=(0, 2)) / ln2_gain.astype(f32)
-    grad_tokens = final_rows(scal, dqkv, qkv_w, row, far_da, grad_hidden, gains)
-
-    grad_qkv = jnp.stack(
-        [jnp.concatenate([s[:, c * PAIR : (c + 1) * PAIR] for s in shards], axis=1) for c in range(3)]
-    )
-    grad_out = jnp.concatenate([s[:, 3 * PAIR :] for s in shards], axis=1).T
-    partial = jnp.sum(grad_qkv * w_qkv.astype(f32), axis=(0, 2))
+
+    grad_qkv, grad_out, partial = finish(shards, w_qkv, [grad_tokens])
     rows_here = ln1_gain.shape[0]
+    partial = partial[:, 0]
     low, high = partial[:rows_here], partial[rows_here:]
     grad_one = (pick(low, high) + core_swap(pick(high, low))) / ln1_gain.astype(f32)
     return (
         result[None],
         grad_tokens[None],
         grad_qkv,
-        grad_out,
+        grad_out.T,
         grad_w_in,
         grad_down,
         grad_one,

time: 320 us -> 300 us (0.938)
  waiting for transfers between devices: 52.4 us -> 25.2 us
  Pallas kernels: 160 us -> 148 us
  local copies, waits for them, and re-layouts: 23.5 us -> 34.8 us
  starting transfers between devices: 58.1 us -> 67.6 us
    ppermute x36 -> x30, waiting for transfers between devices: 43.7 us -> 17.5 us  [xor_permute(): return lax.ppermute(value, 'dp', [(i, i ^ mask) for i in range(count)])]
    unnamed x144 -> x130, local copies, waits for them, and re-layouts: 22.6 us -> 34.6 us
    ppermute x36 -> x30, starting transfers between devices: 56.9 us -> 65.8 us  [xor_permute(): return lax.ppermute(value, 'dp', [(i, i ^ mask) for i in range(count)])]
    pallas_call x3, Pallas kernels: 67 us -> 59.7 us  [backward_pair(): pl.pallas_call(passing(functools.partial(backward_kernel, len(part_shapes...]
    pallas_call x5 -> x8, Pallas kernels: 80.5 us -> 75.8 us  [the longest x3 39.5 us: forward_pair(): pl.pallas_call(passing(kernel, 4 + len(operands), len(deps)), out_shape=t...]
  transfers between devices with their start and end apart: 44 -> 38, of which waited for: 17 -> 10; matrix products, arithmetic and copies ran while one was open for 2% -> 1% of each run, Pallas kernels for 38% -> 40%
where the time goes in v3:
time: 300 us; the launch traced here: 297 us
  Pallas kernels  148 us (49%)
  starting transfers between devices  67.6 us (23%)
  local copies, waits for them, and re-layouts  34.8 us (12%)
  waiting for transfers between devices  25.2 us (8%)
  between operations  15.7 us (5%)
  other arithmetic  6.21 us (2%)
    ppermute x30, starting transfers between devices, xor_permute(): return lax.ppermute(value, 'dp', [(i, i ^ mask) for i in range(count)])  65.8 us
    pallas_call x3, Pallas kernels, backward_pair(): pl.pallas_call(passing(functools.partial(backward_kernel, len(part_shapes...  59.7 us
    pallas_call x3, Pallas kernels, forward_pair(): pl.pallas_call(passing(kernel, 4 + len(operands), len(deps)), out_shape=t...  39.5 us
    unnamed x130, local copies, waits for them, and re-layouts  34.6 us
    pallas_call x1, Pallas kernels, feed_forward(): pl.pallas_call(functools.partial(ffn_kernel, len(outs_of)), out_shape=(sh...  21.3 us
    ppermute x30, waiting for transfers between devices, xor_permute(): return lax.ppermute(value, 'dp', [(i, i ^ mask) for i in range(count)])  17.5 us
    pallas_call x2, Pallas kernels, weight_grads(): pl.pallas_call(passing(functools.partial(weight_grad_kernel, split, own,...  8.09 us
    ppermute x7, waiting for transfers between devices, core_swap(): return lax.ppermute(value, 'head', [(0, 1), (1, 0)])  7.6 us
  transfers between devices with their start and end apart: 38, of which 10 were waited for; matrix products, arithmetic and copies ran while one was open for 1% of the time, Pallas kernels for 40%

profile of v3, /device:TPU:0, one launch (start us, length us, event | category | flops | bytes accessed | tf_op | source)
XLA Modules:
  0.0 296.9 jit_solution(9737075028497924164)
XLA Ops:
  12.8 2.9 collective-permute-start.1
  18.4 3.3 %collective-permute-done.2.refs_2_ = bf16[1,48,512]{2,1,0:T(8,128)(2,1)S(1)} collective-permute-done((bf16[1,48,512]{2,1,0:T(8,128)(2,1)S(1)}, bf16[1,48,512]{2,1,0:T(8,128)(2,1)S(1)}, u32[]{:S(2)}, u32[]{:S(2)}) %collective-permute-start.2) | collective-permute-done | bytes 49184 | tf_op jit(solution)/shard_map/ppermute | solution.py:72
  32.3 7.2 %collective-permute-done.8.refs_2_ = bf16[1,48,1152]{2,1,0:T(8,128)(2,1)S(1)} collective-permute-done((bf16[1,48,1152]{2,1,0:T(8,128)(2,1)S(1)}, bf16[1,48,1152]{2,1,0:T(8,128)(2,1)S(1)}, u32[]{:S(2)}, u32[]{:S(2)}) %collective-permute-start.8) | collective-permute-done | bytes 110624 | tf_op jit(solution)/shard_map/ppermute | solution.py:72
  49.0 13.2 %attention_forward_first.1 = (bf16[2048,768]{1,0:T(8,128)(2,1)S(1)}, f32[16,768]{1,0:T(8,128)S(1)}, bf16[768,512]{1,0:T(8,128)(2,1)S(1)}, bf16[2048,128]{1,0:T(8...) custom-call(s32[6]{0:T(128)S(1)} %pad_add_fusion.refs_0_.scal, ...), custom_call_target="tpu_custom_call" | custom-call | flops 1800000000 | tf_op jit(solution)/shard_map/attention_forward_first/pallas_call | solution.py:408
  67.1 16.3 %attention_forward.2 = (bf16[768,1152]{1,0:T(8,128)(2,1)S(1)}, bf16[2048,128]{1,0:T(8,128)(2,1)S(1)}, bf16[2048,128]{1,0:T(8,128)(2,1)S(1)}, bf16[2048,128]{1,0:...) custom-call(s32[6]{0:T(128)S(1)} %pad_add_fusion.refs_0_.scal, ...), custom_call_target="tpu_custom_call" | custom-call | flops 1800000000 | tf_op jit(solution)/shard_map/attention_forward/pallas_call | solution.py:408
  83.4 10.1 %attention_forward.3 = (bf16[2048,128]{1,0:T(8,128)(2,1)S(1)}, bf16[2048,128]{1,0:T(8,128)(2,1)S(1)}, bf16[2048,128]{1,0:T(8,128)(2,1)S(1)}, bf16[2048,128]{1,0:T(8,128)(2,1)S(1)}, f32[2048,128]{1,0:T(8,128)S(1)}) custom-call(s32[6]{0:T(128)S(1)} %pad_add_fusion.refs_0_.scal, bf16[2048,768]{1,0:T(8,128)(2,1)S(1)} %get-tuple-element.70.refs_1_, ...), custom_call_target="tpu_custom_call" | custom-call | flops 1800000000 | tf_op jit(solution)/shard_map/attention_forward/pallas_call | solution.py:408
  96.5 3.4 %collective-permute-done.13.refs_7_ = bf16[1024,768]{1,0:T(8,128)(2,1)S(1)} collective-permute-done((bf16[1024,768]{1,0:T(8,128)(2,1)S(1)}, bf16[1024,768]{1,0:T(8,128)(2,1)S(1)}, u32[]{:S(2)}, u32[]{:S(2)}) %collective-permute-start.13) | collective-permute-done | bytes 1572896 | tf_op jit(solution)/shard_map/ppermute | solution.py:76
  111.3 21.3 %feed_forward.1 = (bf16[1024,768]{1,0:T(8,128)(2,1)}, bf16[1024,768]{1,0:T(8,128)(2,1)S(1)}, f32[1024,768]{1,0:T(8,128)S(1)}, bf16[1024,1152]{1,0:T(8,128)(2,1)S...) custom-call(s32[6]{0:T(128)S(1)} %pad_add_fusion.refs_0_.scal, ...), custom_call_target="tpu_custom_call" | custom-call | flops 2500000000 | tf_op jit(solution)/shard_map/feed_forward/pallas_call | solution.py:785
  132.6 4.1 %weight_grads.3 = bf16[768,1792]{1,0:T(8,128)(2,1)S(1)} custom-call(s32[6]{0:T(128)S(1)} %pad_add_fusion.refs_0_.scal, bf16[1024,1152]{1,0:T(8,128)(2,1)S(1)} %get-tuple-element.81.refs_1_, bf16[2,1024,1152]{2,1,0:T(8,128)(2,1)S(1)} %get-tuple-element.82.refs_2_, bf16[1024,768]{1,0:T(8,128)(2,1)S(1)} %get-tuple-element.83.refs_3_, ...), custom_call_target="tpu_custom_call" | custom-call | flops 500000000 | tf_op jit(solution)/shard_map/weight_grads/pallas_call | solution.py:765
  137.3 4.0 %weight_grads.2 = bf16[768,1792]{1,0:T(8,128)(2,1)S(1)} custom-call(s32[6]{0:T(128)S(1)} %pad_add_fusion.refs_0_.scal, bf16[1024,1152]{1,0:T(8,128)(2,1)S(1)} %get-tuple-element.81.refs_1_, bf16[2,1024,1152]{2,1,0:T(8,128)(2,1)S(1)} %get-tuple-element.82.refs_2_, bf16[1024,768]{1,0:T(8,128)(2,1)S(1)} %get-tuple-element.83.refs_3_, ...), custom_call_target="tpu_custom_call" | custom-call | flops 500000000 | tf_op jit(solution)/shard_map/weight_grads/pallas_call | solution.py:765
  141.3 2.8 collective-permute-done.15
  147.3 4.6 %collective-permute-start.17 = (bf16[4,48,1792]{2,1,0:T(8,128)(2,1)}, bf16[4,48,1792]{2,1,0:T(8,128)(2,1)}, u32[]{:S(2)}, u32[]{:S(2)}) collective-permute-start(bf16[4,48,1792]{2,1,0:T(8,128)(2,1)} %get-tuple-element.87.refs_14_), channel_id=1, source_target_pairs={{0,4},{2,6},{4,0},{6,2},{8,12},{10,14},{12,8},{14,10},{16,20},{18,... | collective-permute-start | bytes 2064392 | tf_op jit(solution)/shard_map/ppermute | solution.py:72
  161.2 19.4 %attention_backward.3 = (bf16[2048,384]{1,0:T(8,128)(2,1)S(1)}, bf16[768,512]{1,0:T(8,128)(2,1)S(1)}) custom-call(s32[6]{0:T(128)S(1)} %pad_add_fusion.refs_0_.scal, bf16[2048,768]{1,0:T(8,128)(2,1)S(1)} %copy-done.4, bf16[1024,768]{1,0:T(8,128)(2,1)S(1)} %get-tuple-element.76.refs_2_, bf16[1024,768]{1,0:T(8,128)(2,1)} %collective-permute-done.14.refs_3_, ...), custom_call_target="tpu_custom_call" | custom-call | flops 3000000000 | tf_op jit(solution)/shard_map/attention_backward/pallas_call | solution.py:557
  184.5 5.5 %collective-permute-start.19 = (bf16[48,1792]{1,0:T(8,128)(2,1)S(1)}, bf16[48,1792]{1,0:T(8,128)(2,1)S(1)}, u32[]{:S(2)}, u32[]{:S(2)}) collective-permute-start(bf16[48,1792]{1,0:T(8,128)(2,1)S(1)} %get-tuple-element.96.refs_14_), channel_id=1, source_target_pairs={{0,8},{2,10},{4,12},{6,14},{8,0},{10,2},{12,4},{14,6},{16,24},{18,... | collective-permute-start | bytes 516104 | tf_op jit(solution)/shard_map/ppermute | solution.py:72
  190.0 3.2 %collective-permute-start.20 = (bf16[48,1792]{1,0:T(8,128)(2,1)S(1)}, bf16[48,1792]{1,0:T(8,128)(2,1)S(1)}, u32[]{:S(2)}, u32[]{:S(2)}) collective-permute-start(bf16[48,1792]{1,0:T(8,128)(2,1)S(1)} %get-tuple-element.97.refs_15_), channel_id=1, source_target_pairs={{0,16},{2,18},{4,20},{6,22},{8,24},{10,26},{12,28},{14,30},{16,0},... | collective-permute-start | bytes 516104 | tf_op jit(solution)/shard_map/ppermute | solution.py:72
  194.7 20.0 %attention_backward.4 = (bf16[2048,384]{1,0:T(8,128)(2,1)S(1)}, bf16[4,48,1024]{2,1,0:T(8,128)(2,1)S(1)}, bf16[4,48,1024]{2,1,0:T(8,128)(2,1)S(1)}, bf16[4,48,10...) custom-call(s32[6]{0:T(128)S(1)} %pad_add_fusion.refs_0_.scal, bf16[2048,768]{1,0:T(8,128)(2,1)S(1)} %copy-done.4, ...), custom_call_target="tpu_custom_call" | custom-call | flops 3000000000 | tf_op jit(solution)/shard_map/attention_backward/pallas_call | solution.py:557
  214.8 5.3 %collective-permute-start.23 = (bf16[4,48,1024]{2,1,0:T(8,128)(2,1)S(1)}, bf16[4,48,1024]{2,1,0:T(8,128)(2,1)S(1)}, u32[]{:S(2)}, u32[]{:S(2)}) collective-permute-start(bf16[4,48,1024]{2,1,0:T(8,128)(2,1)S(1)} %get-tuple-element.108), channel_id=1, source_target_pairs={{0,4},{2,6},{4,0},{6,2},{8,12},{10,14},{12,8},{14,10},{16,20},{18,... | collective-permute-start | bytes 1179656 | tf_op jit(solution)/shard_map/ppermute | solution.py:72
  220.4 20.3 %attention_backward.5 = (bf16[2048,384]{1,0:T(8,128)(2,1)S(1)}, bf16[4,48,512]{2,1,0:T(8,128)(2,1)S(1)}, bf16[4,48,512]{2,1,0:T(8,128)(2,1)S(1)}, bf16[4,48,512]{2,1,0:T(8,128)(2,1)S(1)}, bf16[4,48,512]{2,1,0:T(8,128)(2,1)S(1)}) custom-call(s32[6]{0:T(128)S(1)} %pad_add_fusion.refs_0_.scal, bf16[2048,768]{1,0:T(8,128)(2,1)S(1)} %copy-done.4, ...), custom_call_target="tpu_custom_call" | custom-call | flops 3000000000 | tf_op jit(solution)/shard_map/attention_backward/pallas_call | solution.py:557
  241.8 3.9 %project_far_half.3.refs_4_ = bf16[1024,768]{1,0:T(8,128)(2,1)S(1)} custom-call(s32[6]{0:T(128)S(1)} %pad_add_fusion.refs_0_.scal, bf16[2048,384]{1,0:T(8,128)(2,1)S(1)} %get-tuple-element.89.refs_4_.refs_1_, bf16[2048,384]{1,0:T(8,128)(2,1)S(1)} %get-tuple-element.99.refs_2_, bf16[2048,384]{1,0:T(8,128)(2,1)S(1)} %get-tuple-element.104.refs_4_.refs_3_, ...), custom_call_target="tpu_custom_call" | custom-call | flops 400000000 | tf_op jit(solution)/shard_map/project_far_half/pallas_call | solution.py:599
  246.3 5.2 %collective-permute-start.27 = (bf16[4,48,512]{2,1,0:T(8,128)(2,1)S(1)}, bf16[4,48,512]{2,1,0:T(8,128)(2,1)S(1)}, u32[]{:S(2)}, u32[]{:S(2)}) collective-permute-start(bf16[4,48,512]{2,1,0:T(8,128)(2,1)S(1)} %get-tuple-element.117), channel_id=1, source_target_pairs={{0,4},{2,6},{4,0},{6,2},{8,12},{10,14},{12,8},{14,10},{16,20},{18,... | collective-permute-start | bytes 589832 | tf_op jit(solution)/shard_map/ppermute | solution.py:72
  252.4 12.1 %collective-permute-start.29 = (bf16[48,1024]{1,0:T(8,128)(2,1)S(1)}, bf16[48,1024]{1,0:T(8,128)(2,1)S(1)}, u32[]{:S(2)}, u32[]{:S(2)}) collective-permute-start(bf16[48,1024]{1,0:T(8,128)(2,1)S(1)} %get-tuple-element.111.refs_8_), channel_id=1, source_target_pairs={{0,8},{2,10},{4,12},{6,14},{8,0},{10,2},{12,4},{14,6},{16,24},{18,... | collective-permute-start | bytes 294920 | tf_op jit(solution)/shard_map/ppermute | solution.py:72
  267.0 5.7 %collective-permute-start.32 = (bf16[48,512]{1,0:T(8,128)(2,1)S(1)}, bf16[48,512]{1,0:T(8,128)(2,1)S(1)}, u32[]{:S(2)}, u32[]{:S(2)}) collective-permute-start(bf16[48,512]{1,0:T(8,128)(2,1)S(1)} %get-tuple-element.120.refs_12_), channel_id=1, source_target_pairs={{0,8},{2,10},{4,12},{6,14},{8,0},{10,2},{12,4},{14,6},{16,24},{18,... | collective-permute-start | bytes 147464 | tf_op jit(solution)/shard_map/ppermute | solution.py:72
  276.5 2.7 collective-permute-start.34
  279.2 6.1 %final_rows.1.refs_9_ = f32[1024,768]{1,0:T(8,128)} custom-call(s32[6]{0:T(128)S(1)} %pad_add_fusion.refs_0_.scal, bf16[2048,384]{1,0:T(8,128)(2,1)S(1)} %get-tuple-element.89.refs_4_.refs_1_, bf16[2048,384]{1,0:T(8,128)(2,1)S(1)} %get-tuple-element.99.refs_2_, bf16[2048,384]{1,0:T(8,128)(2,1)S(1)} %get-tuple-element.104.refs_4_.refs_3_, ...), custom_call_target="tpu_custom_call" | custom-call | flops 700000000 | tf_op jit(solution)/shard_map/final_rows/pallas_call | solution.py:633
  (221 shorter events, 78.6 us)
Async XLA Ops:
  7.2 93.8 %all-gather.2.cloned.1.call-start = ((), (), s32[]{:S(2)}) async-start(), calls=%async_computation | async-start | bytes 5474304 | tf_op jit(solution)/shard_map/all_gather | solution.py:880
  24.4 15.2 %collective-permute-start.4 = (bf16[4,48,512]{2,1,0:T(8,128)(2,1)S(1)}, bf16[4,48,512]{2,1,0:T(8,128)(2,1)S(1)}, u32[]{:S(2)}, u32[]{:S(2)}) collective-permute-start(bf16[4,48,512]{2,1,0:T(8,128)(2,1)S(1)} %stack_parts.3.refs_4_), channel_id=1, source_target_pairs={{0,2},{2,0},{4,6},{6,4},{8,10},{10,8},{12,14},{14,12},{16,18},{18,... | collective-permute-start | bytes 589832 | tf_op jit(solution)/shard_map/ppermute | solution.py:72
  25.9 13.6 %collective-permute-start.5 = (bf16[4,48,512]{2,1,0:T(8,128)(2,1)S(1)}, bf16[4,48,512]{2,1,0:T(8,128)(2,1)S(1)}, u32[]{:S(2)}, u32[]{:S(2)}) collective-permute-start(bf16[4,48,512]{2,1,0:T(8,128)(2,1)S(1)} %stack_parts.3.refs_4_), channel_id=1, source_target_pairs={{0,4},{2,6},{4,0},{6,2},{8,12},{10,14},{12,8},{14,10},{16,20},{18,... | collective-permute-start | bytes 589832 | tf_op jit(solution)/shard_map/ppermute | solution.py:72
  41.0 26.0 %collective-permute-start.10 = (bf16[4,48,1152]{2,1,0:T(8,128)(2,1)}, bf16[4,48,1152]{2,1,0:T(8,128)(2,1)}, u32[]{:S(2)}, u32[]{:S(2)}) collective-permute-start(bf16[4,48,1152]{2,1,0:T(8,128)(2,1)} %stack_parts.5.refs_8_.refs_4_), channel_id=1, source_target_pairs={{0,2},{2,0},{4,6},{6,4},{8,10},{10,8},{12,14},{14,12},{16,18},{18,... | collective-permute-start | bytes 1327112 | tf_op jit(solution)/shard_map/ppermute | solution.py:72
  42.6 24.5 %collective-permute-start.11 = (bf16[4,48,1152]{2,1,0:T(8,128)(2,1)}, bf16[4,48,1152]{2,1,0:T(8,128)(2,1)}, u32[]{:S(2)}, u32[]{:S(2)}) collective-permute-start(bf16[4,48,1152]{2,1,0:T(8,128)(2,1)} %stack_parts.5.refs_8_.refs_4_), channel_id=1, source_target_pairs={{0,4},{2,6},{4,0},{6,2},{8,12},{10,14},{12,8},{14,10},{16,20},{18,... | collective-permute-start | bytes 1327112 | tf_op jit(solution)/shard_map/ppermute | solution.py:72
  43.6 23.5 %collective-permute-start.12 = (bf16[4,48,1152]{2,1,0:T(8,128)(2,1)}, bf16[4,48,1152]{2,1,0:T(8,128)(2,1)}, u32[]{:S(2)}, u32[]{:S(2)}) collective-permute-start(bf16[4,48,1152]{2,1,0:T(8,128)(2,1)} %stack_parts.5.refs_8_.refs_4_), channel_id=1, source_target_pairs={{0,6},{2,4},{4,2},{6,0},{8,14},{10,12},{12,10},{14,8},{16,22},{18,... | collective-permute-start | bytes 1327112 | tf_op jit(solution)/shard_map/ppermute | solution.py:72
  136.9 15.1 %collective-permute-start.14 = (bf16[1024,768]{1,0:T(8,128)(2,1)S(1)}, bf16[1024,768]{1,0:T(8,128)(2,1)}, u32[]{:S(2)}, u32[]{:S(2)}) collective-permute-start(bf16[1024,768]{1,0:T(8,128)(2,1)S(1)} %get-tuple-element.76.refs_2_), channel_id=1, source_target_pairs={{0,1},{1,0},{2,3},{3,2},{4,5},{5,4},{6,7},{7,6},{8,9},{9,8},{10,11... | collective-permute-start | bytes 4718600 | tf_op jit(solution)/shard_map/ppermute | solution.py:76
  147.2 33.4 %collective-permute-start.16 = (bf16[4,48,1792]{2,1,0:T(8,128)(2,1)}, bf16[4,48,1792]{2,1,0:T(8,128)(2,1)}, u32[]{:S(2)}, u32[]{:S(2)}) collective-permute-start(bf16[4,48,1792]{2,1,0:T(8,128)(2,1)} %get-tuple-element.86.refs_13_), channel_id=1, source_target_pairs={{0,2},{2,0},{4,6},{6,4},{8,10},{10,8},{12,14},{14,12},{16,18},{18,... | collective-permute-start | bytes 2064392 | tf_op jit(solution)/shard_map/ppermute | solution.py:72
  147.3 35.1 %collective-permute-start.17 = (bf16[4,48,1792]{2,1,0:T(8,128)(2,1)}, bf16[4,48,1792]{2,1,0:T(8,128)(2,1)}, u32[]{:S(2)}, u32[]{:S(2)}) collective-permute-start(bf16[4,48,1792]{2,1,0:T(8,128)(2,1)} %get-tuple-element.87.refs_14_), channel_id=1, source_target_pairs={{0,4},{2,6},{4,0},{6,2},{8,12},{10,14},{12,8},{14,10},{16,20},{18,... | collective-permute-start | bytes 2064392 | tf_op jit(solution)/shard_map/ppermute | solution.py:72
  151.9 30.5 %collective-permute-start.18 = (bf16[4,48,1792]{2,1,0:T(8,128)(2,1)}, bf16[4,48,1792]{2,1,0:T(8,128)(2,1)}, u32[]{:S(2)}, u32[]{:S(2)}) collective-permute-start(bf16[4,48,1792]{2,1,0:T(8,128)(2,1)} %get-tuple-element.88.refs_15_), channel_id=1, source_target_pairs={{0,6},{2,4},{4,2},{6,0},{8,14},{10,12},{12,10},{14,8},{16,22},{18,... | collective-permute-start | bytes 2064392 | tf_op jit(solution)/shard_map/ppermute | solution.py:72
  184.5 35.6 %collective-permute-start.19 = (bf16[48,1792]{1,0:T(8,128)(2,1)S(1)}, bf16[48,1792]{1,0:T(8,128)(2,1)S(1)}, u32[]{:S(2)}, u32[]{:S(2)}) collective-permute-start(bf16[48,1792]{1,0:T(8,128)(2,1)S(1)} %get-tuple-element.96.refs_14_), channel_id=1, source_target_pairs={{0,8},{2,10},{4,12},{6,14},{8,0},{10,2},{12,4},{14,6},{16,24},{18,... | collective-permute-start | bytes 516104 | tf_op jit(solution)/shard_map/ppermute | solution.py:72
  190.0 30.1 %collective-permute-start.20 = (bf16[48,1792]{1,0:T(8,128)(2,1)S(1)}, bf16[48,1792]{1,0:T(8,128)(2,1)S(1)}, u32[]{:S(2)}, u32[]{:S(2)}) collective-permute-start(bf16[48,1792]{1,0:T(8,128)(2,1)S(1)} %get-tuple-element.97.refs_15_), channel_id=1, source_target_pairs={{0,16},{2,18},{4,20},{6,22},{8,24},{10,26},{12,28},{14,30},{16,0},... | collective-permute-start | bytes 516104 | tf_op jit(solution)/shard_map/ppermute | solution.py:72
  193.2 26.9 %collective-permute-start.21 = (bf16[48,1792]{1,0:T(8,128)(2,1)S(1)}, bf16[48,1792]{1,0:T(8,128)(2,1)S(1)}, u32[]{:S(2)}, u32[]{:S(2)}) collective-permute-start(bf16[48,1792]{1,0:T(8,128)(2,1)S(1)} %get-tuple-element.98.refs_16_), channel_id=1, source_target_pairs={{0,24},{2,26},{4,28},{6,30},{8,16},{10,18},{12,20},{14,22},{16,8},... | collective-permute-start | bytes 516104 | tf_op jit(solution)/shard_map/ppermute | solution.py:72
  214.7 25.9 %collective-permute-start.22 = (bf16[4,48,1024]{2,1,0:T(8,128)(2,1)S(1)}, bf16[4,48,1024]{2,1,0:T(8,128)(2,1)S(1)}, u32[]{:S(2)}, u32[]{:S(2)}) collective-permute-start(bf16[4,48,1024]{2,1,0:T(8,128)(2,1)S(1)} %get-tuple-element.107), channel_id=1, source_target_pairs={{0,2},{2,0},{4,6},{6,4},{8,10},{10,8},{12,14},{14,12},{16,18},{18,... | collective-permute-start | bytes 1179656 | tf_op jit(solution)/shard_map/ppermute | solution.py:72
  214.8 25.8 %collective-permute-start.23 = (bf16[4,48,1024]{2,1,0:T(8,128)(2,1)S(1)}, bf16[4,48,1024]{2,1,0:T(8,128)(2,1)S(1)}, u32[]{:S(2)}, u32[]{:S(2)}) collective-permute-start(bf16[4,48,1024]{2,1,0:T(8,128)(2,1)S(1)} %get-tuple-element.108), channel_id=1, source_target_pairs={{0,4},{2,6},{4,0},{6,2},{8,12},{10,14},{12,8},{14,10},{16,20},{18,... | collective-permute-start | bytes 1179656 | tf_op jit(solution)/shard_map/ppermute | solution.py:72
  220.1 20.6 %collective-permute-start.24 = (bf16[4,48,1024]{2,1,0:T(8,128)(2,1)S(1)}, bf16[4,48,1024]{2,1,0:T(8,128)(2,1)S(1)}, u32[]{:S(2)}, u32[]{:S(2)}) collective-permute-start(bf16[4,48,1024]{2,1,0:T(8,128)(2,1)S(1)} %get-tuple-element.109), channel_id=1, source_target_pairs={{0,6},{2,4},{4,2},{6,0},{8,14},{10,12},{12,10},{14,8},{16,22},{18,... | collective-permute-start | bytes 1179656 | tf_op jit(solution)/shard_map/ppermute | solution.py:72
  220.2 31.2 %collective-permute-start.35 = (f32[24,1792]{1,0:T(8,128)S(1)}, f32[24,1792]{1,0:T(8,128)S(1)}, u32[]{:S(2)}, u32[]{:S(2)}) collective-permute-start(f32[24,1792]{1,0:T(8,128)S(1)} %get-tuple-element.136), channel_id=1, source_target_pairs={{0,1},{1,0},{2,3},{3,2},{4,5},{5,4},{6,7},{7,6},{8,9},{9,8},{10,11... | collective-permute-start | bytes 516104 | tf_op jit(solution)/shard_map/ppermute | solution.py:76
  245.7 30.7 %collective-permute-start.25 = (bf16[1024,768]{1,0:T(8,128)(2,1)S(1)}, bf16[1024,768]{1,0:T(8,128)(2,1)S(1)}, u32[]{:S(2)}, u32[]{:S(2)}) collective-permute-start(bf16[1024,768]{1,0:T(8,128)(2,1)S(1)} %project_far_half.3.refs_4_), channel_id=1, source_target_pairs={{0,1},{1,0},{2,3},{3,2},{4,5},{5,4},{6,7},{7,6},{8,9},{9,8},{10,11... | collective-permute-start | bytes 4718600 | tf_op jit(solution)/shard_map/ppermute | solution.py:76
  246.3 18.2 %collective-permute-start.26 = (bf16[4,48,512]{2,1,0:T(8,128)(2,1)S(1)}, bf16[4,48,512]{2,1,0:T(8,128)(2,1)S(1)}, u32[]{:S(2)}, u32[]{:S(2)}) collective-permute-start(bf16[4,48,512]{2,1,0:T(8,128)(2,1)S(1)} %get-tuple-element.116), channel_id=1, source_target_pairs={{0,2},{2,0},{4,6},{6,4},{8,10},{10,8},{12,14},{14,12},{16,18},{18,... | collective-permute-start | bytes 589832 | tf_op jit(solution)/shard_map/ppermute | solution.py:72
  246.3 18.2 %collective-permute-start.27 = (bf16[4,48,512]{2,1,0:T(8,128)(2,1)S(1)}, bf16[4,48,512]{2,1,0:T(8,128)(2,1)S(1)}, u32[]{:S(2)}, u32[]{:S(2)}) collective-permute-start(bf16[4,48,512]{2,1,0:T(8,128)(2,1)S(1)} %get-tuple-element.117), channel_id=1, source_target_pairs={{0,4},{2,6},{4,0},{6,2},{8,12},{10,14},{12,8},{14,10},{16,20},{18,... | collective-permute-start | bytes 589832 | tf_op jit(solution)/shard_map/ppermute | solution.py:72
  251.5 15.4 %collective-permute-start.28 = (bf16[4,48,512]{2,1,0:T(8,128)(2,1)S(1)}, bf16[4,48,512]{2,1,0:T(8,128)(2,1)S(1)}, u32[]{:S(2)}, u32[]{:S(2)}) collective-permute-start(bf16[4,48,512]{2,1,0:T(8,128)(2,1)S(1)} %get-tuple-element.118), channel_id=1, source_target_pairs={{0,6},{2,4},{4,2},{6,0},{8,14},{10,12},{12,10},{14,8},{16,22},{18,... | collective-permute-start | bytes 589832 | tf_op jit(solution)/shard_map/ppermute | solution.py:72
  252.4 32.9 %collective-permute-start.29 = (bf16[48,1024]{1,0:T(8,128)(2,1)S(1)}, bf16[48,1024]{1,0:T(8,128)(2,1)S(1)}, u32[]{:S(2)}, u32[]{:S(2)}) collective-permute-start(bf16[48,1024]{1,0:T(8,128)(2,1)S(1)} %get-tuple-element.111.refs_8_), channel_id=1, source_target_pairs={{0,8},{2,10},{4,12},{6,14},{8,0},{10,2},{12,4},{14,6},{16,24},{18,... | collective-permute-start | bytes 294920 | tf_op jit(solution)/shard_map/ppermute | solution.py:72
  264.5 20.8 %collective-permute-start.30 = (bf16[48,1024]{1,0:T(8,128)(2,1)S(1)}, bf16[48,1024]{1,0:T(8,128)(2,1)S(1)}, u32[]{:S(2)}, u32[]{:S(2)}) collective-permute-start(bf16[48,1024]{1,0:T(8,128)(2,1)S(1)} %get-tuple-element.112.refs_9_), channel_id=1, source_target_pairs={{0,16},{2,18},{4,20},{6,22},{8,24},{10,26},{12,28},{14,30},{16,0},... | collective-permute-start | bytes 294920 | tf_op jit(solution)/shard_map/ppermute | solution.py:72
  264.5 20.8 %collective-permute-start.31 = (bf16[48,1024]{1,0:T(8,128)(2,1)S(1)}, bf16[48,1024]{1,0:T(8,128)(2,1)S(1)}, u32[]{:S(2)}, u32[]{:S(2)}) collective-permute-start(bf16[48,1024]{1,0:T(8,128)(2,1)S(1)} %get-tuple-element.113.refs_10_), channel_id=1, source_target_pairs={{0,24},{2,26},{4,28},{6,30},{8,16},{10,18},{12,20},{14,22},{16,8},... | collective-permute-start | bytes 294920 | tf_op jit(solution)/shard_map/ppermute | solution.py:72
  (79 other events, 591.1 us)
Sparse Core Ops, SparseCore 0:
  10.9 76.0 all-gather.1

commit v4 on v3

--- a/solution.py
+++ b/solution.py
@@ -17,7 +17,7 @@
 LOG2_SCALE = math.log2(math.e) / math.sqrt(HEAD_DIM)
 SCORE_SCALE = 1.0 / math.sqrt(HEAD_DIM)
 ROW_BLOCK = 256
-FWD_MIB, BWD_MIB, FFN_MIB = 20, 23, 18
+FWD_MIB, BWD_MIB, FFN_MIB = 20, 23, 25
 FWD_BQ, FWD_STEP = 512, 256
 BWD_BQ, BWD_STEP, BWD_CHUNK = 256, 128, 12
 NT = (((1,), (1,)), ((), ()))
@@ -615,7 +615,8 @@
 
 def final_kernel(count, scal, *refs):
     rows, weights = refs[:count], refs[count : 2 * count]
-    tokens, far, grad_hidden, gains, out = refs[2 * count :]
+    tokens, far, grad_hidden, gains, out, mark = refs[2 * count :]
+    mark[...] = jnp.zeros(mark.shape, mark.dtype)
     total = far[...].astype(f32)
     for one, w in zip(rows, weights):
         total = total + lax.dot_general(one[...], w[...], NT, preferred_element_type=f32)
@@ -632,7 +633,7 @@
     plain = pl.BlockSpec((ROW_BLOCK, width), lambda b, s: (b, 0))
     return pl.pallas_call(
         passing(functools.partial(final_kernel, len(rows)), 5 + 2 * len(rows), len(deps)),
-        out_shape=jax.ShapeDtypeStruct((length // 2, width), f32),
+        out_shape=(jax.ShapeDtypeStruct((length // 2, width), f32), jax.ShapeDtypeStruct((8, PAIR), f32)),
         grid_spec=pltpu.PrefetchScalarGridSpec(
             num_scalar_prefetch=1,
             grid=(blocks,),
@@ -640,7 +641,7 @@
             + [columns_of(w, at, cols) for w, at in weights]
             + [near(tokens), plain, plain, whole(gains)]
             + [anywhere()] * len(deps),
-            out_specs=plain,
+            out_specs=(plain, pl.BlockSpec((8, PAIR), lambda b, s: (0, 0))),
         ),
         compiler_params=params(),
         cost_estimate=lasts(7),
@@ -688,14 +689,50 @@
     )(*flat, w_qkv, *deps)
 
 
-def ffn_kernel(count, scal, *refs):
+def ffn_kernel(count, part_count, down_cols, scal, *refs):
     outs_of, weights = refs[:count], refs[count : 2 * count]
-    tokens, far, cot, gains, ffn_w = refs[2 * count : 2 * count + 5]
-    result, dattn, grad_hidden, z_all, pair_all, a2_all, dff_all = refs[2 * count + 5 :]
+    tokens, far, cot, gains = refs[2 * count : 2 * count + 4]
+    sources = refs[2 * count + 4 : -9]
+    result, dattn, grad_hidden, z_all, pair_all, a2_all, dff_all, ffn_w, sems = refs[-9:]
     width, ff = ffn_w.shape[1:]
     live, me, core = scal[0], scal[1], scal[2]
     step = pl.program_id(0)
     block = result.shape[0]
+
+    @pl.when(step == 0)
+    def _():
+        copies = []
+        if part_count == 1:
+            copies.append(pltpu.make_async_copy(sources[0], ffn_w.at[pl.ds(0, 2)], sems.at[0]))
+            copies.append(pltpu.make_async_copy(sources[1], ffn_w.at[2], sems.at[1]))
+        else:
+            offset = ff - down_cols
+            rows_each = sources[0].shape[1]
+            near_at = pl.multiple_of(core * offset, PAIR)
+            far_from = pl.multiple_of(ff + (1 - core) * (down_cols - offset), PAIR)
+            far_at = pl.multiple_of((1 - core) * down_cols, PAIR)
+            for h in range(sources[0].shape[0]):
+                for j in range(part_count):
+                    own = jnp.bitwise_xor(me, h * part_count + j)
+                    at = pl.ds(pl.multiple_of(own * rows_each, 16), rows_each)
+                    number = 4 * (h * part_count + j)
+                    mine, other = sources[j].at[h], sources[part_count + j].at[h]
+                    copies += [
+                        pltpu.make_async_copy(mine.at[:, :ff], ffn_w.at[core, at], sems.at[number]),
+                        pltpu.make_async_copy(other.at[:, :ff], ffn_w.at[1 - core, at], sems.at[number + 1]),
+                        pltpu.make_async_copy(
+                            mine.at[:, ff:], ffn_w.at[2, at, pl.ds(near_at, down_cols)], sems.at[number + 2]
+                        ),
+                        pltpu.make_async_copy(
+                            other.at[:, pl.ds(far_from, offset)],
+                            ffn_w.at[2, at, pl.ds(far_at, offset)],
+                            sems.at[number + 3],
+                        ),
+                    ]
+        for copy in copies:
+            copy.start()
+        for copy in copies:
+            copy.wait()
 
     here = core * (block * pl.num_programs(0)) + step * block
     position = here + lax.broadcasted_iota(jnp.int32, (block, 1), 0)
@@ -773,9 +810,9 @@
     )(scal, z, pair, a2, dff, *deps)
 
 
-def feed_forward(scal, outs_of, weights, tokens, far, cot, gains, ffn_w):
-    length = tokens.shape[0]
-    width, ff = ffn_w.shape[1:]
+def feed_forward(scal, outs_of, weights, tokens, far, cot, gains, sources, ff, down_cols):
+    length, width = tokens.shape
+    part_count = len(sources) // 2
     half = length // 2
     blocks = half // ROW_BLOCK
     shape = jax.ShapeDtypeStruct
@@ -783,7 +820,7 @@
     near = lambda a: pl.BlockSpec((ROW_BLOCK, a.shape[1]), lambda b, s: (b + s[2] * blocks, 0))
     plain = lambda cols: pl.BlockSpec((ROW_BLOCK, cols), lambda b, s: (b, 0))
     return pl.pallas_call(
-        functools.partial(ffn_kernel, len(outs_of)),
+        functools.partial(ffn_kernel, len(outs_of), part_count, down_cols),
         out_shape=(
             shape((half, width), bf16),
             shape((half, width), bf16),
@@ -799,7 +836,7 @@
             in_specs=[near(o) for o in outs_of]
             + [columns_of(w, at, PAIR) for w, at in weights]
             + [near(tokens), plain(width), plain(width), whole(gains)]
-            + [vmem()],
+            + [anywhere()] * len(sources),
             out_specs=(
                 plain(width),
                 plain(width),
@@ -809,11 +846,12 @@
                 plain(width),
                 plain(width),
             ),
+            scratch_shapes=[pltpu.VMEM((3, width, ff), bf16), pltpu.SemaphoreType.DMA((64,))],
         ),
         compiler_params=params(FFN_MIB),
         cost_estimate=lasts(25),
         name="feed_forward",
-    )(scal, *outs_of, *[w for w, _ in weights], tokens, far, cot, gains, ffn_w)
+    )(scal, *outs_of, *[w for w, _ in weights], tokens, far, cot, gains, *sources)
 
 
 def pack_kernel(wide, scal, keep, got, *outs):
@@ -877,7 +915,6 @@
     tables = rotary_tables(length)
     out_at = 3 * PAIR * (pairs - 1)
     everyone = ("dp", "head")
-    ffn_w = lax.all_gather(jnp.concatenate([w_in, down_turned[None]]), everyone, axis=1, tiled=True)
 
     if fast:
         high_bits, low_bits = bit_groups(count)
@@ -886,17 +923,31 @@
         head_parts = gather_step(stack_parts(head_high), count, low_bits)
         rest_high = gather_step(rest_load, count, high_bits)
         rest_all = stack_parts(rest_high, head_parts[1:])
+        zero_one = jnp.concatenate([w_in[0], down_turned[:, :down_cols]], axis=1)
+        one_two = jnp.concatenate([w_in[1], down_turned[:, offset:]], axis=1)
+        ffn_load = join(pick(zero_one, one_two), core_swap(pick(one_two, zero_one)))
+        ffn_load = stack_parts([ffn_load[None]], rest_high[1:])
+        ffn_high = gather_step(ffn_load, count, high_bits)
         a1, gains, *kept = forward_pair(
-            True, scal, row, tables, head_parts, 0, [rest_all]
+            True, scal, row, tables, head_parts, 0, [rest_all, ffn_load]
         )
         rest_parts = gather_step(rest_all, count, low_bits)
+        ffn_all = stack_parts(ffn_high, [a1])
+        ffn_parts = gather_step(ffn_all, count, low_bits)
+        sources = ffn_parts + [core_swap(p) for p in ffn_parts]
+        deps, late_deps = [ffn_all], ffn_parts[1:]
     else:
         head_parts = [lax.all_gather(head_load, "dp", axis=0, tiled=True)]
         rest_parts = [lax.all_gather(rest_load, "dp", axis=0, tiled=True)]
+        sources = [
+            lax.all_gather(w_in, everyone, axis=1, tiled=True),
+            lax.all_gather(down_turned, everyone, axis=0, tiled=True),
+        ]
         a1, gains, *kept = forward_pair(True, scal, row, tables, head_parts, 0)
+        deps, late_deps = [], []
 
     head_w, saved = kept[0], [kept[1:]]
-    rest_w, *kept = forward_pair(False, scal, a1, tables, rest_parts, 0)
+    rest_w, *kept = forward_pair(False, scal, a1, tables, rest_parts, 0, deps)
     saved.append(kept)
     for i in range(2, pairs):
         saved.append(forward_pair(False, scal, a1, tables, rest_w, 3 * PAIR * (i - 1)))
@@ -904,8 +955,8 @@
     out_w = [(rest_w, out_at + i * PAIR) for i in range(pairs)]
     outs_of = [s[3] for s in saved]
 
-    far = core_swap(project_far_half(scal, outs_of, out_w))
-    result, near_grad, grad_hidden, *kept = feed_forward(scal, outs_of, out_w, row, far, cot, gains, ffn_w)
+    far = core_swap(project_far_half(scal, outs_of, out_w, late_deps))
+    result, near_grad, grad_hidden, *kept = feed_forward(scal, outs_of, out_w, row, far, cot, gains, sources, ff, down_cols)
     far_grad = core_swap(near_grad)
 
     def backward(i, part_shapes, before=(), deps=()):
@@ -946,7 +997,7 @@
         pieces = sum_parts(late_near, [far_da])
         shards = [early, far_pieces(pieces, count, wide)]
         far_da = core_swap(far_da)
-        grad_tokens = final_rows(scal, dqkv, qkv_w, row, far_da, grad_hidden, gains, pieces)
+        grad_tokens, mark = final_rows(scal, dqkv, qkv_w, row, far_da, grad_hidden, gains, pieces)
         rows_here = w_in.shape[1]
         low, high = done[:rows_here], done[rows_here:]
         mine = pick(low, high)
@@ -968,11 +1019,11 @@
             dqkv.append(one)
             shards.append([lax.psum_scatter(parts.astype(f32), "dp", scatter_dimension=0, tiled=True)])
         far_da = core_swap(project_far_half(scal, dqkv, qkv_w))
-        grad_tokens = final_rows(scal, dqkv, qkv_w, row, far_da, grad_hidden, gains)
+        grad_tokens, mark = final_rows(scal, dqkv, qkv_w, row, far_da, grad_hidden, gains)
 
     grad_two = jnp.sum(grad_w_in * w_in.astype(f32), axis=(0, 2)) / ln2_gain.astype(f32)
 
-    grad_qkv, grad_out, partial = finish(shards, w_qkv, [grad_tokens])
+    grad_qkv, grad_out, partial = finish(shards, w_qkv, [mark])
     rows_here = ln1_gain.shape[0]
     partial = partial[:, 0]
     low, high = partial[:rows_here], partial[rows_here:]

time: 300 us -> 261 us (0.87)
  local copies, waits for them, and re-layouts: 34.8 us -> 7.01 us
  Pallas kernels: 148 us -> 125 us
  waiting for transfers between devices: 25.2 us -> 41.1 us
  between operations: 15.7 us -> 2.15 us
  starting transfers between devices: 67.6 us -> 78.3 us
    unnamed x130 -> x66, local copies, waits for them, and re-layouts: 34.6 us -> 5.12 us
    pallas_call x3, Pallas kernels: 59.7 us -> 43.4 us  [backward_pair(): pl.pallas_call(passing(functools.partial(backward_kernel, len(part_shapes...]
    ppermute x30 -> x36, waiting for transfers between devices: 17.5 us -> 33.7 us  [xor_permute(): return lax.ppermute(value, 'dp', [(i, i ^ mask) for i in range(count)])]
    ppermute x30 -> x36, starting transfers between devices: 65.8 us -> 75.8 us  [xor_permute(): return lax.ppermute(value, 'dp', [(i, i ^ mask) for i in range(count)])]
    pallas_call x3, Pallas kernels: 39.5 us -> 34.8 us  [forward_pair(): pl.pallas_call(passing(kernel, 4 + len(operands), len(deps)), out_shape=t...]
    ppermute x7 -> x12, waiting for transfers between devices: 7.6 us -> 7.39 us  [core_swap(): return lax.ppermute(value, 'head', [(0, 1), (1, 0)])]
  transfers between devices with their start and end apart: 38 -> 48, of which waited for: 10 -> 15; matrix products, arithmetic and copies ran while one was open for 1% -> 2% of each run, Pallas kernels for 40% -> 37%
where the time goes in v4:
time: 261 us; the launch traced here: 257 us
  Pallas kernels  125 us (48%)
  starting transfers between devices  78.3 us (30%)
  waiting for transfers between devices  41.1 us (16%)
  local copies, waits for them, and re-layouts  7.01 us (3%)
  other arithmetic  3.82 us (1%)
    ppermute x36, starting transfers between devices, xor_permute(): return lax.ppermute(value, 'dp', [(i, i ^ mask) for i in range(count)])  75.8 us
    pallas_call x3, Pallas kernels, backward_pair(): pl.pallas_call(passing(functools.partial(backward_kernel, len(part_shapes...  43.4 us
    pallas_call x3, Pallas kernels, forward_pair(): pl.pallas_call(passing(kernel, 4 + len(operands), len(deps)), out_shape=t...  34.8 us
    ppermute x36, waiting for transfers between devices, xor_permute(): return lax.ppermute(value, 'dp', [(i, i ^ mask) for i in range(count)])  33.7 us
    pallas_call x1, Pallas kernels, feed_forward(): pl.pallas_call(functools.partial(ffn_kernel, len(outs_of), part_count, do...  22.9 us
    pallas_call x2, Pallas kernels, weight_grads(): pl.pallas_call(passing(functools.partial(weight_grad_kernel, split, own,...  8.08 us
    ppermute x12, waiting for transfers between devices, core_swap(): return lax.ppermute(value, 'head', [(0, 1), (1, 0)])  7.39 us
    pallas_call x2, Pallas kernels, project_far_half(): pl.pallas_call(passing(functools.partial(project_kernel, count), 1 + 2 *...  6.57 us
  transfers between devices with their start and end apart: 48, of which 15 were waited for; matrix products, arithmetic and copies ran while one was open for 2% of the time, Pallas kernels for 37%

profile of v4, /device:TPU:0, one launch (start us, length us, event | category | flops | bytes accessed | tf_op | source)
XLA Modules:
  0.0 257.0 jit_solution(4291168026392771361)
XLA Ops:
  11.3 2.8 %collective-permute-done.2.refs_2_ = bf16[1,48,512]{2,1,0:T(8,128)(2,1)S(1)} collective-permute-done((bf16[1,48,512]{2,1,0:T(8,128)(2,1)S(1)}, bf16[1,48,512]{2,1,0:T(8,128)(2,1)S(1)}, u32[]{:S(2)}, u32[]{:S(2)}) %collective-permute-start.2) | collective-permute-done | bytes 49184 | tf_op jit(solution)/shard_map/ppermute | solution.py:72
  24.5 5.4 %collective-permute-done.8.refs_2_ = bf16[1,48,1152]{2,1,0:T(8,128)(2,1)S(1)} collective-permute-done((bf16[1,48,1152]{2,1,0:T(8,128)(2,1)S(1)}, bf16[1,48,1152]{2,1,0:T(8,128)(2,1)S(1)}, u32[]{:S(2)}, u32[]{:S(2)}) %collective-permute-start.8) | collective-permute-done | bytes 110624 | tf_op jit(solution)/shard_map/ppermute | solution.py:72
  40.5 11.2 %attention_forward_first.1 = (bf16[2048,768]{1,0:T(8,128)(2,1)S(1)}, f32[16,768]{1,0:T(8,128)S(1)}, bf16[768,512]{1,0:T(8,128)(2,1)S(1)}, bf16[2048,128]{1,0:T(8...) custom-call(s32[6]{0:T(128)S(1)} %pad_add_fusion.refs_0_.scal, ...), custom_call_target="tpu_custom_call" | custom-call | flops 1800000000 | tf_op jit(solution)/shard_map/attention_forward_first/pallas_call | solution.py:408
  53.3 4.8 %collective-permute-start.17 = (bf16[4,48,1792]{2,1,0:T(8,128)(2,1)S(1)}, bf16[4,48,1792]{2,1,0:T(8,128)(2,1)S(1)}, u32[]{:S(2)}, u32[]{:S(2)}) collective-permute-start(bf16[4,48,1792]{2,1,0:T(8,128)(2,1)S(1)} %stack_parts.9.refs_8_.refs_10_), channel_id=1, source_target_pairs={{0,2},{2,0},{4,6},{6,4},{8,10},{10,8},{12,14},{14,12},{16,18},{18,... | collective-permute-start | bytes 2064392 | tf_op jit(solution)/shard_map/ppermute | solution.py:72
  59.5 14.9 %attention_forward.2 = (bf16[768,1152]{1,0:T(8,128)(2,1)S(1)}, bf16[2048,128]{1,0:T(8,128)(2,1)S(1)}, bf16[2048,128]{1,0:T(8,128)(2,1)S(1)}, bf16[2048,128]{1,0:...) custom-call(s32[6]{0:T(128)S(1)} %pad_add_fusion.refs_0_.scal, ...), custom_call_target="tpu_custom_call" | custom-call | flops 1800000000 | tf_op jit(solution)/shard_map/attention_forward/pallas_call | solution.py:408
  75.4 8.6 %attention_forward.3 = (bf16[2048,128]{1,0:T(8,128)(2,1)S(1)}, bf16[2048,128]{1,0:T(8,128)(2,1)S(1)}, bf16[2048,128]{1,0:T(8,128)(2,1)S(1)}, bf16[2048,128]{1,0:T(8,128)(2,1)S(1)}, f32[2048,128]{1,0:T(8,128)S(1)}) custom-call(s32[6]{0:T(128)S(1)} %pad_add_fusion.refs_0_.scal, bf16[2048,768]{1,0:T(8,128)(2,1)S(1)} %get-tuple-element.72.refs_4_.refs_1_, ...), custom_call_target="tpu_custom_call" | custom-call | flops 1800000000 | tf_op jit(solution)/shard_map/attention_forward/pallas_call | solution.py:408
  85.1 2.6 %project_far_half.2 = bf16[1024,768]{1,0:T(8,128)(2,1)S(1)} custom-call(s32[6]{0:T(128)S(1)} %pad_add_fusion.refs_0_.scal, bf16[2048,128]{1,0:T(8,128)(2,1)S(1)} %get-tuple-element.71.refs_1_.refs_0_.refs_8_, bf16[2048,128]{1,0:T(8,128)(2,1)S(1)} %get-tuple-element.73.refs_2_.refs_1_.refs_8_, ...), custom_call_target="tpu_custom_call" | custom-call | flops 400000000 | tf_op jit(solution)/shard_map/project_far_half/pallas_call | solution.py:599
  88.9 3.3 %collective-permute-done.21.refs_14_ = bf16[4,48,1792]{2,1,0:T(8,128)(2,1)S(1)} collective-permute-done((bf16[4,48,1792]{2,1,0:T(8,128)(2,1)S(1)}, bf16[4,48,1792]{2,1,0:T(8,128)(2,1)S(1)}, u32[]{:S(2)}, u32[]{:S(2)}) %collective-permute-start.21) | collective-permute-done | bytes 688160 | tf_op jit(solution)/shard_map/ppermute | solution.py:76
  95.2 22.9 %feed_forward.1 = (bf16[1024,768]{1,0:T(8,128)(2,1)}, bf16[1024,768]{1,0:T(8,128)(2,1)S(1)}, f32[1024,768]{1,0:T(8,128)S(1)}, bf16[1024,1152]{1,0:T(8,128)(2,1)S...) custom-call(s32[6]{0:T(128)S(1)} %pad_add_fusion.refs_0_.scal, ...), custom_call_target="tpu_custom_call" | custom-call | flops 2500000000 | tf_op jit(solution)/shard_map/feed_forward/pallas_call | solution.py:822
  118.1 4.1 %weight_grads.3 = bf16[768,1792]{1,0:T(8,128)(2,1)S(1)} custom-call(s32[6]{0:T(128)S(1)} %pad_add_fusion.refs_0_.scal, bf16[1024,1152]{1,0:T(8,128)(2,1)S(1)} %get-tuple-element.83.refs_1_, bf16[2,1024,1152]{2,1,0:T(8,128)(2,1)S(1)} %get-tuple-element.84.refs_2_, bf16[1024,768]{1,0:T(8,128)(2,1)S(1)} %get-tuple-element.85.refs_3_, ...), custom_call_target="tpu_custom_call" | custom-call | flops 500000000 | tf_op jit(solution)/shard_map/weight_grads/pallas_call | solution.py:802
  122.8 4.0 %weight_grads.2 = bf16[768,1792]{1,0:T(8,128)(2,1)S(1)} custom-call(s32[6]{0:T(128)S(1)} %pad_add_fusion.refs_0_.scal, bf16[1024,1152]{1,0:T(8,128)(2,1)S(1)} %get-tuple-element.83.refs_1_, bf16[2,1024,1152]{2,1,0:T(8,128)(2,1)S(1)} %get-tuple-element.84.refs_2_, bf16[1024,768]{1,0:T(8,128)(2,1)S(1)} %get-tuple-element.85.refs_3_, ...), custom_call_target="tpu_custom_call" | custom-call | flops 500000000 | tf_op jit(solution)/shard_map/weight_grads/pallas_call | solution.py:802
  128.5 4.9 %collective-permute-start.27 = (bf16[4,48,1792]{2,1,0:T(8,128)(2,1)S(1)}, bf16[4,48,1792]{2,1,0:T(8,128)(2,1)S(1)}, u32[]{:S(2)}, u32[]{:S(2)}) collective-permute-start(bf16[4,48,1792]{2,1,0:T(8,128)(2,1)S(1)} %get-tuple-element.88.refs_13_), channel_id=1, source_target_pairs={{0,2},{2,0},{4,6},{6,4},{8,10},{10,8},{12,14},{14,12},{16,18},{18,... | collective-permute-start | bytes 2064392 | tf_op jit(solution)/shard_map/ppermute | solution.py:72
  135.1 13.8 %attention_backward.3 = (bf16[2048,384]{1,0:T(8,128)(2,1)S(1)}, bf16[768,512]{1,0:T(8,128)(2,1)S(1)}) custom-call(s32[6]{0:T(128)S(1)} %pad_add_fusion.refs_0_.scal, bf16[2048,768]{1,0:T(8,128)(2,1)S(1)} %get-tuple-element.72.refs_4_.refs_1_, bf16[1024,768]{1,0:T(8,128)(2,1)S(1)} %get-tuple-element.78.refs_2_, ...), custom_call_target="tpu_custom_call" | custom-call | flops 3000000000 | tf_op jit(solution)/shard_map/attention_backward/pallas_call | solution.py:557
  149.7 15.7 %collective-permute-done.28.refs_2_ = bf16[4,48,1792]{2,1,0:T(8,128)(2,1)S(1)} collective-permute-done((bf16[4,48,1792]{2,1,0:T(8,128)(2,1)S(1)}, bf16[4,48,1792]{2,1,0:T(8,128)(2,1)S(1)}, u32[]{:S(2)}, u32[]{:S(2)}) %collective-permute-start.28) | collective-permute-done | bytes 688160 | tf_op jit(solution)/shard_map/ppermute | solution.py:72
  165.7 3.1 %collective-permute-start.30 = (bf16[48,1792]{1,0:T(8,128)(2,1)S(1)}, bf16[48,1792]{1,0:T(8,128)(2,1)S(1)}, u32[]{:S(2)}, u32[]{:S(2)}) collective-permute-start(bf16[48,1792]{1,0:T(8,128)(2,1)S(1)} %get-tuple-element.98.refs_14_), channel_id=1, source_target_pairs={{0,8},{2,10},{4,12},{6,14},{8,0},{10,2},{12,4},{14,6},{16,24},{18,... | collective-permute-start | bytes 516104 | tf_op jit(solution)/shard_map/ppermute | solution.py:72
  171.3 14.3 %attention_backward.4 = (bf16[2048,384]{1,0:T(8,128)(2,1)S(1)}, bf16[4,48,1024]{2,1,0:T(8,128)(2,1)S(1)}, bf16[4,48,1024]{2,1,0:T(8,128)(2,1)S(1)}, bf16[4,48,10...) custom-call(s32[6]{0:T(128)S(1)} %pad_add_fusion.refs_0_.scal, bf16[2048,768]{1,0:T(8,128)(2,1)S(1)} %get-tuple-element.72.refs_4_.refs_1_, ...), custom_call_target="tpu_custom_call" | custom-call | flops 3000000000 | tf_op jit(solution)/shard_map/attention_backward/pallas_call | solution.py:557
  185.6 9.5 %collective-permute-start.33 = (bf16[4,48,1024]{2,1,0:T(8,128)(2,1)S(1)}, bf16[4,48,1024]{2,1,0:T(8,128)(2,1)S(1)}, u32[]{:S(2)}, u32[]{:S(2)}) collective-permute-start(bf16[4,48,1024]{2,1,0:T(8,128)(2,1)S(1)} %get-tuple-element.109), channel_id=1, source_target_pairs={{0,2},{2,0},{4,6},{6,4},{8,10},{10,8},{12,14},{14,12},{16,18},{18,... | collective-permute-start | bytes 1179656 | tf_op jit(solution)/shard_map/ppermute | solution.py:72
  196.9 15.3 %attention_backward.5 = (bf16[2048,384]{1,0:T(8,128)(2,1)S(1)}, bf16[4,48,512]{2,1,0:T(8,128)(2,1)S(1)}, bf16[4,48,512]{2,1,0:T(8,128)(2,1)S(1)}, bf16[4,48,512]{2,1,0:T(8,128)(2,1)S(1)}, bf16[4,48,512]{2,1,0:T(8,128)(2,1)S(1)}) custom-call(s32[6]{0:T(128)S(1)} %pad_add_fusion.refs_0_.scal, bf16[2048,768]{1,0:T(8,128)(2,1)S(1)} %get-tuple-element.72.refs_4_.refs_1_, ...), custom_call_target="tpu_custom_call" | custom-call | flops 3000000000 | tf_op jit(solution)/shard_map/attention_backward/pallas_call | solution.py:557
  212.9 4.0 %project_far_half.3.refs_4_ = bf16[1024,768]{1,0:T(8,128)(2,1)S(1)} custom-call(s32[6]{0:T(128)S(1)} %pad_add_fusion.refs_0_.scal, bf16[2048,384]{1,0:T(8,128)(2,1)S(1)} %get-tuple-element.91.refs_4_.refs_1_, bf16[2048,384]{1,0:T(8,128)(2,1)S(1)} %get-tuple-element.101.refs_2_, bf16[2048,384]{1,0:T(8,128)(2,1)S(1)} %get-tuple-element.106.refs_4_.refs_3_, ...), custom_call_target="tpu_custom_call" | custom-call | flops 400000000 | tf_op jit(solution)/shard_map/project_far_half/pallas_call | solution.py:599
  217.0 9.2 %collective-permute-start.37 = (bf16[4,48,512]{2,1,0:T(8,128)(2,1)S(1)}, bf16[4,48,512]{2,1,0:T(8,128)(2,1)S(1)}, u32[]{:S(2)}, u32[]{:S(2)}) collective-permute-start(bf16[4,48,512]{2,1,0:T(8,128)(2,1)S(1)} %get-tuple-element.118), channel_id=1, source_target_pairs={{0,2},{2,0},{4,6},{6,4},{8,10},{10,8},{12,14},{14,12},{16,18},{18,... | collective-permute-start | bytes 589832 | tf_op jit(solution)/shard_map/ppermute | solution.py:72
  228.6 6.1 %collective-permute-start.40 = (bf16[48,1024]{1,0:T(8,128)(2,1)S(1)}, bf16[48,1024]{1,0:T(8,128)(2,1)S(1)}, u32[]{:S(2)}, u32[]{:S(2)}) collective-permute-start(bf16[48,1024]{1,0:T(8,128)(2,1)S(1)} %get-tuple-element.113.refs_8_), channel_id=1, source_target_pairs={{0,8},{2,10},{4,12},{6,14},{8,0},{10,2},{12,4},{14,6},{16,24},{18,... | collective-permute-start | bytes 294920 | tf_op jit(solution)/shard_map/ppermute | solution.py:72
  237.0 3.3 %collective-permute-start.42 = (bf16[48,1024]{1,0:T(8,128)(2,1)S(1)}, bf16[48,1024]{1,0:T(8,128)(2,1)S(1)}, u32[]{:S(2)}, u32[]{:S(2)}) collective-permute-start(bf16[48,1024]{1,0:T(8,128)(2,1)S(1)} %get-tuple-element.115.refs_10_), channel_id=1, source_target_pairs={{0,24},{2,26},{4,28},{6,30},{8,16},{10,18},{12,20},{14,22},{16,8},... | collective-permute-start | bytes 294920 | tf_op jit(solution)/shard_map/ppermute | solution.py:72
  242.2 2.7 %collective-permute-done.43.refs_5_ = bf16[48,512]{1,0:T(8,128)(2,1)S(1)} collective-permute-done((bf16[48,512]{1,0:T(8,128)(2,1)S(1)}, bf16[48,512]{1,0:T(8,128)(2,1)S(1)}, u32[]{:S(2)}, u32[]{:S(2)}) %collective-permute-start.43) | collective-permute-done | bytes 49184 | tf_op jit(solution)/shard_map/ppermute | solution.py:72
  248.0 6.1 %final_rows.1 = (f32[1024,768]{1,0:T(8,128)}, f32[8,128]{1,0:T(8,128)S(1)}) custom-call(s32[6]{0:T(128)S(1)} %pad_add_fusion.refs_0_.scal, bf16[2048,384]{1,0:T(8,128)(2,1)S(1)} %get-tuple-element.91.refs_4_.refs_1_, bf16[2048,384]{1,0:T(8,128)(2,1)S(1)} %get-tuple-element.101.refs_2_, bf16[2048,384]{1,0:T(8,128)(2,1)S(1)} %get-tuple-element.106.refs_4_.refs_3_, ...), custom_call_target="tpu_custom_call" | custom-call | flops 700000000 | tf_op jit(solution)/shard_map/final_rows/pallas_call | solution.py:634
  (182 shorter events, 62.1 us)
Async XLA Ops:
  30.0 28.6 %collective-permute-start.11 = (bf16[4,48,1152]{2,1,0:T(8,128)(2,1)S(1)}, bf16[4,48,1152]{2,1,0:T(8,128)(2,1)S(1)}, u32[]{:S(2)}, u32[]{:S(2)}) collective-permute-start(bf16[4,48,1152]{2,1,0:T(8,128)(2,1)S(1)} %stack_parts.7.refs_8_.refs_4_), channel_id=1, source_target_pairs={{0,2},{2,0},{4,6},{6,4},{8,10},{10,8},{12,14},{14,12},{16,18},{18,... | collective-permute-start | bytes 1327112 | tf_op jit(solution)/shard_map/ppermute | solution.py:72
  33.6 18.3 %collective-permute-start.15 = (bf16[1,48,1792]{2,1,0:T(8,128)(2,1)S(1)}, bf16[1,48,1792]{2,1,0:T(8,128)(2,1)S(1)}, u32[]{:S(2)}, u32[]{:S(2)}) collective-permute-start(bf16[1,48,1792]{2,1,0:T(8,128)(2,1)S(1)} %stack_parts.8.refs_9_.refs_0_), channel_id=1, source_target_pairs={{0,16},{2,18},{4,20},{6,22},{8,24},{10,26},{12,28},{14,30},{16,0},... | collective-permute-start | bytes 516104 | tf_op jit(solution)/shard_map/ppermute | solution.py:72
  34.8 17.0 %collective-permute-start.16 = (bf16[1,48,1792]{2,1,0:T(8,128)(2,1)S(1)}, bf16[1,48,1792]{2,1,0:T(8,128)(2,1)S(1)}, u32[]{:S(2)}, u32[]{:S(2)}) collective-permute-start(bf16[1,48,1792]{2,1,0:T(8,128)(2,1)S(1)} %stack_parts.8.refs_9_.refs_0_), channel_id=1, source_target_pairs={{0,24},{2,26},{4,28},{6,30},{8,16},{10,18},{12,20},{14,22},{16,8},... | collective-permute-start | bytes 516104 | tf_op jit(solution)/shard_map/ppermute | solution.py:72
  36.3 23.2 %collective-permute-start.12 = (bf16[4,48,1152]{2,1,0:T(8,128)(2,1)S(1)}, bf16[4,48,1152]{2,1,0:T(8,128)(2,1)S(1)}, u32[]{:S(2)}, u32[]{:S(2)}) collective-permute-start(bf16[4,48,1152]{2,1,0:T(8,128)(2,1)S(1)} %stack_parts.7.refs_8_.refs_4_), channel_id=1, source_target_pairs={{0,4},{2,6},{4,0},{6,2},{8,12},{10,14},{12,8},{14,10},{16,20},{18,... | collective-permute-start | bytes 1327112 | tf_op jit(solution)/shard_map/ppermute | solution.py:72
  39.0 20.5 %collective-permute-start.13 = (bf16[4,48,1152]{2,1,0:T(8,128)(2,1)S(1)}, bf16[4,48,1152]{2,1,0:T(8,128)(2,1)S(1)}, u32[]{:S(2)}, u32[]{:S(2)}) collective-permute-start(bf16[4,48,1152]{2,1,0:T(8,128)(2,1)S(1)} %stack_parts.7.refs_8_.refs_4_), channel_id=1, source_target_pairs={{0,6},{2,4},{4,2},{6,0},{8,14},{10,12},{12,10},{14,8},{16,22},{18,... | collective-permute-start | bytes 1327112 | tf_op jit(solution)/shard_map/ppermute | solution.py:72
  53.3 31.8 %collective-permute-start.17 = (bf16[4,48,1792]{2,1,0:T(8,128)(2,1)S(1)}, bf16[4,48,1792]{2,1,0:T(8,128)(2,1)S(1)}, u32[]{:S(2)}, u32[]{:S(2)}) collective-permute-start(bf16[4,48,1792]{2,1,0:T(8,128)(2,1)S(1)} %stack_parts.9.refs_8_.refs_10_), channel_id=1, source_target_pairs={{0,2},{2,0},{4,6},{6,4},{8,10},{10,8},{12,14},{14,12},{16,18},{18,... | collective-permute-start | bytes 2064392 | tf_op jit(solution)/shard_map/ppermute | solution.py:72
  58.1 27.0 %collective-permute-start.18 = (bf16[4,48,1792]{2,1,0:T(8,128)(2,1)S(1)}, bf16[4,48,1792]{2,1,0:T(8,128)(2,1)S(1)}, u32[]{:S(2)}, u32[]{:S(2)}) collective-permute-start(bf16[4,48,1792]{2,1,0:T(8,128)(2,1)S(1)} %stack_parts.9.refs_8_.refs_10_), channel_id=1, source_target_pairs={{0,4},{2,6},{4,0},{6,2},{8,12},{10,14},{12,8},{14,10},{16,20},{18,... | collective-permute-start | bytes 2064392 | tf_op jit(solution)/shard_map/ppermute | solution.py:72
  58.6 26.5 %collective-permute-start.19 = (bf16[4,48,1792]{2,1,0:T(8,128)(2,1)S(1)}, bf16[4,48,1792]{2,1,0:T(8,128)(2,1)S(1)}, u32[]{:S(2)}, u32[]{:S(2)}) collective-permute-start(bf16[4,48,1792]{2,1,0:T(8,128)(2,1)S(1)} %stack_parts.9.refs_8_.refs_10_), channel_id=1, source_target_pairs={{0,6},{2,4},{4,2},{6,0},{8,14},{10,12},{12,10},{14,8},{16,22},{18,... | collective-permute-start | bytes 2064392 | tf_op jit(solution)/shard_map/ppermute | solution.py:72
  128.5 21.1 %collective-permute-start.27 = (bf16[4,48,1792]{2,1,0:T(8,128)(2,1)S(1)}, bf16[4,48,1792]{2,1,0:T(8,128)(2,1)S(1)}, u32[]{:S(2)}, u32[]{:S(2)}) collective-permute-start(bf16[4,48,1792]{2,1,0:T(8,128)(2,1)S(1)} %get-tuple-element.88.refs_13_), channel_id=1, source_target_pairs={{0,2},{2,0},{4,6},{6,4},{8,10},{10,8},{12,14},{14,12},{16,18},{18,... | collective-permute-start | bytes 2064392 | tf_op jit(solution)/shard_map/ppermute | solution.py:72
  133.4 31.9 %collective-permute-start.28 = (bf16[4,48,1792]{2,1,0:T(8,128)(2,1)S(1)}, bf16[4,48,1792]{2,1,0:T(8,128)(2,1)S(1)}, u32[]{:S(2)}, u32[]{:S(2)}) collective-permute-start(bf16[4,48,1792]{2,1,0:T(8,128)(2,1)S(1)} %get-tuple-element.89.refs_14_), channel_id=1, source_target_pairs={{0,4},{2,6},{4,0},{6,2},{8,12},{10,14},{12,8},{14,10},{16,20},{18,... | collective-permute-start | bytes 2064392 | tf_op jit(solution)/shard_map/ppermute | solution.py:72
  134.0 31.4 %collective-permute-start.29 = (bf16[4,48,1792]{2,1,0:T(8,128)(2,1)S(1)}, bf16[4,48,1792]{2,1,0:T(8,128)(2,1)S(1)}, u32[]{:S(2)}, u32[]{:S(2)}) collective-permute-start(bf16[4,48,1792]{2,1,0:T(8,128)(2,1)S(1)} %get-tuple-element.90.refs_15_), channel_id=1, source_target_pairs={{0,6},{2,4},{4,2},{6,0},{8,14},{10,12},{12,10},{14,8},{16,22},{18,... | collective-permute-start | bytes 2064392 | tf_op jit(solution)/shard_map/ppermute | solution.py:72
  165.7 29.7 %collective-permute-start.30 = (bf16[48,1792]{1,0:T(8,128)(2,1)S(1)}, bf16[48,1792]{1,0:T(8,128)(2,1)S(1)}, u32[]{:S(2)}, u32[]{:S(2)}) collective-permute-start(bf16[48,1792]{1,0:T(8,128)(2,1)S(1)} %get-tuple-element.98.refs_14_), channel_id=1, source_target_pairs={{0,8},{2,10},{4,12},{6,14},{8,0},{10,2},{12,4},{14,6},{16,24},{18,... | collective-permute-start | bytes 516104 | tf_op jit(solution)/shard_map/ppermute | solution.py:72
  168.9 27.8 %collective-permute-start.31 = (bf16[48,1792]{1,0:T(8,128)(2,1)S(1)}, bf16[48,1792]{1,0:T(8,128)(2,1)S(1)}, u32[]{:S(2)}, u32[]{:S(2)}) collective-permute-start(bf16[48,1792]{1,0:T(8,128)(2,1)S(1)} %get-tuple-element.99.refs_15_), channel_id=1, source_target_pairs={{0,16},{2,18},{4,20},{6,22},{8,24},{10,26},{12,28},{14,30},{16,0},... | collective-permute-start | bytes 516104 | tf_op jit(solution)/shard_map/ppermute | solution.py:72
  168.9 27.8 %collective-permute-start.32 = (bf16[48,1792]{1,0:T(8,128)(2,1)S(1)}, bf16[48,1792]{1,0:T(8,128)(2,1)S(1)}, u32[]{:S(2)}, u32[]{:S(2)}) collective-permute-start(bf16[48,1792]{1,0:T(8,128)(2,1)S(1)} %get-tuple-element.100.refs_16_), channel_id=1, source_target_pairs={{0,24},{2,26},{4,28},{6,30},{8,16},{10,18},{12,20},{14,22},{16,8},... | collective-permute-start | bytes 516104 | tf_op jit(solution)/shard_map/ppermute | solution.py:72
  185.6 26.6 %collective-permute-start.33 = (bf16[4,48,1024]{2,1,0:T(8,128)(2,1)S(1)}, bf16[4,48,1024]{2,1,0:T(8,128)(2,1)S(1)}, u32[]{:S(2)}, u32[]{:S(2)}) collective-permute-start(bf16[4,48,1024]{2,1,0:T(8,128)(2,1)S(1)} %get-tuple-element.109), channel_id=1, source_target_pairs={{0,2},{2,0},{4,6},{6,4},{8,10},{10,8},{12,14},{14,12},{16,18},{18,... | collective-permute-start | bytes 1179656 | tf_op jit(solution)/shard_map/ppermute | solution.py:72
  195.1 17.6 %collective-permute-start.34 = (bf16[4,48,1024]{2,1,0:T(8,128)(2,1)S(1)}, bf16[4,48,1024]{2,1,0:T(8,128)(2,1)S(1)}, u32[]{:S(2)}, u32[]{:S(2)}) collective-permute-start(bf16[4,48,1024]{2,1,0:T(8,128)(2,1)S(1)} %get-tuple-element.110), channel_id=1, source_target_pairs={{0,4},{2,6},{4,0},{6,2},{8,12},{10,14},{12,8},{14,10},{16,20},{18,... | collective-permute-start | bytes 1179656 | tf_op jit(solution)/shard_map/ppermute | solution.py:72
  195.5 17.3 %collective-permute-start.35 = (bf16[4,48,1024]{2,1,0:T(8,128)(2,1)S(1)}, bf16[4,48,1024]{2,1,0:T(8,128)(2,1)S(1)}, u32[]{:S(2)}, u32[]{:S(2)}) collective-permute-start(bf16[4,48,1024]{2,1,0:T(8,128)(2,1)S(1)} %get-tuple-element.111), channel_id=1, source_target_pairs={{0,6},{2,4},{4,2},{6,0},{8,14},{10,12},{12,10},{14,8},{16,22},{18,... | collective-permute-start | bytes 1179656 | tf_op jit(solution)/shard_map/ppermute | solution.py:72
  196.8 30.9 %collective-permute-start.46 = (f32[24,1792]{1,0:T(8,128)S(1)}, f32[24,1792]{1,0:T(8,128)S(1)}, u32[]{:S(2)}, u32[]{:S(2)}) collective-permute-start(f32[24,1792]{1,0:T(8,128)S(1)} %get-tuple-element.140), channel_id=1, source_target_pairs={{0,1},{1,0},{2,3},{3,2},{4,5},{5,4},{6,7},{7,6},{8,9},{9,8},{10,11... | collective-permute-start | bytes 516104 | tf_op jit(solution)/shard_map/ppermute | solution.py:76
  216.9 30.2 %collective-permute-start.36 = (bf16[1024,768]{1,0:T(8,128)(2,1)S(1)}, bf16[1024,768]{1,0:T(8,128)(2,1)S(1)}, u32[]{:S(2)}, u32[]{:S(2)}) collective-permute-start(bf16[1024,768]{1,0:T(8,128)(2,1)S(1)} %project_far_half.3.refs_4_), channel_id=1, source_target_pairs={{0,1},{1,0},{2,3},{3,2},{4,5},{5,4},{6,7},{7,6},{8,9},{9,8},{10,11... | collective-permute-start | bytes 4718600 | tf_op jit(solution)/shard_map/ppermute | solution.py:76
  217.0 17.7 %collective-permute-start.37 = (bf16[4,48,512]{2,1,0:T(8,128)(2,1)S(1)}, bf16[4,48,512]{2,1,0:T(8,128)(2,1)S(1)}, u32[]{:S(2)}, u32[]{:S(2)}) collective-permute-start(bf16[4,48,512]{2,1,0:T(8,128)(2,1)S(1)} %get-tuple-element.118), channel_id=1, source_target_pairs={{0,2},{2,0},{4,6},{6,4},{8,10},{10,8},{12,14},{14,12},{16,18},{18,... | collective-permute-start | bytes 589832 | tf_op jit(solution)/shard_map/ppermute | solution.py:72
  226.6 13.8 %collective-permute-start.39 = (bf16[4,48,512]{2,1,0:T(8,128)(2,1)S(1)}, bf16[4,48,512]{2,1,0:T(8,128)(2,1)S(1)}, u32[]{:S(2)}, u32[]{:S(2)}) collective-permute-start(bf16[4,48,512]{2,1,0:T(8,128)(2,1)S(1)} %get-tuple-element.120), channel_id=1, source_target_pairs={{0,6},{2,4},{4,2},{6,0},{8,14},{10,12},{12,10},{14,8},{16,22},{18,... | collective-permute-start | bytes 589832 | tf_op jit(solution)/shard_map/ppermute | solution.py:72
  228.6 25.5 %collective-permute-start.40 = (bf16[48,1024]{1,0:T(8,128)(2,1)S(1)}, bf16[48,1024]{1,0:T(8,128)(2,1)S(1)}, u32[]{:S(2)}, u32[]{:S(2)}) collective-permute-start(bf16[48,1024]{1,0:T(8,128)(2,1)S(1)} %get-tuple-element.113.refs_8_), channel_id=1, source_target_pairs={{0,8},{2,10},{4,12},{6,14},{8,0},{10,2},{12,4},{14,6},{16,24},{18,... | collective-permute-start | bytes 294920 | tf_op jit(solution)/shard_map/ppermute | solution.py:72
  234.7 19.4 %collective-permute-start.41 = (bf16[48,1024]{1,0:T(8,128)(2,1)S(1)}, bf16[48,1024]{1,0:T(8,128)(2,1)S(1)}, u32[]{:S(2)}, u32[]{:S(2)}) collective-permute-start(bf16[48,1024]{1,0:T(8,128)(2,1)S(1)} %get-tuple-element.114.refs_9_), channel_id=1, source_target_pairs={{0,16},{2,18},{4,20},{6,22},{8,24},{10,26},{12,28},{14,30},{16,0},... | collective-permute-start | bytes 294920 | tf_op jit(solution)/shard_map/ppermute | solution.py:72
  237.0 17.1 %collective-permute-start.42 = (bf16[48,1024]{1,0:T(8,128)(2,1)S(1)}, bf16[48,1024]{1,0:T(8,128)(2,1)S(1)}, u32[]{:S(2)}, u32[]{:S(2)}) collective-permute-start(bf16[48,1024]{1,0:T(8,128)(2,1)S(1)} %get-tuple-element.115.refs_10_), channel_id=1, source_target_pairs={{0,24},{2,26},{4,28},{6,30},{8,16},{10,18},{12,20},{14,22},{16,8},... | collective-permute-start | bytes 294920 | tf_op jit(solution)/shard_map/ppermute | solution.py:72
  (57 other events, 475.6 us)

commit v5 on v4

--- a/solution.py
+++ b/solution.py
@@ -17,6 +17,7 @@
 LOG2_SCALE = math.log2(math.e) / math.sqrt(HEAD_DIM)
 SCORE_SCALE = 1.0 / math.sqrt(HEAD_DIM)
 ROW_BLOCK = 256
+PREP_BLOCK = 512
 FWD_MIB, BWD_MIB, FFN_MIB = 20, 23, 25
 FWD_BQ, FWD_STEP = 512, 256
 BWD_BQ, BWD_STEP, BWD_CHUNK = 256, 128, 12
@@ -76,25 +77,23 @@
     return lax.ppermute(value, "head", [(0, 1), (1, 0)])
 
 
-def stack_kernel(*refs):
+def stack_kernel(at, *refs):
     ins, out = refs[:-1], refs[-1]
-    wide = len(ins)
     for j, one in enumerate(ins):
-        for h in range(one.shape[0]):
-            out[h * wide + j] = one[h]
-
-
-def stack_parts(parts, deps=()):
-    m, rows, cols = parts[0].shape
+        out[jnp.bitwise_xor(at[0], j) if len(ins) > 1 else 0] = one[0]
+
+
+def stack_parts(at, parts, deps=()):
+    _, rows, cols = parts[0].shape
     return pl.pallas_call(
-        passing(stack_kernel, len(parts), len(deps)),
-        out_shape=jax.ShapeDtypeStruct((m * len(parts), rows, cols), parts[0].dtype),
-        in_specs=[vmem()] * len(parts) + [anywhere()] * len(deps),
+        passing(stack_kernel, 1 + len(parts), len(deps)),
+        out_shape=jax.ShapeDtypeStruct((len(parts), rows, cols), parts[0].dtype),
+        in_specs=[smem()] + [vmem()] * len(parts) + [anywhere()] * len(deps),
         out_specs=vmem(),
         compiler_params=params(),
         cost_estimate=lasts(1),
         name="stack_parts",
-    )(*parts, *deps)
+    )(at, *parts, *deps)
 
 
 def gather_step(current, count, group):
@@ -102,28 +101,29 @@
     return [current] + [xor_permute(current, count, j << shift) for j in range(1, 1 << wide)]
 
 
-def sum_kernel(count, *refs):
+def sum_kernel(count, at, *refs):
     ins, outs = refs[:count], refs[count:]
     for i, out in enumerate(outs):
-        total = ins[0][i].astype(f32)
+        entry = jnp.bitwise_xor(at[0], i)
+        total = ins[0][entry].astype(f32)
         for one in ins[1:]:
-            total = total + one[i].astype(f32)
+            total = total + one[entry].astype(f32)
         out[...] = total.astype(out.dtype)
 
 
-def sum_parts(arrays, deps=()):
+def sum_parts(at, arrays, deps=()):
     m, rows, cols = arrays[0].shape
     return pl.pallas_call(
-        passing(functools.partial(sum_kernel, len(arrays)), len(arrays), len(deps)),
+        passing(functools.partial(sum_kernel, len(arrays)), 1 + len(arrays), len(deps)),
         out_shape=tuple(
             jax.ShapeDtypeStruct((rows, cols), f32 if i == 0 else bf16) for i in range(m)
         ),
-        in_specs=[vmem()] * len(arrays) + [anywhere()] * len(deps),
+        in_specs=[smem()] + [vmem()] * len(arrays) + [anywhere()] * len(deps),
         out_specs=(vmem(),) * m,
         compiler_params=params(),
         cost_estimate=lasts(2),
         name="sum_parts",
-    )(*arrays, *deps)
+    )(at, *arrays, *deps)
 
 
 def reduce_near(parts, count):
@@ -171,21 +171,16 @@
     )(scal, w_qkv, out_turned, mine, other)
 
 
-def placed_copies(parts, target, sems, me, rows, cols):
+def placed_copies(parts, target, sems, me, cols):
     if len(parts) == 1:
         return [pltpu.make_async_copy(parts[0].at[:, cols], target.at[:, cols], sems.at[0])]
+    wide = len(parts)
     copies = []
-    wide = len(parts)
-    for h in range(parts[0].shape[0]):
-        for j in range(wide):
-            own = jnp.bitwise_xor(me, h * wide + j)
-            copies.append(
-                pltpu.make_async_copy(
-                    parts[j].at[h, :, cols],
-                    target.at[pl.ds(pl.multiple_of(own * rows, 16), rows), cols],
-                    sems.at[h * wide + j],
-                )
-            )
+    for j in range(wide):
+        low = jnp.bitwise_xor(me & (wide - 1), j)
+        copies.append(
+            pltpu.make_async_copy(parts[j].at[:, :, cols], target.at[:, low, :, cols], sems.at[j])
+        )
     return copies
 
 
@@ -316,9 +311,10 @@
     copies, later = [], []
     if part_count:
         soon = 4 * PAIR if first else 3 * PAIR
-        copies = placed_copies(parts, w, sems.at[0], me, parts[0].shape[-2], slice(0, soon))
-        if w.shape[1] > soon:
-            later = placed_copies(parts, w, sems.at[1], me, parts[0].shape[-2], slice(soon, w.shape[1]))
+        copies = placed_copies(parts, w, sems.at[0], me, slice(0, soon))
+        if w.shape[-1] > soon:
+            later = placed_copies(parts, w, sems.at[1], me, slice(soon, w.shape[-1]))
+        w = w.reshape(width, w.shape[-1])
     for copy in copies + later:
         copy.start()
     starts = document_starts(scal, length)
@@ -329,14 +325,14 @@
         turned = jnp.transpose(w[:, 3 * PAIR : 4 * PAIR].astype(f32))
         gains[0:8, :] = turned[0:8]
         gains[8:16, :] = turned[HEAD_DIM : HEAD_DIM + 8]
-    lane = lax.broadcasted_iota(jnp.int32, (ROW_BLOCK, PAIR), 1)
+    lane = lax.broadcasted_iota(jnp.int32, (PREP_BLOCK, PAIR), 1)
     low_head = lane < HEAD_DIM
     in_first = (lane & (HEAD_DIM - 1)) < HEAD_DIM // 2
-    zero = jnp.zeros((ROW_BLOCK, PAIR), bf16)
-
-    @pl.loop(0, length // ROW_BLOCK)
+    zero = jnp.zeros((PREP_BLOCK, PAIR), bf16)
+
+    @pl.loop(0, length // PREP_BLOCK)
     def _(b):
-        rows = pl.ds(pl.multiple_of(b * ROW_BLOCK, ROW_BLOCK), ROW_BLOCK)
+        rows = pl.ds(pl.multiple_of(b * PREP_BLOCK, PREP_BLOCK), PREP_BLOCK)
         if first:
             normed, _ = norm_stats(src[rows, :].astype(f32))
             a = (normed * gains[0:1, :]).astype(bf16)
@@ -345,7 +341,7 @@
             a = src[rows, :]
         qkv = jnp.dot(a, w[:, at : at + 3 * PAIR], preferred_element_type=f32)
         cos, sin = rotary_block(table, turns, b)
-        query_mask, key_mask = mask_features(bounds, b * ROW_BLOCK, ROW_BLOCK)
+        query_mask, key_mask = mask_features(bounds, b * PREP_BLOCK, PREP_BLOCK)
         query_mask, key_mask = query_mask.astype(bf16), key_mask.astype(bf16)
         u = qkv[:, :PAIR]
         q = (u * cos + half_swap(u, in_first) * sin).astype(bf16)
@@ -365,7 +361,7 @@
             kx[h, rows, :PAIR] = k
             kx[h, rows, PAIR:] = jnp.where(mine, k, key_mask)
         vx[rows, :PAIR] = v
-        vx[rows, PAIR:] = jnp.ones((ROW_BLOCK, PAIR), bf16)
+        vx[rows, PAIR:] = jnp.ones((PREP_BLOCK, PAIR), bf16)
 
     lane_q = lax.broadcasted_iota(jnp.int32, (FWD_BQ, PAIR), 1) < HEAD_DIM
 
@@ -401,11 +397,12 @@
     pieces = isinstance(parts, list)
     operands = parts if pieces else [parts]
     if pieces:
-        outs = [shape((width, parts[0].shape[-1]), bf16)] + outs
+        placed = (width,) if len(parts) == 1 else (parts[0].shape[0], len(parts), parts[0].shape[1])
+        outs = [shape(placed + (parts[0].shape[-1],), bf16)] + outs
     if first:
         outs = [shape((length, width), bf16), shape((16, width), f32)] + outs
     kernel = functools.partial(forward_kernel, first, len(parts) if pieces else 0, at)
-    return pl.pallas_call(
+    made = pl.pallas_call(
         passing(kernel, 4 + len(operands), len(deps)),
         out_shape=tuple(outs),
         in_specs=[smem(), vmem(), vmem(), vmem()]
@@ -416,12 +413,17 @@
             pltpu.VMEM((2, length, 2 * PAIR), bf16),
             pltpu.VMEM((2, length, 2 * PAIR), bf16),
             pltpu.VMEM((length, 2 * PAIR), bf16),
-            pltpu.SemaphoreType.DMA((2, 16)),
+            pltpu.SemaphoreType.DMA((2, 4)),
         ],
         compiler_params=params(FWD_MIB),
         cost_estimate=lasts(18),
         name="attention_forward_first" if first else "attention_forward",
     )(scal, src, *tables, *operands, *deps)
+    made = list(made)
+    if pieces:
+        number = 2 if first else 0
+        made[number] = made[number].reshape(width, -1)
+    return made
 
 
 def backward_kernel(part_count, carried, *refs):
@@ -436,18 +438,18 @@
     starts = document_starts(scal, length)
     bounds = lane_bounds(starts, live, length)
     halves = ((near, core), (far, 1 - core))
-    lane = lax.broadcasted_iota(jnp.int32, (ROW_BLOCK, PAIR), 1)
+    lane = lax.broadcasted_iota(jnp.int32, (PREP_BLOCK, PAIR), 1)
     in_head = lane & (HEAD_DIM - 1)
     low_head = lane < HEAD_DIM
     in_first = in_head < HEAD_DIM // 2
-    zero = jnp.zeros((ROW_BLOCK, PAIR), bf16)
-    minus = jnp.full((ROW_BLOCK, PAIR), -1, bf16)
+    zero = jnp.zeros((PREP_BLOCK, PAIR), bf16)
+    minus = jnp.full((PREP_BLOCK, PAIR), -1, bf16)
 
     def prepare(source, at, b):
-        first = pl.multiple_of(at * half + b * ROW_BLOCK, ROW_BLOCK)
-        rows = pl.ds(first, ROW_BLOCK)
-        grad = jnp.dot(source[pl.ds(pl.multiple_of(b * ROW_BLOCK, ROW_BLOCK), ROW_BLOCK), :], w[...], preferred_element_type=f32).astype(bf16)
-        query_mask, key_mask = mask_features(bounds, first, ROW_BLOCK)
+        first = pl.multiple_of(at * half + b * PREP_BLOCK, PREP_BLOCK)
+        rows = pl.ds(first, PREP_BLOCK)
+        grad = jnp.dot(source[pl.ds(pl.multiple_of(b * PREP_BLOCK, PREP_BLOCK), PREP_BLOCK), :], w[...], preferred_element_type=f32).astype(bf16)
+        query_mask, key_mask = mask_features(bounds, first, PREP_BLOCK)
         q, k = q_in[rows, :], k_in[rows, :]
         scaled = q.astype(f32) * LOG2_SCALE
         high = scaled.astype(bf16)
@@ -468,19 +470,19 @@
             km[h, rows, :] = jnp.where(mine, k, zero)
             dx[h, rows, :PAIR] = jnp.where(mine, grad, zero)
             delta = jnp.sum(jnp.where(mine, inner, 0.0), axis=1, keepdims=True)
-            da, db, dc = split3(jnp.broadcast_to(delta, (ROW_BLOCK, PAIR)))
+            da, db, dc = split3(jnp.broadcast_to(delta, (PREP_BLOCK, PAIR)))
             dx[h, rows, PAIR:] = jnp.where(
                 lane == 0, da, jnp.where(lane == 1, db, jnp.where(lane == 2, dc, zero))
             )
         vx[rows, :PAIR] = v_in[rows, :]
         vx[rows, PAIR:] = jnp.where(lane < 3, minus, zero)
-        dq[rows, :] = jnp.zeros((ROW_BLOCK, PAIR), f32)
-        dk[rows, :] = jnp.zeros((ROW_BLOCK, PAIR), f32)
-        dv[rows, :] = jnp.zeros((ROW_BLOCK, PAIR), f32)
+        dq[rows, :] = jnp.zeros((PREP_BLOCK, PAIR), f32)
+        dk[rows, :] = jnp.zeros((PREP_BLOCK, PAIR), f32)
+        dv[rows, :] = jnp.zeros((PREP_BLOCK, PAIR), f32)
 
     for source, at in halves:
 
-        @pl.loop(0, half // ROW_BLOCK)
+        @pl.loop(0, half // PREP_BLOCK)
         def _(b):
             prepare(source, at, b)
 
@@ -504,9 +506,9 @@
 
     each_key_chunk(starts, live, length, BWD_BQ, BWD_STEP, BWD_CHUNK, work)
 
-    @pl.loop(0, length // ROW_BLOCK)
+    @pl.loop(0, length // PREP_BLOCK)
     def _(b):
-        rows = pl.ds(pl.multiple_of(b * ROW_BLOCK, ROW_BLOCK), ROW_BLOCK)
+        rows = pl.ds(pl.multiple_of(b * PREP_BLOCK, PREP_BLOCK), PREP_BLOCK)
         cos, sin = rotary_block(table, turns, b)
         u = dq[rows, :] * SCORE_SCALE
         dqkv[rows, :PAIR] = (u * cos - half_swap(u, in_first) * sin).astype(bf16)
@@ -514,9 +516,10 @@
         dqkv[rows, PAIR : 2 * PAIR] = (u * cos - half_swap(u, in_first) * sin).astype(bf16)
         dqkv[rows, 2 * PAIR :] = dv[rows, :].astype(bf16)
 
+    grad_sums = grads if len(grads.shape) == 2 else grads.reshape(width, grads.shape[-1])
     for m in range(width // ROW_BLOCK):
         part = slice(m * ROW_BLOCK, (m + 1) * ROW_BLOCK)
-        grads[part, : 3 * PAIR] = lax.dot_general(
+        grad_sums[part, : 3 * PAIR] = lax.dot_general(
             a1[:, part], dqkv[...], TN, preferred_element_type=f32
         ).astype(bf16)
         total = None
@@ -524,26 +527,18 @@
             rows = pl.ds(pl.multiple_of(at * half, half), half)
             term = lax.dot_general(source[:, part], o_in[rows, :], TN, preferred_element_type=f32)
             total = term if total is None else total + term
-        grads[part, 3 * PAIR :] = total.astype(bf16)
+        grad_sums[part, 3 * PAIR :] = total.astype(bf16)
     made = [*before, grads]
-    cols = grads.shape[1]
+    cols = grads.shape[-1]
     stores = []
     for n, one in enumerate(made):
         at = slice(n * cols, (n + 1) * cols)
         if part_count == 1:
-            stores.append(pltpu.make_async_copy(one, parts[0].at[:, at], sems.at[n, 0]))
+            stores.append(pltpu.make_async_copy(one, parts[0], sems.at[n, 0]))
             continue
-        rows_each = parts[0].shape[1]
-        for h in range(parts[0].shape[0]):
-            for j in range(part_count):
-                own = jnp.bitwise_xor(me, h * part_count + j)
-                stores.append(
-                    pltpu.make_async_copy(
-                        one.at[pl.ds(pl.multiple_of(own * rows_each, 16), rows_each)],
-                        parts[j].at[h, :, at],
-                        sems.at[n, h * part_count + j],
-                    )
-                )
+        for j in range(part_count):
+            low = jnp.bitwise_xor(me & (part_count - 1), j)
+            stores.append(pltpu.make_async_copy(one.at[:, low], parts[j].at[:, :, at], sems.at[n, j]))
     for copy in stores:
         copy.start()
     for copy in stores:
@@ -554,6 +549,11 @@
     length, width = a1.shape
     shape = jax.ShapeDtypeStruct
     outs = [shape((length, 3 * PAIR), bf16)] + [shape(s, bf16) for s in part_shapes]
+    grads_shape = (width, 4 * PAIR)
+    if len(part_shapes) > 1:
+        high, rows_each, _ = part_shapes[0]
+        grads_shape = (high, len(part_shapes), rows_each, 4 * PAIR)
+        before = [x.reshape(grads_shape) for x in before]
     return pl.pallas_call(
         passing(functools.partial(backward_kernel, len(part_shapes), len(before)), 12 + len(before), len(deps)),
         out_shape=tuple(outs),
@@ -569,8 +569,8 @@
             pltpu.VMEM((length, PAIR), f32),
             pltpu.VMEM((length, PAIR), f32),
             pltpu.VMEM((length, PAIR), f32),
-            pltpu.VMEM((width, 4 * PAIR), bf16),
-            pltpu.SemaphoreType.DMA((len(before) + 1, 16)),
+            pltpu.VMEM(grads_shape, bf16),
+            pltpu.SemaphoreType.DMA((len(before) + 1, len(part_shapes))),
         ],
         compiler_params=params(BWD_MIB),
         cost_estimate=lasts(30),
@@ -694,45 +694,43 @@
     tokens, far, cot, gains = refs[2 * count : 2 * count + 4]
     sources = refs[2 * count + 4 : -9]
     result, dattn, grad_hidden, z_all, pair_all, a2_all, dff_all, ffn_w, sems = refs[-9:]
-    width, ff = ffn_w.shape[1:]
+    width, ff = result.shape[1], z_all.shape[1]
     live, me, core = scal[0], scal[1], scal[2]
     step = pl.program_id(0)
     block = result.shape[0]
 
+    def loads():
+        if part_count == 1:
+            return [
+                pltpu.make_async_copy(sources[0], ffn_w.at[pl.ds(0, 2)], sems.at[0]),
+                pltpu.make_async_copy(sources[1], ffn_w.at[2], sems.at[1]),
+            ]
+        copies = []
+        offset = ff - down_cols
+        near_at = pl.multiple_of(core * offset, PAIR)
+        far_from = pl.multiple_of(ff + (1 - core) * (down_cols - offset), PAIR)
+        far_at = pl.multiple_of((1 - core) * down_cols, PAIR)
+        for j in range(part_count):
+            low = jnp.bitwise_xor(me & (part_count - 1), j)
+            mine, other = sources[j], sources[part_count + j]
+            copies += [
+                pltpu.make_async_copy(mine.at[:, :, :ff], ffn_w.at[core, :, low], sems.at[4 * j]),
+                pltpu.make_async_copy(other.at[:, :, :ff], ffn_w.at[1 - core, :, low], sems.at[4 * j + 1]),
+                pltpu.make_async_copy(
+                    mine.at[:, :, ff:], ffn_w.at[2, :, low, :, pl.ds(near_at, down_cols)], sems.at[4 * j + 2]
+                ),
+                pltpu.make_async_copy(
+                    other.at[:, :, pl.ds(far_from, offset)],
+                    ffn_w.at[2, :, low, :, pl.ds(far_at, offset)],
+                    sems.at[4 * j + 3],
+                ),
+            ]
+        return copies
+
     @pl.when(step == 0)
     def _():
-        copies = []
-        if part_count == 1:
-            copies.append(pltpu.make_async_copy(sources[0], ffn_w.at[pl.ds(0, 2)], sems.at[0]))
-            copies.append(pltpu.make_async_copy(sources[1], ffn_w.at[2], sems.at[1]))
-        else:
-            offset = ff - down_cols
-            rows_each = sources[0].shape[1]
-            near_at = pl.multiple_of(core * offset, PAIR)
-            far_from = pl.multiple_of(ff + (1 - core) * (down_cols - offset), PAIR)
-            far_at = pl.multiple_of((1 - core) * down_cols, PAIR)
-            for h in range(sources[0].shape[0]):
-                for j in range(part_count):
-                    own = jnp.bitwise_xor(me, h * part_count + j)
-                    at = pl.ds(pl.multiple_of(own * rows_each, 16), rows_each)
-                    number = 4 * (h * part_count + j)
-                    mine, other = sources[j].at[h], sources[part_count + j].at[h]
-                    copies += [
-                        pltpu.make_async_copy(mine.at[:, :ff], ffn_w.at[core, at], sems.at[number]),
-                        pltpu.make_async_copy(other.at[:, :ff], ffn_w.at[1 - core, at], sems.at[number + 1]),
-                        pltpu.make_async_copy(
-                            mine.at[:, ff:], ffn_w.at[2, at, pl.ds(near_at, down_cols)], sems.at[number + 2]
-                        ),
-                        pltpu.make_async_copy(
-                            other.at[:, pl.ds(far_from, offset)],
-                            ffn_w.at[2, at, pl.ds(far_at, offset)],
-                            sems.at[number + 3],
-                        ),
-                    ]
-        for copy in copies:
+        for copy in loads():
             copy.start()
-        for copy in copies:
-            copy.wait()
 
     here = core * (block * pl.num_programs(0)) + step * block
     position = here + lax.broadcasted_iota(jnp.int32, (block, 1), 0)
@@ -744,22 +742,29 @@
     normed, inv = norm_stats(hidden)
     gain = gains[8:9, :]
     a2 = (normed * gain).astype(bf16)
-    up = jnp.dot(a2, ffn_w[0], preferred_element_type=f32)
-    gate = jnp.dot(a2, ffn_w[1], preferred_element_type=f32)
+
+    @pl.when(step == 0)
+    def _():
+        for copy in loads():
+            copy.wait()
+
+    weights_in = ffn_w.reshape(3, width, ff) if part_count > 1 else ffn_w
+    up = jnp.dot(a2, weights_in[0], preferred_element_type=f32)
+    gate = jnp.dot(a2, weights_in[1], preferred_element_type=f32)
     below = 0.5 * (1.0 + lax.erf(up * math.sqrt(0.5)))
     act = up * below
     slope = below + up * jnp.exp(up * up * -0.5) * (1.0 / math.sqrt(2.0 * math.pi))
     z = (act * gate).astype(bf16)
     result[...] = (
-        hidden + valid * lax.dot_general(z, ffn_w[2], NT, preferred_element_type=f32)
+        hidden + valid * lax.dot_general(z, weights_in[2], NT, preferred_element_type=f32)
     ).astype(bf16)
     dy = cot[...].astype(f32)
     dff = (valid * dy).astype(bf16)
-    dz = jnp.dot(dff, ffn_w[2], preferred_element_type=f32)
+    dz = jnp.dot(dff, weights_in[2], preferred_element_type=f32)
     du = (dz * gate * slope).astype(bf16)
     dg = (dz * act).astype(bf16)
-    da2 = lax.dot_general(du, ffn_w[0], NT, preferred_element_type=f32) + lax.dot_general(
-        dg, ffn_w[1], NT, preferred_element_type=f32
+    da2 = lax.dot_general(du, weights_in[0], NT, preferred_element_type=f32) + lax.dot_general(
+        dg, weights_in[1], NT, preferred_element_type=f32
     )
     grad = dy + norm_back(da2 * gain, normed, inv)
     grad_hidden[...] = grad
@@ -813,6 +818,9 @@
 def feed_forward(scal, outs_of, weights, tokens, far, cot, gains, sources, ff, down_cols):
     length, width = tokens.shape
     part_count = len(sources) // 2
+    placed = (3, width, ff)
+    if part_count > 1:
+        placed = (3, sources[0].shape[0], part_count, sources[0].shape[1], ff)
     half = length // 2
     blocks = half // ROW_BLOCK
     shape = jax.ShapeDtypeStruct
@@ -846,7 +854,7 @@
                 plain(width),
                 plain(width),
             ),
-            scratch_shapes=[pltpu.VMEM((3, width, ff), bf16), pltpu.SemaphoreType.DMA((64,))],
+            scratch_shapes=[pltpu.VMEM(placed, bf16), pltpu.SemaphoreType.DMA((16,))],
         ),
         compiler_params=params(FFN_MIB),
         cost_estimate=lasts(25),
@@ -858,7 +866,7 @@
     me = scal[1]
     for j in range(wide):
         for h in range(outs[0].shape[0]):
-            own = jnp.bitwise_xor(me, h * wide + j)
+            own = h * wide + jnp.bitwise_xor(me & (wide - 1), j)
             outs[j][h] = (keep[own].astype(f32) + got[own].astype(f32)).astype(bf16)
 
 
@@ -887,7 +895,7 @@
         angles = positions[:, None] * freqs[None, :]
         return jnp.asarray(np.stack([np.cos(angles), np.sin(angles) * sign]), f32)
 
-    return both(np.arange(ROW_BLOCK)), both(np.arange(0, length, ROW_BLOCK))
+    return both(np.arange(PREP_BLOCK)), both(np.arange(0, length, PREP_BLOCK))
 
 
 def local(tokens, segment_ids, counts, w_qkv, w_out, w_in, w_down, ln1_gain, ln2_gain, cotangent):
@@ -919,20 +927,21 @@
     if fast:
         high_bits, low_bits = bit_groups(count)
         head_high = gather_step(head_load[None], count, high_bits)
-        rest_load = stack_parts([rest_load[None]], head_high[1:])
-        head_parts = gather_step(stack_parts(head_high), count, low_bits)
+        at = (dp >> low_bits[1]).astype(jnp.int32)[None]
+        rest_load = stack_parts(at, [rest_load[None]], head_high[1:])
+        head_parts = gather_step(stack_parts(at, head_high), count, low_bits)
         rest_high = gather_step(rest_load, count, high_bits)
-        rest_all = stack_parts(rest_high, head_parts[1:])
+        rest_all = stack_parts(at, rest_high, head_parts[1:])
         zero_one = jnp.concatenate([w_in[0], down_turned[:, :down_cols]], axis=1)
         one_two = jnp.concatenate([w_in[1], down_turned[:, offset:]], axis=1)
         ffn_load = join(pick(zero_one, one_two), core_swap(pick(one_two, zero_one)))
-        ffn_load = stack_parts([ffn_load[None]], rest_high[1:])
+        ffn_load = stack_parts(at, [ffn_load[None]], rest_high[1:])
         ffn_high = gather_step(ffn_load, count, high_bits)
         a1, gains, *kept = forward_pair(
             True, scal, row, tables, head_parts, 0, [rest_all, ffn_load]
         )
         rest_parts = gather_step(rest_all, count, low_bits)
-        ffn_all = stack_parts(ffn_high, [a1])
+        ffn_all = stack_parts(at, ffn_high, [a1])
         ffn_parts = gather_step(ffn_all, count, low_bits)
         sources = ffn_parts + [core_swap(p) for p in ffn_parts]
         deps, late_deps = [ffn_all], ffn_parts[1:]
@@ -983,18 +992,16 @@
             )
             dqkv.append(one)
             before += parts
-            if i == 0:
-                pieces = sum_parts(ffn_near, [one])
-                deps = pieces
+        pieces = sum_parts(at, ffn_near, [one])
         done = reduce_far(pieces, count, wide)
         early_near = reduce_near(parts, count)
-        one, *parts = backward(pairs - 1, parts_of(1), (), [done])
+        one, *parts = backward(pairs - 1, parts_of(1), (), pieces)
         dqkv.append(one)
         late_near = reduce_near(parts, count)
-        pieces = sum_parts(early_near, [one])
+        pieces = sum_parts(at, early_near, [one])
         early = far_pieces(pieces, count, wide)
         far_da = project_far_half(scal, dqkv, qkv_w, pieces)
-        pieces = sum_parts(late_near, [far_da])
+        pieces = sum_parts(at, late_near, pieces)
         shards = [early, far_pieces(pieces, count, wide)]
         far_da = core_swap(far_da)
         grad_tokens, mark = final_rows(scal, dqkv, qkv_w, row, far_da, grad_hidden, gains, pieces)

time: 261 us -> 249 us (0.954)
  waiting for transfers between devices: 41.1 us -> 24.4 us
  Pallas kernels: 125 us -> 130 us
    ppermute x36, waiting for transfers between devices: 33.7 us -> 17.1 us  [xor_permute(): return lax.ppermute(value, 'dp', [(i, i ^ mask) for i in range(count)])]
    pallas_call x3, Pallas kernels: 43.4 us -> 52.3 us  [backward_pair(): pl.pallas_call(passing(functools.partial(backward_kernel, len(part_shapes...]
  transfers between devices with their start and end apart: 48 -> 48, of which waited for: 15 -> 12; matrix products, arithmetic and copies ran while one was open for 2% -> 2% of each run, Pallas kernels for 37% -> 41%
where the time goes in v5:
time: 249 us; the launch traced here: 246 us
  Pallas kernels  130 us (52%)
  starting transfers between devices  79.5 us (32%)
  waiting for transfers between devices  24.4 us (10%)
  local copies, waits for them, and re-layouts  6.5 us (3%)
  other arithmetic  3.82 us (2%)
    ppermute x36, starting transfers between devices, xor_permute(): return lax.ppermute(value, 'dp', [(i, i ^ mask) for i in range(count)])  76.6 us
    pallas_call x3, Pallas kernels, backward_pair(): pl.pallas_call(passing(functools.partial(backward_kernel, len(part_shapes...  52.3 us
    pallas_call x3, Pallas kernels, forward_pair(): pl.pallas_call(passing(kernel, 4 + len(operands), len(deps)), out_shape=t...  32.4 us
    pallas_call x1, Pallas kernels, feed_forward(): pl.pallas_call(functools.partial(ffn_kernel, len(outs_of), part_count, do...  21.9 us
    ppermute x36, waiting for transfers between devices, xor_permute(): return lax.ppermute(value, 'dp', [(i, i ^ mask) for i in range(count)])  17.1 us
    pallas_call x2, Pallas kernels, weight_grads(): pl.pallas_call(passing(functools.partial(weight_grad_kernel, split, own,...  8.09 us
    ppermute x12, waiting for transfers between devices, core_swap(): return lax.ppermute(value, 'head', [(0, 1), (1, 0)])  7.28 us
    pallas_call x2, Pallas kernels, project_far_half(): pl.pallas_call(passing(functools.partial(project_kernel, count), 1 + 2 *...  6.57 us
  transfers between devices with their start and end apart: 48, of which 12 were waited for; matrix products, arithmetic and copies ran while one was open for 2% of the time, Pallas kernels for 41%

profile of v5, /device:TPU:0, one launch (start us, length us, event | category | flops | bytes accessed | tf_op | source)
XLA Modules:
  0.0 246.4 jit_solution(6272589027759582816)
XLA Ops:
  5.3 2.6 %collective-permute-start.1 = (bf16[1,48,512]{2,1,0:T(8,128)(2,1)S(1)}, bf16[1,48,512]{2,1,0:T(8,128)(2,1)S(1)}, u32[]{:S(2)}, u32[]{:S(2)}) collective-permute-start(bf16[1,48,512]{2,1,0:T(8,128)(2,1)S(1)} %bitcast.53), channel_id=1, source_target_pairs={{0,8},{2,10},{4,12},{6,14},{8,0},{10,2},{12,4},{14,6},{16,24},{18,... | collective-permute-start | bytes 147464 | tf_op jit(solution)/shard_map/ppermute | solution.py:73
  7.9 2.6 %collective-permute-start.2 = (bf16[1,48,512]{2,1,0:T(8,128)(2,1)S(1)}, bf16[1,48,512]{2,1,0:T(8,128)(2,1)S(1)}, u32[]{:S(2)}, u32[]{:S(2)}) collective-permute-start(bf16[1,48,512]{2,1,0:T(8,128)(2,1)S(1)} %bitcast.54), channel_id=1, source_target_pairs={{0,16},{2,18},{4,20},{6,22},{8,24},{10,26},{12,28},{14,30},{16,0},... | collective-permute-start | bytes 147464 | tf_op jit(solution)/shard_map/ppermute | solution.py:73
  11.3 2.8 %collective-permute-done.2.refs_3_ = bf16[1,48,512]{2,1,0:T(8,128)(2,1)S(1)} collective-permute-done((bf16[1,48,512]{2,1,0:T(8,128)(2,1)S(1)}, bf16[1,48,512]{2,1,0:T(8,128)(2,1)S(1)}, u32[]{:S(2)}, u32[]{:S(2)}) %collective-permute-start.2) | collective-permute-done | bytes 49184 | tf_op jit(solution)/shard_map/ppermute | solution.py:73
  24.5 5.4 %collective-permute-done.8.refs_3_ = bf16[1,48,1152]{2,1,0:T(8,128)(2,1)S(1)} collective-permute-done((bf16[1,48,1152]{2,1,0:T(8,128)(2,1)S(1)}, bf16[1,48,1152]{2,1,0:T(8,128)(2,1)S(1)}, u32[]{:S(2)}, u32[]{:S(2)}) %collective-permute-start.8) | collective-permute-done | bytes 110624 | tf_op jit(solution)/shard_map/ppermute | solution.py:73
  40.5 9.9 %attention_forward_first.1 = (bf16[2048,768]{1,0:T(8,128)(2,1)S(1)}, f32[16,768]{1,0:T(8,128)S(1)}, bf16[4,4,48,512]{3,2,1,0:T(8,128)(2,1)S(1)}, bf16[2048,128]{...) custom-call(s32[6]{0:T(128)S(1)} %pad_add_fusion.refs_0_.scal, ...), custom_call_target="tpu_custom_call" | custom-call | flops 1800000000 | tf_op jit(solution)/shard_map/attention_forward_first/pallas_call | solution.py:405
  55.3 3.0 %collective-permute-done.12.refs_6_ = bf16[4,48,1152]{2,1,0:T(8,128)(2,1)S(1)} collective-permute-done((bf16[4,48,1152]{2,1,0:T(8,128)(2,1)S(1)}, bf16[4,48,1152]{2,1,0:T(8,128)(2,1)S(1)}, u32[]{:S(2)}, u32[]{:S(2)}) %collective-permute-start.12) | collective-permute-done | bytes 442400 | tf_op jit(solution)/shard_map/ppermute | solution.py:73
  58.3 8.6 %attention_forward.2 = (bf16[4,4,48,1152]{3,2,1,0:T(8,128)(2,1)S(1)}, bf16[2048,128]{1,0:T(8,128)(2,1)S(1)}, bf16[2048,128]{1,0:T(8,128)(2,1)S(1)}, bf16[2048,12...) custom-call(s32[6]{0:T(128)S(1)} %pad_add_fusion.refs_0_.scal, ...), custom_call_target="tpu_custom_call" | custom-call | flops 1800000000 | tf_op jit(solution)/shard_map/attention_forward/pallas_call | solution.py:405
  67.7 13.9 %attention_forward.3 = (bf16[2048,128]{1,0:T(8,128)(2,1)S(1)}, bf16[2048,128]{1,0:T(8,128)(2,1)S(1)}, bf16[2048,128]{1,0:T(8,128)(2,1)S(1)}, bf16[2048,128]{1,0:T(8,128)(2,1)S(1)}, f32[2048,128]{1,0:T(8,128)S(1)}) custom-call(s32[6]{0:T(128)S(1)} %pad_add_fusion.refs_0_.scal, bf16[2048,768]{1,0:T(8,128)(2,1)S(1)} %get-tuple-element.72.refs_5_.refs_1_, ...), custom_call_target="tpu_custom_call" | custom-call | flops 1800000000 | tf_op jit(solution)/shard_map/attention_forward/pallas_call | solution.py:405
  84.9 2.6 %project_far_half.2 = bf16[1024,768]{1,0:T(8,128)(2,1)S(1)} custom-call(s32[6]{0:T(128)S(1)} %pad_add_fusion.refs_0_.scal, bf16[2048,128]{1,0:T(8,128)(2,1)S(1)} %get-tuple-element.71.refs_1_.refs_0_.refs_8_, bf16[2048,128]{1,0:T(8,128)(2,1)S(1)} %get-tuple-element.73.refs_2_.refs_1_.refs_8_, ...), custom_call_target="tpu_custom_call" | custom-call | flops 400000000 | tf_op jit(solution)/shard_map/project_far_half/pallas_call | solution.py:599
  88.7 3.3 %collective-permute-done.21.refs_14_ = bf16[4,48,1792]{2,1,0:T(8,128)(2,1)S(1)} collective-permute-done((bf16[4,48,1792]{2,1,0:T(8,128)(2,1)S(1)}, bf16[4,48,1792]{2,1,0:T(8,128)(2,1)S(1)}, u32[]{:S(2)}, u32[]{:S(2)}) %collective-permute-start.21) | collective-permute-done | bytes 688160 | tf_op jit(solution)/shard_map/ppermute | solution.py:77
  95.0 21.9 %feed_forward.1 = (bf16[1024,768]{1,0:T(8,128)(2,1)}, bf16[1024,768]{1,0:T(8,128)(2,1)S(1)}, f32[1024,768]{1,0:T(8,128)S(1)}, bf16[1024,1152]{1,0:T(8,128)(2,1)S...) custom-call(s32[6]{0:T(128)S(1)} %pad_add_fusion.refs_0_.scal, ...), custom_call_target="tpu_custom_call" | custom-call | flops 2500000000 | tf_op jit(solution)/shard_map/feed_forward/pallas_call | solution.py:830
  116.8 4.1 %weight_grads.3 = bf16[768,1792]{1,0:T(8,128)(2,1)S(1)} custom-call(s32[6]{0:T(128)S(1)} %pad_add_fusion.refs_0_.scal, bf16[1024,1152]{1,0:T(8,128)(2,1)S(1)} %get-tuple-element.83.refs_1_, bf16[2,1024,1152]{2,1,0:T(8,128)(2,1)S(1)} %get-tuple-element.84.refs_2_, bf16[1024,768]{1,0:T(8,128)(2,1)S(1)} %get-tuple-element.85.refs_3_, ...), custom_call_target="tpu_custom_call" | custom-call | flops 500000000 | tf_op jit(solution)/shard_map/weight_grads/pallas_call | solution.py:807
  121.6 4.0 %weight_grads.2 = bf16[768,1792]{1,0:T(8,128)(2,1)S(1)} custom-call(s32[6]{0:T(128)S(1)} %pad_add_fusion.refs_0_.scal, bf16[1024,1152]{1,0:T(8,128)(2,1)S(1)} %get-tuple-element.83.refs_1_, bf16[2,1024,1152]{2,1,0:T(8,128)(2,1)S(1)} %get-tuple-element.84.refs_2_, bf16[1024,768]{1,0:T(8,128)(2,1)S(1)} %get-tuple-element.85.refs_3_, ...), custom_call_target="tpu_custom_call" | custom-call | flops 500000000 | tf_op jit(solution)/shard_map/weight_grads/pallas_call | solution.py:807
  130.9 16.2 %attention_backward.3 = (bf16[2048,384]{1,0:T(8,128)(2,1)S(1)}, bf16[768,512]{1,0:T(8,128)(2,1)S(1)}) custom-call(s32[6]{0:T(128)S(1)} %pad_add_fusion.refs_0_.scal, bf16[2048,768]{1,0:T(8,128)(2,1)S(1)} %get-tuple-element.72.refs_5_.refs_1_, bf16[1024,768]{1,0:T(8,128)(2,1)S(1)} %get-tuple-element.78.refs_2_, ...), custom_call_target="tpu_custom_call" | custom-call | flops 3000000000 | tf_op jit(solution)/shard_map/attention_backward/pallas_call | solution.py:557
  147.1 19.7 %attention_backward.4 = (bf16[2048,384]{1,0:T(8,128)(2,1)S(1)}, bf16[4,48,1024]{2,1,0:T(8,128)(2,1)S(1)}, bf16[4,48,1024]{2,1,0:T(8,128)(2,1)S(1)}, bf16[4,48,10...) custom-call(s32[6]{0:T(128)S(1)} %pad_add_fusion.refs_0_.scal, bf16[2048,768]{1,0:T(8,128)(2,1)S(1)} %get-tuple-element.72.refs_5_.refs_1_, ...), custom_call_target="tpu_custom_call" | custom-call | flops 3000000000 | tf_op jit(solution)/shard_map/attention_backward/pallas_call | solution.py:557
  167.0 3.6 %collective-permute-start.31 = (bf16[4,48,1024]{2,1,0:T(8,128)(2,1)S(1)}, bf16[4,48,1024]{2,1,0:T(8,128)(2,1)S(1)}, u32[]{:S(2)}, u32[]{:S(2)}) collective-permute-start(bf16[4,48,1024]{2,1,0:T(8,128)(2,1)S(1)} %get-tuple-element.110), channel_id=1, source_target_pairs={{0,4},{2,6},{4,0},{6,2},{8,12},{10,14},{12,8},{14,10},{16,20},{18,... | collective-permute-start | bytes 1179656 | tf_op jit(solution)/shard_map/ppermute | solution.py:73
  171.2 6.8 %collective-permute-start.43 = (bf16[48,1792]{1,0:T(8,128)(2,1)S(1)}, bf16[48,1792]{1,0:T(8,128)(2,1)S(1)}, u32[]{:S(2)}, u32[]{:S(2)}) collective-permute-start(bf16[48,1792]{1,0:T(8,128)(2,1)S(1)} %get-tuple-element.103.refs_13_), channel_id=1, source_target_pairs={{0,8},{2,10},{4,12},{6,14},{8,0},{10,2},{12,4},{14,6},{16,24},{18,... | collective-permute-start | bytes 516104 | tf_op jit(solution)/shard_map/ppermute | solution.py:73
  178.0 11.7 %collective-permute-start.44 = (bf16[48,1792]{1,0:T(8,128)(2,1)S(1)}, bf16[48,1792]{1,0:T(8,128)(2,1)S(1)}, u32[]{:S(2)}, u32[]{:S(2)}) collective-permute-start(bf16[48,1792]{1,0:T(8,128)(2,1)S(1)} %get-tuple-element.104.refs_14_), channel_id=1, source_target_pairs={{0,16},{2,18},{4,20},{6,22},{8,24},{10,26},{12,28},{14,30},{16,0},... | collective-permute-start | bytes 516104 | tf_op jit(solution)/shard_map/ppermute | solution.py:73
  191.1 16.3 %attention_backward.5 = (bf16[2048,384]{1,0:T(8,128)(2,1)S(1)}, bf16[4,48,512]{2,1,0:T(8,128)(2,1)S(1)}, bf16[4,48,512]{2,1,0:T(8,128)(2,1)S(1)}, bf16[4,48,512]{2,1,0:T(8,128)(2,1)S(1)}, bf16[4,48,512]{2,1,0:T(8,128)(2,1)S(1)}) custom-call(s32[6]{0:T(128)S(1)} %pad_add_fusion.refs_0_.scal, bf16[2048,768]{1,0:T(8,128)(2,1)S(1)} %get-tuple-element.72.refs_5_.refs_1_, ...), custom_call_target="tpu_custom_call" | custom-call | flops 3000000000 | tf_op jit(solution)/shard_map/attention_backward/pallas_call | solution.py:557
  207.5 4.4 %collective-permute-start.35 = (bf16[4,48,512]{2,1,0:T(8,128)(2,1)S(1)}, bf16[4,48,512]{2,1,0:T(8,128)(2,1)S(1)}, u32[]{:S(2)}, u32[]{:S(2)}) collective-permute-start(bf16[4,48,512]{2,1,0:T(8,128)(2,1)S(1)} %get-tuple-element.119), channel_id=1, source_target_pairs={{0,4},{2,6},{4,0},{6,2},{8,12},{10,14},{12,8},{14,10},{16,20},{18,... | collective-permute-start | bytes 589832 | tf_op jit(solution)/shard_map/ppermute | solution.py:73
  212.1 4.0 %project_far_half.3 = bf16[1024,768]{1,0:T(8,128)(2,1)S(1)} custom-call(s32[6]{0:T(128)S(1)} %pad_add_fusion.refs_0_.scal, bf16[2048,384]{1,0:T(8,128)(2,1)S(1)} %get-tuple-element.91.refs_1_, bf16[2048,384]{1,0:T(8,128)(2,1)S(1)} %get-tuple-element.97.refs_5_.refs_2_, bf16[2048,384]{1,0:T(8,128)(2,1)S(1)} %get-tuple-element.106.refs_5_.refs_3_, ...), custom_call_target="tpu_custom_call" | custom-call | flops 400000000 | tf_op jit(solution)/shard_map/project_far_half/pallas_call | solution.py:599
  217.9 7.0 %collective-permute-start.37 = (bf16[48,1024]{1,0:T(8,128)(2,1)S(1)}, bf16[48,1024]{1,0:T(8,128)(2,1)S(1)}, u32[]{:S(2)}, u32[]{:S(2)}) collective-permute-start(bf16[48,1024]{1,0:T(8,128)(2,1)S(1)} %get-tuple-element.113.refs_8_.refs_6_), channel_id=1, source_target_pairs={{0,8},{2,10},{4,12},{6,14},{8,0},{10,2},{12,4},{14,6},{16,24},{18,... | collective-permute-start | bytes 294920 | tf_op jit(solution)/shard_map/ppermute | solution.py:73
  225.0 5.0 %collective-permute-start.38 = (bf16[48,1024]{1,0:T(8,128)(2,1)S(1)}, bf16[48,1024]{1,0:T(8,128)(2,1)S(1)}, u32[]{:S(2)}, u32[]{:S(2)}) collective-permute-start(bf16[48,1024]{1,0:T(8,128)(2,1)S(1)} %get-tuple-element.114.refs_9_.refs_7_), channel_id=1, source_target_pairs={{0,16},{2,18},{4,20},{6,22},{8,24},{10,26},{12,28},{14,30},{16,0},... | collective-permute-start | bytes 294920 | tf_op jit(solution)/shard_map/ppermute | solution.py:73
  237.5 6.0 %final_rows.1 = (f32[1024,768]{1,0:T(8,128)}, f32[8,128]{1,0:T(8,128)S(1)}) custom-call(s32[6]{0:T(128)S(1)} %pad_add_fusion.refs_0_.scal, bf16[2048,384]{1,0:T(8,128)(2,1)S(1)} %get-tuple-element.91.refs_1_, bf16[2048,384]{1,0:T(8,128)(2,1)S(1)} %get-tuple-element.97.refs_5_.refs_2_, bf16[2048,384]{1,0:T(8,128)(2,1)S(1)} %get-tuple-element.106.refs_5_.refs_3_, ...), custom_call_target="tpu_custom_call" | custom-call | flops 700000000 | tf_op jit(solution)/shard_map/final_rows/pallas_call | solution.py:634
  (186 shorter events, 58.8 us)
Async XLA Ops:
  30.0 24.3 %collective-permute-start.11 = (bf16[4,48,1152]{2,1,0:T(8,128)(2,1)S(1)}, bf16[4,48,1152]{2,1,0:T(8,128)(2,1)S(1)}, u32[]{:S(2)}, u32[]{:S(2)}) collective-permute-start(bf16[4,48,1152]{2,1,0:T(8,128)(2,1)S(1)} %stack_parts.7.refs_8_.refs_4_), channel_id=1, source_target_pairs={{0,2},{2,0},{4,6},{6,4},{8,10},{10,8},{12,14},{14,12},{16,18},{18,... | collective-permute-start | bytes 1327112 | tf_op jit(solution)/shard_map/ppermute | solution.py:73
  33.6 16.9 %collective-permute-start.15 = (bf16[1,48,1792]{2,1,0:T(8,128)(2,1)S(1)}, bf16[1,48,1792]{2,1,0:T(8,128)(2,1)S(1)}, u32[]{:S(2)}, u32[]{:S(2)}) collective-permute-start(bf16[1,48,1792]{2,1,0:T(8,128)(2,1)S(1)} %stack_parts.8.refs_9_.refs_1_), channel_id=1, source_target_pairs={{0,16},{2,18},{4,20},{6,22},{8,24},{10,26},{12,28},{14,30},{16,0},... | collective-permute-start | bytes 516104 | tf_op jit(solution)/shard_map/ppermute | solution.py:73
  34.8 15.7 %collective-permute-start.16 = (bf16[1,48,1792]{2,1,0:T(8,128)(2,1)S(1)}, bf16[1,48,1792]{2,1,0:T(8,128)(2,1)S(1)}, u32[]{:S(2)}, u32[]{:S(2)}) collective-permute-start(bf16[1,48,1792]{2,1,0:T(8,128)(2,1)S(1)} %stack_parts.8.refs_9_.refs_1_), channel_id=1, source_target_pairs={{0,24},{2,26},{4,28},{6,30},{8,16},{10,18},{12,20},{14,22},{16,8},... | collective-permute-start | bytes 516104 | tf_op jit(solution)/shard_map/ppermute | solution.py:73
  36.4 21.9 %collective-permute-start.12 = (bf16[4,48,1152]{2,1,0:T(8,128)(2,1)S(1)}, bf16[4,48,1152]{2,1,0:T(8,128)(2,1)S(1)}, u32[]{:S(2)}, u32[]{:S(2)}) collective-permute-start(bf16[4,48,1152]{2,1,0:T(8,128)(2,1)S(1)} %stack_parts.7.refs_8_.refs_4_), channel_id=1, source_target_pairs={{0,4},{2,6},{4,0},{6,2},{8,12},{10,14},{12,8},{14,10},{16,20},{18,... | collective-permute-start | bytes 1327112 | tf_op jit(solution)/shard_map/ppermute | solution.py:73
  39.0 19.3 %collective-permute-start.13 = (bf16[4,48,1152]{2,1,0:T(8,128)(2,1)S(1)}, bf16[4,48,1152]{2,1,0:T(8,128)(2,1)S(1)}, u32[]{:S(2)}, u32[]{:S(2)}) collective-permute-start(bf16[4,48,1152]{2,1,0:T(8,128)(2,1)S(1)} %stack_parts.7.refs_8_.refs_4_), channel_id=1, source_target_pairs={{0,6},{2,4},{4,2},{6,0},{8,14},{10,12},{12,10},{14,8},{16,22},{18,... | collective-permute-start | bytes 1327112 | tf_op jit(solution)/shard_map/ppermute | solution.py:73
  51.8 30.7 %collective-permute-start.17 = (bf16[4,48,1792]{2,1,0:T(8,128)(2,1)S(1)}, bf16[4,48,1792]{2,1,0:T(8,128)(2,1)S(1)}, u32[]{:S(2)}, u32[]{:S(2)}) collective-permute-start(bf16[4,48,1792]{2,1,0:T(8,128)(2,1)S(1)} %stack_parts.9.refs_8_.refs_10_), channel_id=1, source_target_pairs={{0,2},{2,0},{4,6},{6,4},{8,10},{10,8},{12,14},{14,12},{16,18},{18,... | collective-permute-start | bytes 2064392 | tf_op jit(solution)/shard_map/ppermute | solution.py:73
  52.0 32.8 %collective-permute-start.18 = (bf16[4,48,1792]{2,1,0:T(8,128)(2,1)S(1)}, bf16[4,48,1792]{2,1,0:T(8,128)(2,1)S(1)}, u32[]{:S(2)}, u32[]{:S(2)}) collective-permute-start(bf16[4,48,1792]{2,1,0:T(8,128)(2,1)S(1)} %stack_parts.9.refs_8_.refs_10_), channel_id=1, source_target_pairs={{0,4},{2,6},{4,0},{6,2},{8,12},{10,14},{12,8},{14,10},{16,20},{18,... | collective-permute-start | bytes 2064392 | tf_op jit(solution)/shard_map/ppermute | solution.py:73
  54.3 30.6 %collective-permute-start.19 = (bf16[4,48,1792]{2,1,0:T(8,128)(2,1)S(1)}, bf16[4,48,1792]{2,1,0:T(8,128)(2,1)S(1)}, u32[]{:S(2)}, u32[]{:S(2)}) collective-permute-start(bf16[4,48,1792]{2,1,0:T(8,128)(2,1)S(1)} %stack_parts.9.refs_8_.refs_10_), channel_id=1, source_target_pairs={{0,6},{2,4},{4,2},{6,0},{8,14},{10,12},{12,10},{14,8},{16,22},{18,... | collective-permute-start | bytes 2064392 | tf_op jit(solution)/shard_map/ppermute | solution.py:73
  127.3 43.3 %collective-permute-start.27 = (bf16[4,48,1792]{2,1,0:T(8,128)(2,1)S(1)}, bf16[4,48,1792]{2,1,0:T(8,128)(2,1)S(1)}, u32[]{:S(2)}, u32[]{:S(2)}) collective-permute-start(bf16[4,48,1792]{2,1,0:T(8,128)(2,1)S(1)} %get-tuple-element.88.refs_13_.refs_14_), channel_id=1, source_target_pairs={{0,2},{2,0},{4,6},{6,4},{8,10},{10,8},{12,14},{14,12},{16,18},{18,... | collective-permute-start | bytes 2064392 | tf_op jit(solution)/shard_map/ppermute | solution.py:73
  127.9 42.9 %collective-permute-start.28 = (bf16[4,48,1792]{2,1,0:T(8,128)(2,1)S(1)}, bf16[4,48,1792]{2,1,0:T(8,128)(2,1)S(1)}, u32[]{:S(2)}, u32[]{:S(2)}) collective-permute-start(bf16[4,48,1792]{2,1,0:T(8,128)(2,1)S(1)} %get-tuple-element.89.refs_14_.refs_15_), channel_id=1, source_target_pairs={{0,4},{2,6},{4,0},{6,2},{8,12},{10,14},{12,8},{14,10},{16,20},{18,... | collective-permute-start | bytes 2064392 | tf_op jit(solution)/shard_map/ppermute | solution.py:73
  129.4 41.4 %collective-permute-start.29 = (bf16[4,48,1792]{2,1,0:T(8,128)(2,1)S(1)}, bf16[4,48,1792]{2,1,0:T(8,128)(2,1)S(1)}, u32[]{:S(2)}, u32[]{:S(2)}) collective-permute-start(bf16[4,48,1792]{2,1,0:T(8,128)(2,1)S(1)} %get-tuple-element.90.refs_15_.refs_16_), channel_id=1, source_target_pairs={{0,6},{2,4},{4,2},{6,0},{8,14},{10,12},{12,10},{14,8},{16,22},{18,... | collective-permute-start | bytes 2064392 | tf_op jit(solution)/shard_map/ppermute | solution.py:73
  166.9 22.8 %collective-permute-start.30 = (bf16[4,48,1024]{2,1,0:T(8,128)(2,1)S(1)}, bf16[4,48,1024]{2,1,0:T(8,128)(2,1)S(1)}, u32[]{:S(2)}, u32[]{:S(2)}) collective-permute-start(bf16[4,48,1024]{2,1,0:T(8,128)(2,1)S(1)} %get-tuple-element.109), channel_id=1, source_target_pairs={{0,2},{2,0},{4,6},{6,4},{8,10},{10,8},{12,14},{14,12},{16,18},{18,... | collective-permute-start | bytes 1179656 | tf_op jit(solution)/shard_map/ppermute | solution.py:73
  167.0 40.4 %collective-permute-start.31 = (bf16[4,48,1024]{2,1,0:T(8,128)(2,1)S(1)}, bf16[4,48,1024]{2,1,0:T(8,128)(2,1)S(1)}, u32[]{:S(2)}, u32[]{:S(2)}) collective-permute-start(bf16[4,48,1024]{2,1,0:T(8,128)(2,1)S(1)} %get-tuple-element.110), channel_id=1, source_target_pairs={{0,4},{2,6},{4,0},{6,2},{8,12},{10,14},{12,8},{14,10},{16,20},{18,... | collective-permute-start | bytes 1179656 | tf_op jit(solution)/shard_map/ppermute | solution.py:73
  170.6 36.9 %collective-permute-start.32 = (bf16[4,48,1024]{2,1,0:T(8,128)(2,1)S(1)}, bf16[4,48,1024]{2,1,0:T(8,128)(2,1)S(1)}, u32[]{:S(2)}, u32[]{:S(2)}) collective-permute-start(bf16[4,48,1024]{2,1,0:T(8,128)(2,1)S(1)} %get-tuple-element.111), channel_id=1, source_target_pairs={{0,6},{2,4},{4,2},{6,0},{8,14},{10,12},{12,10},{14,8},{16,22},{18,... | collective-permute-start | bytes 1179656 | tf_op jit(solution)/shard_map/ppermute | solution.py:73
  171.2 44.9 %collective-permute-start.43 = (bf16[48,1792]{1,0:T(8,128)(2,1)S(1)}, bf16[48,1792]{1,0:T(8,128)(2,1)S(1)}, u32[]{:S(2)}, u32[]{:S(2)}) collective-permute-start(bf16[48,1792]{1,0:T(8,128)(2,1)S(1)} %get-tuple-element.103.refs_13_), channel_id=1, source_target_pairs={{0,8},{2,10},{4,12},{6,14},{8,0},{10,2},{12,4},{14,6},{16,24},{18,... | collective-permute-start | bytes 516104 | tf_op jit(solution)/shard_map/ppermute | solution.py:73
  178.0 39.2 %collective-permute-start.44 = (bf16[48,1792]{1,0:T(8,128)(2,1)S(1)}, bf16[48,1792]{1,0:T(8,128)(2,1)S(1)}, u32[]{:S(2)}, u32[]{:S(2)}) collective-permute-start(bf16[48,1792]{1,0:T(8,128)(2,1)S(1)} %get-tuple-element.104.refs_14_), channel_id=1, source_target_pairs={{0,16},{2,18},{4,20},{6,22},{8,24},{10,26},{12,28},{14,30},{16,0},... | collective-permute-start | bytes 516104 | tf_op jit(solution)/shard_map/ppermute | solution.py:73
  189.7 27.6 %collective-permute-start.45 = (bf16[48,1792]{1,0:T(8,128)(2,1)S(1)}, bf16[48,1792]{1,0:T(8,128)(2,1)S(1)}, u32[]{:S(2)}, u32[]{:S(2)}) collective-permute-start(bf16[48,1792]{1,0:T(8,128)(2,1)S(1)} %get-tuple-element.105.refs_15_), channel_id=1, source_target_pairs={{0,24},{2,26},{4,28},{6,30},{8,16},{10,18},{12,20},{14,22},{16,8},... | collective-permute-start | bytes 516104 | tf_op jit(solution)/shard_map/ppermute | solution.py:73
  207.5 17.5 %collective-permute-start.35 = (bf16[4,48,512]{2,1,0:T(8,128)(2,1)S(1)}, bf16[4,48,512]{2,1,0:T(8,128)(2,1)S(1)}, u32[]{:S(2)}, u32[]{:S(2)}) collective-permute-start(bf16[4,48,512]{2,1,0:T(8,128)(2,1)S(1)} %get-tuple-element.119), channel_id=1, source_target_pairs={{0,4},{2,6},{4,0},{6,2},{8,12},{10,14},{12,8},{14,10},{16,20},{18,... | collective-permute-start | bytes 589832 | tf_op jit(solution)/shard_map/ppermute | solution.py:73
  216.0 13.9 %collective-permute-start.36 = (bf16[4,48,512]{2,1,0:T(8,128)(2,1)S(1)}, bf16[4,48,512]{2,1,0:T(8,128)(2,1)S(1)}, u32[]{:S(2)}, u32[]{:S(2)}) collective-permute-start(bf16[4,48,512]{2,1,0:T(8,128)(2,1)S(1)} %get-tuple-element.120), channel_id=1, source_target_pairs={{0,6},{2,4},{4,2},{6,0},{8,14},{10,12},{12,10},{14,8},{16,22},{18,... | collective-permute-start | bytes 589832 | tf_op jit(solution)/shard_map/ppermute | solution.py:73
  217.2 18.8 %collective-permute-start.33 = (bf16[1024,768]{1,0:T(8,128)(2,1)S(1)}, bf16[1024,768]{1,0:T(8,128)(2,1)S(1)}, u32[]{:S(2)}, u32[]{:S(2)}) collective-permute-start(bf16[1024,768]{1,0:T(8,128)(2,1)S(1)} %project_far_half.3), channel_id=1, source_target_pairs={{0,1},{1,0},{2,3},{3,2},{4,5},{5,4},{6,7},{7,6},{8,9},{9,8},{10,11... | collective-permute-start | bytes 4718600 | tf_op jit(solution)/shard_map/ppermute | solution.py:77
  217.3 14.2 %collective-permute-start.46 = (f32[24,1792]{1,0:T(8,128)S(1)}, f32[24,1792]{1,0:T(8,128)S(1)}, u32[]{:S(2)}, u32[]{:S(2)}) collective-permute-start(f32[24,1792]{1,0:T(8,128)S(1)} %get-tuple-element.140), channel_id=1, source_target_pairs={{0,1},{1,0},{2,3},{3,2},{4,5},{5,4},{6,7},{7,6},{8,9},{9,8},{10,11... | collective-permute-start | bytes 516104 | tf_op jit(solution)/shard_map/ppermute | solution.py:77
  217.9 17.2 %collective-permute-start.37 = (bf16[48,1024]{1,0:T(8,128)(2,1)S(1)}, bf16[48,1024]{1,0:T(8,128)(2,1)S(1)}, u32[]{:S(2)}, u32[]{:S(2)}) collective-permute-start(bf16[48,1024]{1,0:T(8,128)(2,1)S(1)} %get-tuple-element.113.refs_8_.refs_6_), channel_id=1, source_target_pairs={{0,8},{2,10},{4,12},{6,14},{8,0},{10,2},{12,4},{14,6},{16,24},{18,... | collective-permute-start | bytes 294920 | tf_op jit(solution)/shard_map/ppermute | solution.py:73
  225.0 18.6 %collective-permute-start.38 = (bf16[48,1024]{1,0:T(8,128)(2,1)S(1)}, bf16[48,1024]{1,0:T(8,128)(2,1)S(1)}, u32[]{:S(2)}, u32[]{:S(2)}) collective-permute-start(bf16[48,1024]{1,0:T(8,128)(2,1)S(1)} %get-tuple-element.114.refs_9_.refs_7_), channel_id=1, source_target_pairs={{0,16},{2,18},{4,20},{6,22},{8,24},{10,26},{12,28},{14,30},{16,0},... | collective-permute-start | bytes 294920 | tf_op jit(solution)/shard_map/ppermute | solution.py:73
  229.9 13.6 %collective-permute-start.39 = (bf16[48,1024]{1,0:T(8,128)(2,1)S(1)}, bf16[48,1024]{1,0:T(8,128)(2,1)S(1)}, u32[]{:S(2)}, u32[]{:S(2)}) collective-permute-start(bf16[48,1024]{1,0:T(8,128)(2,1)S(1)} %get-tuple-element.115.refs_10_.refs_8_), channel_id=1, source_target_pairs={{0,24},{2,26},{4,28},{6,30},{8,16},{10,18},{12,20},{14,22},{16,8},... | collective-permute-start | bytes 294920 | tf_op jit(solution)/shard_map/ppermute | solution.py:73
  (59 other events, 572.6 us)

commit v6 on v5

--- a/solution.py
+++ b/solution.py
@@ -20,7 +20,7 @@
 PREP_BLOCK = 512
 FWD_MIB, BWD_MIB, FFN_MIB = 20, 23, 25
 FWD_BQ, FWD_STEP = 512, 256
-BWD_BQ, BWD_STEP, BWD_CHUNK = 256, 128, 12
+BWD_BQ, BWD_STEP, BWD_CHUNK = 256, 128, 10
 NT = (((1,), (1,)), ((), ()))
 TN = (((0,), (0,)), ((), ()))
 bf16 = jnp.bfloat16

time: 249 us -> 245 us (0.984)
  starting transfers between devices: 79.5 us -> 59.3 us
  Pallas kernels: 130 us -> 149 us
  waiting for transfers between devices: 24.4 us -> 20.9 us
    ppermute x36, starting transfers between devices: 76.6 us -> 56.4 us  [xor_permute(): return lax.ppermute(value, 'dp', [(i, i ^ mask) for i in range(count)])]
    pallas_call x3, Pallas kernels: 52.3 us -> 65.1 us  [backward_pair(): pl.pallas_call(passing(functools.partial(backward_kernel, len(part_shapes...]
    pallas_call x3, Pallas kernels: 32.4 us -> 38.5 us  [forward_pair(): pl.pallas_call(passing(kernel, 4 + len(operands), len(deps)), out_shape=t...]
    ppermute x36, waiting for transfers between devices: 17.1 us -> 13.6 us  [xor_permute(): return lax.ppermute(value, 'dp', [(i, i ^ mask) for i in range(count)])]
  transfers between devices with their start and end apart: 48 -> 48, of which waited for: 12 -> 11; matrix products, arithmetic and copies ran while one was open for 2% -> 2% of each run, Pallas kernels for 41% -> 49%
where the time goes in v6:
time: 245 us; the launch traced here: 242 us
  Pallas kernels  149 us (61%)
  starting transfers between devices  59.3 us (24%)
  waiting for transfers between devices  20.9 us (9%)
  local copies, waits for them, and re-layouts  6.5 us (3%)
  other arithmetic  3.82 us (2%)
    pallas_call x3, Pallas kernels, backward_pair(): pl.pallas_call(passing(functools.partial(backward_kernel, len(part_shapes...  65.1 us
    ppermute x36, starting transfers between devices, xor_permute(): return lax.ppermute(value, 'dp', [(i, i ^ mask) for i in range(count)])  56.4 us
    pallas_call x3, Pallas kernels, forward_pair(): pl.pallas_call(passing(kernel, 4 + len(operands), len(deps)), out_shape=t...  38.5 us
    pallas_call x1, Pallas kernels, feed_forward(): pl.pallas_call(functools.partial(ffn_kernel, len(outs_of), part_count, do...  21.9 us
    ppermute x36, waiting for transfers between devices, xor_permute(): return lax.ppermute(value, 'dp', [(i, i ^ mask) for i in range(count)])  13.6 us
    pallas_call x2, Pallas kernels, weight_grads(): pl.pallas_call(passing(functools.partial(weight_grad_kernel, split, own,...  8.09 us
    ppermute x12, waiting for transfers between devices, core_swap(): return lax.ppermute(value, 'head', [(0, 1), (1, 0)])  7.28 us
    pallas_call x2, Pallas kernels, project_far_half(): pl.pallas_call(passing(functools.partial(project_kernel, count), 1 + 2 *...  6.55 us
  transfers between devices with their start and end apart: 48, of which 11 were waited for; matrix products, arithmetic and copies ran while one was open for 2% of the time, Pallas kernels for 49%

profile of v6, /device:TPU:0, one launch (start us, length us, event | category | flops | bytes accessed | tf_op | source)
XLA Modules:
  0.0 241.8 jit_solution(10088731533399647709)
XLA Ops:
  5.3 2.6 %collective-permute-start.1 = (bf16[1,48,512]{2,1,0:T(8,128)(2,1)S(1)}, bf16[1,48,512]{2,1,0:T(8,128)(2,1)S(1)}, u32[]{:S(2)}, u32[]{:S(2)}) collective-permute-start(bf16[1,48,512]{2,1,0:T(8,128)(2,1)S(1)} %bitcast.53), channel_id=1, source_target_pairs={{0,8},{2,10},{4,12},{6,14},{8,0},{10,2},{12,4},{14,6},{16,24},{18,... | collective-permute-start | bytes 147464 | tf_op jit(solution)/shard_map/ppermute | solution.py:73
  7.9 2.6 %collective-permute-start.2 = (bf16[1,48,512]{2,1,0:T(8,128)(2,1)S(1)}, bf16[1,48,512]{2,1,0:T(8,128)(2,1)S(1)}, u32[]{:S(2)}, u32[]{:S(2)}) collective-permute-start(bf16[1,48,512]{2,1,0:T(8,128)(2,1)S(1)} %bitcast.54), channel_id=1, source_target_pairs={{0,16},{2,18},{4,20},{6,22},{8,24},{10,26},{12,28},{14,30},{16,0},... | collective-permute-start | bytes 147464 | tf_op jit(solution)/shard_map/ppermute | solution.py:73
  11.3 2.8 %collective-permute-done.2.refs_3_ = bf16[1,48,512]{2,1,0:T(8,128)(2,1)S(1)} collective-permute-done((bf16[1,48,512]{2,1,0:T(8,128)(2,1)S(1)}, bf16[1,48,512]{2,1,0:T(8,128)(2,1)S(1)}, u32[]{:S(2)}, u32[]{:S(2)}) %collective-permute-start.2) | collective-permute-done | bytes 49184 | tf_op jit(solution)/shard_map/ppermute | solution.py:73
  14.1 2.3 collective-permute-done.3.refs_4_
  22.0 2.4 collective-permute-start.9
  24.5 5.4 %collective-permute-done.8.refs_3_ = bf16[1,48,1152]{2,1,0:T(8,128)(2,1)S(1)} collective-permute-done((bf16[1,48,1152]{2,1,0:T(8,128)(2,1)S(1)}, bf16[1,48,1152]{2,1,0:T(8,128)(2,1)S(1)}, u32[]{:S(2)}, u32[]{:S(2)}) %collective-permute-start.8) | collective-permute-done | bytes 110624 | tf_op jit(solution)/shard_map/ppermute | solution.py:73
  40.5 13.0 %attention_forward_first.1 = (bf16[2048,768]{1,0:T(8,128)(2,1)S(1)}, f32[16,768]{1,0:T(8,128)S(1)}, bf16[4,4,48,512]{3,2,1,0:T(8,128)(2,1)S(1)}, bf16[2048,128]{...) custom-call(s32[6]{0:T(128)S(1)} %pad_add_fusion.refs_0_.scal, ...), custom_call_target="tpu_custom_call" | custom-call | flops 1800000000 | tf_op jit(solution)/shard_map/attention_forward_first/pallas_call | solution.py:405
  54.9 3.5 %collective-permute-start.19 = (bf16[4,48,1792]{2,1,0:T(8,128)(2,1)S(1)}, bf16[4,48,1792]{2,1,0:T(8,128)(2,1)S(1)}, u32[]{:S(2)}, u32[]{:S(2)}) collective-permute-start(bf16[4,48,1792]{2,1,0:T(8,128)(2,1)S(1)} %stack_parts.9.refs_8_.refs_10_), channel_id=1, source_target_pairs={{0,6},{2,4},{4,2},{6,0},{8,14},{10,12},{12,10},{14,8},{16,22},{18,... | collective-permute-start | bytes 2064392 | tf_op jit(solution)/shard_map/ppermute | solution.py:73
  58.3 11.6 %attention_forward.2 = (bf16[4,4,48,1152]{3,2,1,0:T(8,128)(2,1)S(1)}, bf16[2048,128]{1,0:T(8,128)(2,1)S(1)}, bf16[2048,128]{1,0:T(8,128)(2,1)S(1)}, bf16[2048,12...) custom-call(s32[6]{0:T(128)S(1)} %pad_add_fusion.refs_0_.scal, ...), custom_call_target="tpu_custom_call" | custom-call | flops 1800000000 | tf_op jit(solution)/shard_map/attention_forward/pallas_call | solution.py:405
  70.8 13.9 %attention_forward.3 = (bf16[2048,128]{1,0:T(8,128)(2,1)S(1)}, bf16[2048,128]{1,0:T(8,128)(2,1)S(1)}, bf16[2048,128]{1,0:T(8,128)(2,1)S(1)}, bf16[2048,128]{1,0:T(8,128)(2,1)S(1)}, f32[2048,128]{1,0:T(8,128)S(1)}) custom-call(s32[6]{0:T(128)S(1)} %pad_add_fusion.refs_0_.scal, bf16[2048,768]{1,0:T(8,128)(2,1)S(1)} %get-tuple-element.72.refs_5_.refs_1_, ...), custom_call_target="tpu_custom_call" | custom-call | flops 1800000000 | tf_op jit(solution)/shard_map/attention_forward/pallas_call | solution.py:405
  85.7 2.6 %project_far_half.2 = bf16[1024,768]{1,0:T(8,128)(2,1)S(1)} custom-call(s32[6]{0:T(128)S(1)} %pad_add_fusion.refs_0_.scal, bf16[2048,128]{1,0:T(8,128)(2,1)S(1)} %get-tuple-element.71.refs_1_.refs_0_.refs_8_, bf16[2048,128]{1,0:T(8,128)(2,1)S(1)} %get-tuple-element.73.refs_2_.refs_1_.refs_8_, ...), custom_call_target="tpu_custom_call" | custom-call | flops 400000000 | tf_op jit(solution)/shard_map/project_far_half/pallas_call | solution.py:599
  89.5 3.3 %collective-permute-done.21.refs_14_ = bf16[4,48,1792]{2,1,0:T(8,128)(2,1)S(1)} collective-permute-done((bf16[4,48,1792]{2,1,0:T(8,128)(2,1)S(1)}, bf16[4,48,1792]{2,1,0:T(8,128)(2,1)S(1)}, u32[]{:S(2)}, u32[]{:S(2)}) %collective-permute-start.21) | collective-permute-done | bytes 688160 | tf_op jit(solution)/shard_map/ppermute | solution.py:77
  95.7 21.9 %feed_forward.1 = (bf16[1024,768]{1,0:T(8,128)(2,1)}, bf16[1024,768]{1,0:T(8,128)(2,1)S(1)}, f32[1024,768]{1,0:T(8,128)S(1)}, bf16[1024,1152]{1,0:T(8,128)(2,1)S...) custom-call(s32[6]{0:T(128)S(1)} %pad_add_fusion.refs_0_.scal, ...), custom_call_target="tpu_custom_call" | custom-call | flops 2500000000 | tf_op jit(solution)/shard_map/feed_forward/pallas_call | solution.py:830
  117.6 4.1 %weight_grads.3 = bf16[768,1792]{1,0:T(8,128)(2,1)S(1)} custom-call(s32[6]{0:T(128)S(1)} %pad_add_fusion.refs_0_.scal, bf16[1024,1152]{1,0:T(8,128)(2,1)S(1)} %get-tuple-element.83.refs_1_, bf16[2,1024,1152]{2,1,0:T(8,128)(2,1)S(1)} %get-tuple-element.84.refs_2_, bf16[1024,768]{1,0:T(8,128)(2,1)S(1)} %get-tuple-element.85.refs_3_, ...), custom_call_target="tpu_custom_call" | custom-call | flops 500000000 | tf_op jit(solution)/shard_map/weight_grads/pallas_call | solution.py:807
  122.4 4.0 %weight_grads.2 = bf16[768,1792]{1,0:T(8,128)(2,1)S(1)} custom-call(s32[6]{0:T(128)S(1)} %pad_add_fusion.refs_0_.scal, bf16[1024,1152]{1,0:T(8,128)(2,1)S(1)} %get-tuple-element.83.refs_1_, bf16[2,1024,1152]{2,1,0:T(8,128)(2,1)S(1)} %get-tuple-element.84.refs_2_, bf16[1024,768]{1,0:T(8,128)(2,1)S(1)} %get-tuple-element.85.refs_3_, ...), custom_call_target="tpu_custom_call" | custom-call | flops 500000000 | tf_op jit(solution)/shard_map/weight_grads/pallas_call | solution.py:807
  131.6 21.8 %attention_backward.3 = (bf16[2048,384]{1,0:T(8,128)(2,1)S(1)}, bf16[768,512]{1,0:T(8,128)(2,1)S(1)}) custom-call(s32[6]{0:T(128)S(1)} %pad_add_fusion.refs_0_.scal, bf16[2048,768]{1,0:T(8,128)(2,1)S(1)} %get-tuple-element.72.refs_5_.refs_1_, bf16[1024,768]{1,0:T(8,128)(2,1)S(1)} %get-tuple-element.78.refs_2_, ...), custom_call_target="tpu_custom_call" | custom-call | flops 3000000000 | tf_op jit(solution)/shard_map/attention_backward/pallas_call | solution.py:557
  153.5 21.6 %attention_backward.4 = (bf16[2048,384]{1,0:T(8,128)(2,1)S(1)}, bf16[4,48,1024]{2,1,0:T(8,128)(2,1)S(1)}, bf16[4,48,1024]{2,1,0:T(8,128)(2,1)S(1)}, bf16[4,48,10...) custom-call(s32[6]{0:T(128)S(1)} %pad_add_fusion.refs_0_.scal, bf16[2048,768]{1,0:T(8,128)(2,1)S(1)} %get-tuple-element.72.refs_5_.refs_1_, ...), custom_call_target="tpu_custom_call" | custom-call | flops 3000000000 | tf_op jit(solution)/shard_map/attention_backward/pallas_call | solution.py:557
  175.3 3.4 %collective-permute-start.32 = (bf16[4,48,1024]{2,1,0:T(8,128)(2,1)S(1)}, bf16[4,48,1024]{2,1,0:T(8,128)(2,1)S(1)}, u32[]{:S(2)}, u32[]{:S(2)}) collective-permute-start(bf16[4,48,1024]{2,1,0:T(8,128)(2,1)S(1)} %get-tuple-element.111), channel_id=1, source_target_pairs={{0,6},{2,4},{4,2},{6,0},{8,14},{10,12},{12,10},{14,8},{16,22},{18,... | collective-permute-start | bytes 1179656 | tf_op jit(solution)/shard_map/ppermute | solution.py:73
  179.1 6.2 %collective-permute-start.44 = (bf16[48,1792]{1,0:T(8,128)(2,1)S(1)}, bf16[48,1792]{1,0:T(8,128)(2,1)S(1)}, u32[]{:S(2)}, u32[]{:S(2)}) collective-permute-start(bf16[48,1792]{1,0:T(8,128)(2,1)S(1)} %get-tuple-element.104.refs_14_), channel_id=1, source_target_pairs={{0,16},{2,18},{4,20},{6,22},{8,24},{10,26},{12,28},{14,30},{16,0},... | collective-permute-start | bytes 516104 | tf_op jit(solution)/shard_map/ppermute | solution.py:73
  187.3 21.7 %attention_backward.5 = (bf16[2048,384]{1,0:T(8,128)(2,1)S(1)}, bf16[4,48,512]{2,1,0:T(8,128)(2,1)S(1)}, bf16[4,48,512]{2,1,0:T(8,128)(2,1)S(1)}, bf16[4,48,512]{2,1,0:T(8,128)(2,1)S(1)}, bf16[4,48,512]{2,1,0:T(8,128)(2,1)S(1)}) custom-call(s32[6]{0:T(128)S(1)} %pad_add_fusion.refs_0_.scal, bf16[2048,768]{1,0:T(8,128)(2,1)S(1)} %get-tuple-element.72.refs_5_.refs_1_, ...), custom_call_target="tpu_custom_call" | custom-call | flops 3000000000 | tf_op jit(solution)/shard_map/attention_backward/pallas_call | solution.py:557
  209.4 3.9 %project_far_half.3 = bf16[1024,768]{1,0:T(8,128)(2,1)S(1)} custom-call(s32[6]{0:T(128)S(1)} %pad_add_fusion.refs_0_.scal, bf16[2048,384]{1,0:T(8,128)(2,1)S(1)} %get-tuple-element.91.refs_1_, bf16[2048,384]{1,0:T(8,128)(2,1)S(1)} %get-tuple-element.97.refs_5_.refs_2_, bf16[2048,384]{1,0:T(8,128)(2,1)S(1)} %get-tuple-element.106.refs_5_.refs_3_, ...), custom_call_target="tpu_custom_call" | custom-call | flops 400000000 | tf_op jit(solution)/shard_map/project_far_half/pallas_call | solution.py:599
  213.3 3.4 %collective-permute-start.36 = (bf16[4,48,512]{2,1,0:T(8,128)(2,1)S(1)}, bf16[4,48,512]{2,1,0:T(8,128)(2,1)S(1)}, u32[]{:S(2)}, u32[]{:S(2)}) collective-permute-start(bf16[4,48,512]{2,1,0:T(8,128)(2,1)S(1)} %get-tuple-element.120), channel_id=1, source_target_pairs={{0,6},{2,4},{4,2},{6,0},{8,14},{10,12},{12,10},{14,8},{16,22},{18,... | collective-permute-start | bytes 589832 | tf_op jit(solution)/shard_map/ppermute | solution.py:73
  217.5 7.9 %collective-permute-start.38 = (bf16[48,1024]{1,0:T(8,128)(2,1)S(1)}, bf16[48,1024]{1,0:T(8,128)(2,1)S(1)}, u32[]{:S(2)}, u32[]{:S(2)}) collective-permute-start(bf16[48,1024]{1,0:T(8,128)(2,1)S(1)} %get-tuple-element.114.refs_9_.refs_7_), channel_id=1, source_target_pairs={{0,16},{2,18},{4,20},{6,22},{8,24},{10,26},{12,28},{14,30},{16,0},... | collective-permute-start | bytes 294920 | tf_op jit(solution)/shard_map/ppermute | solution.py:73
  232.9 6.0 %final_rows.1 = (f32[1024,768]{1,0:T(8,128)}, f32[8,128]{1,0:T(8,128)S(1)}) custom-call(s32[6]{0:T(128)S(1)} %pad_add_fusion.refs_0_.scal, bf16[2048,384]{1,0:T(8,128)(2,1)S(1)} %get-tuple-element.91.refs_1_, bf16[2048,384]{1,0:T(8,128)(2,1)S(1)} %get-tuple-element.97.refs_5_.refs_2_, bf16[2048,384]{1,0:T(8,128)(2,1)S(1)} %get-tuple-element.106.refs_5_.refs_3_, ...), custom_call_target="tpu_custom_call" | custom-call | flops 700000000 | tf_op jit(solution)/shard_map/final_rows/pallas_call | solution.py:634
  (186 shorter events, 47.6 us)
Async XLA Ops:
  16.6 13.4 %collective-permute-start.4 = (bf16[4,48,512]{2,1,0:T(8,128)(2,1)S(1)}, bf16[4,48,512]{2,1,0:T(8,128)(2,1)S(1)}, u32[]{:S(2)}, u32[]{:S(2)}) collective-permute-start(bf16[4,48,512]{2,1,0:T(8,128)(2,1)S(1)} %stack_parts.5.refs_4_), channel_id=1, source_target_pairs={{0,2},{2,0},{4,6},{6,4},{8,10},{10,8},{12,14},{14,12},{16,18},{18,... | collective-permute-start | bytes 589832 | tf_op jit(solution)/shard_map/ppermute | solution.py:73
  30.0 24.9 %collective-permute-start.11 = (bf16[4,48,1152]{2,1,0:T(8,128)(2,1)S(1)}, bf16[4,48,1152]{2,1,0:T(8,128)(2,1)S(1)}, u32[]{:S(2)}, u32[]{:S(2)}) collective-permute-start(bf16[4,48,1152]{2,1,0:T(8,128)(2,1)S(1)} %stack_parts.7.refs_8_.refs_4_), channel_id=1, source_target_pairs={{0,2},{2,0},{4,6},{6,4},{8,10},{10,8},{12,14},{14,12},{16,18},{18,... | collective-permute-start | bytes 1327112 | tf_op jit(solution)/shard_map/ppermute | solution.py:73
  33.6 20.0 %collective-permute-start.15 = (bf16[1,48,1792]{2,1,0:T(8,128)(2,1)S(1)}, bf16[1,48,1792]{2,1,0:T(8,128)(2,1)S(1)}, u32[]{:S(2)}, u32[]{:S(2)}) collective-permute-start(bf16[1,48,1792]{2,1,0:T(8,128)(2,1)S(1)} %stack_parts.8.refs_9_.refs_1_), channel_id=1, source_target_pairs={{0,16},{2,18},{4,20},{6,22},{8,24},{10,26},{12,28},{14,30},{16,0},... | collective-permute-start | bytes 516104 | tf_op jit(solution)/shard_map/ppermute | solution.py:73
  34.8 18.8 %collective-permute-start.16 = (bf16[1,48,1792]{2,1,0:T(8,128)(2,1)S(1)}, bf16[1,48,1792]{2,1,0:T(8,128)(2,1)S(1)}, u32[]{:S(2)}, u32[]{:S(2)}) collective-permute-start(bf16[1,48,1792]{2,1,0:T(8,128)(2,1)S(1)} %stack_parts.8.refs_9_.refs_1_), channel_id=1, source_target_pairs={{0,24},{2,26},{4,28},{6,30},{8,16},{10,18},{12,20},{14,22},{16,8},... | collective-permute-start | bytes 516104 | tf_op jit(solution)/shard_map/ppermute | solution.py:73
  36.4 22.0 %collective-permute-start.12 = (bf16[4,48,1152]{2,1,0:T(8,128)(2,1)S(1)}, bf16[4,48,1152]{2,1,0:T(8,128)(2,1)S(1)}, u32[]{:S(2)}, u32[]{:S(2)}) collective-permute-start(bf16[4,48,1152]{2,1,0:T(8,128)(2,1)S(1)} %stack_parts.7.refs_8_.refs_4_), channel_id=1, source_target_pairs={{0,4},{2,6},{4,0},{6,2},{8,12},{10,14},{12,8},{14,10},{16,20},{18,... | collective-permute-start | bytes 1327112 | tf_op jit(solution)/shard_map/ppermute | solution.py:73
  39.0 19.3 %collective-permute-start.13 = (bf16[4,48,1152]{2,1,0:T(8,128)(2,1)S(1)}, bf16[4,48,1152]{2,1,0:T(8,128)(2,1)S(1)}, u32[]{:S(2)}, u32[]{:S(2)}) collective-permute-start(bf16[4,48,1152]{2,1,0:T(8,128)(2,1)S(1)} %stack_parts.7.refs_8_.refs_4_), channel_id=1, source_target_pairs={{0,6},{2,4},{4,2},{6,0},{8,14},{10,12},{12,10},{14,8},{16,22},{18,... | collective-permute-start | bytes 1327112 | tf_op jit(solution)/shard_map/ppermute | solution.py:73
  54.8 30.8 %collective-permute-start.17 = (bf16[4,48,1792]{2,1,0:T(8,128)(2,1)S(1)}, bf16[4,48,1792]{2,1,0:T(8,128)(2,1)S(1)}, u32[]{:S(2)}, u32[]{:S(2)}) collective-permute-start(bf16[4,48,1792]{2,1,0:T(8,128)(2,1)S(1)} %stack_parts.9.refs_8_.refs_10_), channel_id=1, source_target_pairs={{0,2},{2,0},{4,6},{6,4},{8,10},{10,8},{12,14},{14,12},{16,18},{18,... | collective-permute-start | bytes 2064392 | tf_op jit(solution)/shard_map/ppermute | solution.py:73
  54.8 30.8 %collective-permute-start.18 = (bf16[4,48,1792]{2,1,0:T(8,128)(2,1)S(1)}, bf16[4,48,1792]{2,1,0:T(8,128)(2,1)S(1)}, u32[]{:S(2)}, u32[]{:S(2)}) collective-permute-start(bf16[4,48,1792]{2,1,0:T(8,128)(2,1)S(1)} %stack_parts.9.refs_8_.refs_10_), channel_id=1, source_target_pairs={{0,4},{2,6},{4,0},{6,2},{8,12},{10,14},{12,8},{14,10},{16,20},{18,... | collective-permute-start | bytes 2064392 | tf_op jit(solution)/shard_map/ppermute | solution.py:73
  54.9 30.8 %collective-permute-start.19 = (bf16[4,48,1792]{2,1,0:T(8,128)(2,1)S(1)}, bf16[4,48,1792]{2,1,0:T(8,128)(2,1)S(1)}, u32[]{:S(2)}, u32[]{:S(2)}) collective-permute-start(bf16[4,48,1792]{2,1,0:T(8,128)(2,1)S(1)} %stack_parts.9.refs_8_.refs_10_), channel_id=1, source_target_pairs={{0,6},{2,4},{4,2},{6,0},{8,14},{10,12},{12,10},{14,8},{16,22},{18,... | collective-permute-start | bytes 2064392 | tf_op jit(solution)/shard_map/ppermute | solution.py:73
  128.0 47.2 %collective-permute-start.27 = (bf16[4,48,1792]{2,1,0:T(8,128)(2,1)S(1)}, bf16[4,48,1792]{2,1,0:T(8,128)(2,1)S(1)}, u32[]{:S(2)}, u32[]{:S(2)}) collective-permute-start(bf16[4,48,1792]{2,1,0:T(8,128)(2,1)S(1)} %get-tuple-element.88.refs_13_.refs_14_), channel_id=1, source_target_pairs={{0,2},{2,0},{4,6},{6,4},{8,10},{10,8},{12,14},{14,12},{16,18},{18,... | collective-permute-start | bytes 2064392 | tf_op jit(solution)/shard_map/ppermute | solution.py:73
  128.1 50.6 %collective-permute-start.28 = (bf16[4,48,1792]{2,1,0:T(8,128)(2,1)S(1)}, bf16[4,48,1792]{2,1,0:T(8,128)(2,1)S(1)}, u32[]{:S(2)}, u32[]{:S(2)}) collective-permute-start(bf16[4,48,1792]{2,1,0:T(8,128)(2,1)S(1)} %get-tuple-element.89.refs_14_.refs_15_), channel_id=1, source_target_pairs={{0,4},{2,6},{4,0},{6,2},{8,12},{10,14},{12,8},{14,10},{16,20},{18,... | collective-permute-start | bytes 2064392 | tf_op jit(solution)/shard_map/ppermute | solution.py:73
  129.4 49.3 %collective-permute-start.29 = (bf16[4,48,1792]{2,1,0:T(8,128)(2,1)S(1)}, bf16[4,48,1792]{2,1,0:T(8,128)(2,1)S(1)}, u32[]{:S(2)}, u32[]{:S(2)}) collective-permute-start(bf16[4,48,1792]{2,1,0:T(8,128)(2,1)S(1)} %get-tuple-element.90.refs_15_.refs_16_), channel_id=1, source_target_pairs={{0,6},{2,4},{4,2},{6,0},{8,14},{10,12},{12,10},{14,8},{16,22},{18,... | collective-permute-start | bytes 2064392 | tf_op jit(solution)/shard_map/ppermute | solution.py:73
  175.1 12.1 %collective-permute-start.30 = (bf16[4,48,1024]{2,1,0:T(8,128)(2,1)S(1)}, bf16[4,48,1024]{2,1,0:T(8,128)(2,1)S(1)}, u32[]{:S(2)}, u32[]{:S(2)}) collective-permute-start(bf16[4,48,1024]{2,1,0:T(8,128)(2,1)S(1)} %get-tuple-element.109), channel_id=1, source_target_pairs={{0,2},{2,0},{4,6},{6,4},{8,10},{10,8},{12,14},{14,12},{16,18},{18,... | collective-permute-start | bytes 1179656 | tf_op jit(solution)/shard_map/ppermute | solution.py:73
  175.2 33.8 %collective-permute-start.31 = (bf16[4,48,1024]{2,1,0:T(8,128)(2,1)S(1)}, bf16[4,48,1024]{2,1,0:T(8,128)(2,1)S(1)}, u32[]{:S(2)}, u32[]{:S(2)}) collective-permute-start(bf16[4,48,1024]{2,1,0:T(8,128)(2,1)S(1)} %get-tuple-element.110), channel_id=1, source_target_pairs={{0,4},{2,6},{4,0},{6,2},{8,12},{10,14},{12,8},{14,10},{16,20},{18,... | collective-permute-start | bytes 1179656 | tf_op jit(solution)/shard_map/ppermute | solution.py:73
  175.3 33.8 %collective-permute-start.32 = (bf16[4,48,1024]{2,1,0:T(8,128)(2,1)S(1)}, bf16[4,48,1024]{2,1,0:T(8,128)(2,1)S(1)}, u32[]{:S(2)}, u32[]{:S(2)}) collective-permute-start(bf16[4,48,1024]{2,1,0:T(8,128)(2,1)S(1)} %get-tuple-element.111), channel_id=1, source_target_pairs={{0,6},{2,4},{4,2},{6,0},{8,14},{10,12},{12,10},{14,8},{16,22},{18,... | collective-permute-start | bytes 1179656 | tf_op jit(solution)/shard_map/ppermute | solution.py:73
  179.1 34.2 %collective-permute-start.43 = (bf16[48,1792]{1,0:T(8,128)(2,1)S(1)}, bf16[48,1792]{1,0:T(8,128)(2,1)S(1)}, u32[]{:S(2)}, u32[]{:S(2)}) collective-permute-start(bf16[48,1792]{1,0:T(8,128)(2,1)S(1)} %get-tuple-element.103.refs_13_), channel_id=1, source_target_pairs={{0,8},{2,10},{4,12},{6,14},{8,0},{10,2},{12,4},{14,6},{16,24},{18,... | collective-permute-start | bytes 516104 | tf_op jit(solution)/shard_map/ppermute | solution.py:73
  179.1 37.6 %collective-permute-start.44 = (bf16[48,1792]{1,0:T(8,128)(2,1)S(1)}, bf16[48,1792]{1,0:T(8,128)(2,1)S(1)}, u32[]{:S(2)}, u32[]{:S(2)}) collective-permute-start(bf16[48,1792]{1,0:T(8,128)(2,1)S(1)} %get-tuple-element.104.refs_14_), channel_id=1, source_target_pairs={{0,16},{2,18},{4,20},{6,22},{8,24},{10,26},{12,28},{14,30},{16,0},... | collective-permute-start | bytes 516104 | tf_op jit(solution)/shard_map/ppermute | solution.py:73
  187.2 29.5 %collective-permute-start.45 = (bf16[48,1792]{1,0:T(8,128)(2,1)S(1)}, bf16[48,1792]{1,0:T(8,128)(2,1)S(1)}, u32[]{:S(2)}, u32[]{:S(2)}) collective-permute-start(bf16[48,1792]{1,0:T(8,128)(2,1)S(1)} %get-tuple-element.105.refs_15_), channel_id=1, source_target_pairs={{0,24},{2,26},{4,28},{6,30},{8,16},{10,18},{12,20},{14,22},{16,8},... | collective-permute-start | bytes 516104 | tf_op jit(solution)/shard_map/ppermute | solution.py:73
  213.3 12.0 %collective-permute-start.36 = (bf16[4,48,512]{2,1,0:T(8,128)(2,1)S(1)}, bf16[4,48,512]{2,1,0:T(8,128)(2,1)S(1)}, u32[]{:S(2)}, u32[]{:S(2)}) collective-permute-start(bf16[4,48,512]{2,1,0:T(8,128)(2,1)S(1)} %get-tuple-element.120), channel_id=1, source_target_pairs={{0,6},{2,4},{4,2},{6,0},{8,14},{10,12},{12,10},{14,8},{16,22},{18,... | collective-permute-start | bytes 589832 | tf_op jit(solution)/shard_map/ppermute | solution.py:73
  216.8 14.7 %collective-permute-start.33 = (bf16[1024,768]{1,0:T(8,128)(2,1)S(1)}, bf16[1024,768]{1,0:T(8,128)(2,1)S(1)}, u32[]{:S(2)}, u32[]{:S(2)}) collective-permute-start(bf16[1024,768]{1,0:T(8,128)(2,1)S(1)} %project_far_half.3), channel_id=1, source_target_pairs={{0,1},{1,0},{2,3},{3,2},{4,5},{5,4},{6,7},{7,6},{8,9},{9,8},{10,11... | collective-permute-start | bytes 4718600 | tf_op jit(solution)/shard_map/ppermute | solution.py:77
  217.5 13.0 %collective-permute-start.37 = (bf16[48,1024]{1,0:T(8,128)(2,1)S(1)}, bf16[48,1024]{1,0:T(8,128)(2,1)S(1)}, u32[]{:S(2)}, u32[]{:S(2)}) collective-permute-start(bf16[48,1024]{1,0:T(8,128)(2,1)S(1)} %get-tuple-element.113.refs_8_.refs_6_), channel_id=1, source_target_pairs={{0,8},{2,10},{4,12},{6,14},{8,0},{10,2},{12,4},{14,6},{16,24},{18,... | collective-permute-start | bytes 294920 | tf_op jit(solution)/shard_map/ppermute | solution.py:73
  217.5 21.5 %collective-permute-start.38 = (bf16[48,1024]{1,0:T(8,128)(2,1)S(1)}, bf16[48,1024]{1,0:T(8,128)(2,1)S(1)}, u32[]{:S(2)}, u32[]{:S(2)}) collective-permute-start(bf16[48,1024]{1,0:T(8,128)(2,1)S(1)} %get-tuple-element.114.refs_9_.refs_7_), channel_id=1, source_target_pairs={{0,16},{2,18},{4,20},{6,22},{8,24},{10,26},{12,28},{14,30},{16,0},... | collective-permute-start | bytes 294920 | tf_op jit(solution)/shard_map/ppermute | solution.py:73
  225.4 13.6 %collective-permute-start.39 = (bf16[48,1024]{1,0:T(8,128)(2,1)S(1)}, bf16[48,1024]{1,0:T(8,128)(2,1)S(1)}, u32[]{:S(2)}, u32[]{:S(2)}) collective-permute-start(bf16[48,1024]{1,0:T(8,128)(2,1)S(1)} %get-tuple-element.115.refs_10_.refs_8_), channel_id=1, source_target_pairs={{0,24},{2,26},{4,28},{6,30},{8,16},{10,18},{12,20},{14,22},{16,8},... | collective-permute-start | bytes 294920 | tf_op jit(solution)/shard_map/ppermute | solution.py:73
  226.9 12.0 %collective-permute-start.40 = (bf16[48,512]{1,0:T(8,128)(2,1)S(1)}, bf16[48,512]{1,0:T(8,128)(2,1)S(1)}, u32[]{:S(2)}, u32[]{:S(2)}) collective-permute-start(bf16[48,512]{1,0:T(8,128)(2,1)S(1)} %get-tuple-element.122.refs_12_), channel_id=1, source_target_pairs={{0,8},{2,10},{4,12},{6,14},{8,0},{10,2},{12,4},{14,6},{16,24},{18,... | collective-permute-start | bytes 147464 | tf_op jit(solution)/shard_map/ppermute | solution.py:73
  (59 other events, 514.1 us)
